TPU v7x, 128 devices: a whole 4x4x4 slice. The times are simulated.
128 devices in a mesh: grp: 4 (over y_lo, core), dev: 32 (over x, z, y_hi).
Axes of the slice: x: 4, y: 4 (y_hi: 2, y_lo: 2; y = y_hi * 2 + y_lo), z: 4, core: 2. Of those that a mesh axis runs over, the one named last changes fastest.
Arguments:
- tokens: bfloat16 [16384, 2048], P(('grp', 'dev')), may hold values from -6 to 6
- cotangent: bfloat16 [16384, 2048], P(('grp', 'dev')), may hold values from -1.5 to 1.5
- route_weight: float32 [16384, 2], P(('grp', 'dev')), may hold values from 0.1 to 1
- slot_expert: int32 [128], replicated, may hold values from 0 to 15, as said below
- targets: int32 [16384, 2], P(('grp', 'dev')), may hold values from 0 to 127, as said below
- proj_in: float32 [16, 2048, 2048], P('grp', 'dev'), may hold values from -0.125 to 0.125
- first_in: float32 [16, 2048, 2048], P('grp', 'dev'), may hold values from -6 to 6
- second_in: float32 [16, 2048, 2048], P('grp', 'dev'), may hold values from 0.01 to 1
- proj_out: float32 [16, 1024, 2048], P('grp', 'dev'), may hold values from -0.1875 to 0.1875
- first_out: float32 [16, 1024, 2048], P('grp', 'dev'), may hold values from -6 to 6
- second_out: float32 [16, 1024, 2048], P('grp', 'dev'), may hold values from 0.01 to 1
Outputs:
- mixed: bfloat16 [16384, 2048], P(('grp', 'dev'))
- token_grad: bfloat16 [16384, 2048], P(('grp', 'dev'))
- mix_grad: float32 [16384, 2], P(('grp', 'dev'))
- trained_in: float32 [16, 2048, 2048], P('grp', 'dev')
- mean_in: float32 [16, 2048, 2048], P('grp', 'dev')
- square_in: float32 [16, 2048, 2048], P('grp', 'dev')
- trained_out: float32 [16, 1024, 2048], P('grp', 'dev')
- mean_out: float32 [16, 1024, 2048], P('grp', 'dev')
- square_out: float32 [16, 1024, 2048], P('grp', 'dev')
Inputs may be any that keep to these rules, and one draw needn't show every extreme that they name: `slot_expert`: entry s is the expert held by slot s, the device s in grp+dev order; each of the 16 experts is held by at least one slot. `targets`: entry [t, k] is the slot that serves the k-th expert of token t; the two slots of a token hold different experts.
All inputs are finite; a program needn't handle non-finite values.
Results may differ from a plain program's by a relative error of at most 0.015.
The roundings to bfloat16 on the way count: a program that leaves them out, or rounds other values in their place, can miss the bound.
Values may be sent and summed in bfloat16 or wider, within the bound.
No kernel may reach another device: no remote copies, remote signals or barrier semaphores. Data moves between devices by JAX's collectives and lax.ppermute only.
A program may use at most 128 MiB of HBM per device.

v0:
```python
import jax
import jax.numpy as jnp
from jax import lax
from jax.sharding import PartitionSpec as P

D = 2048
FF = 1024
E = 16


beta_first = 0.9
beta_second = 0.95
learn_rate = 0.01
decay_rate = 0.1
adam_eps = 1e-08
bias_first = 1.0 - 0.9**10
bias_second = 1.0 - 0.95**10


def silu_parts(values):
    logistic = jax.nn.sigmoid(values)
    return (values * logistic, logistic * (1.0 + values * (1.0 - logistic)))


def slot_pass(rows_x, rows_dy, weight_up, weight_down):
    gate_up = jnp.dot(rows_x, weight_up, preferred_element_type=jnp.float32)
    gating = gate_up[:, :FF]
    upward = gate_up[:, FF:]
    active, derivative = silu_parts(gating)
    hidden = (active * upward).astype(jnp.bfloat16)
    result = jnp.dot(hidden, weight_down, preferred_element_type=jnp.float32).astype(jnp.bfloat16)
    dhidden = lax.dot_general(
        rows_dy, weight_down, (((1,), (1,)), ((), ())), preferred_element_type=jnp.float32
    )
    grad_gateup = jnp.concatenate([dhidden * upward * derivative, dhidden * active], axis=1).astype(
        jnp.bfloat16
    )
    rows_dx = lax.dot_general(
        grad_gateup, weight_up, (((1,), (1,)), ((), ())), preferred_element_type=jnp.float32
    ).astype(jnp.bfloat16)
    grad_up = lax.dot_general(
        rows_x, grad_gateup, (((0,), (0,)), ((), ())), preferred_element_type=jnp.float32
    ).astype(jnp.bfloat16)
    grad_down = lax.dot_general(
        hidden, rows_dy, (((0,), (0,)), ((), ())), preferred_element_type=jnp.float32
    ).astype(jnp.bfloat16)
    return (result, rows_dx, grad_up, grad_down)


def adam_step(weight, moment, square, gradient):
    new_moment = beta_first * moment + (1.0 - beta_first) * gradient
    new_square = beta_second * square + (1.0 - beta_second) * gradient * gradient
    update = (
        new_moment / bias_first / (jnp.sqrt(new_square / bias_second) + adam_eps)
        + decay_rate * weight
    )
    return (weight - learn_rate * update, new_moment, new_square)


def to_slots(payload_x, payload_dy):
    moved_x, moved_dy = (
        lax.all_to_all(payload_x, ("grp", "dev"), split_axis=0, concat_axis=0, tiled=True),
        lax.all_to_all(payload_dy, ("grp", "dev"), split_axis=0, concat_axis=0, tiled=True),
    )
    return (moved_x, moved_dy)


def to_sources(payload_out, payload_dx):
    moved_out, moved_dx = (
        lax.all_to_all(payload_out, ("grp", "dev"), split_axis=0, concat_axis=0, tiled=True),
        lax.all_to_all(payload_dx, ("grp", "dev"), split_axis=0, concat_axis=0, tiled=True),
    )
    return (moved_out, moved_dx)


def on_device(
    tokens,
    cotangent,
    route_weight,
    slot_expert,
    targets,
    proj_in,
    first_in,
    second_in,
    proj_out,
    first_out,
    second_out,
):
    groups = lax.axis_size("grp")
    members = lax.axis_size("dev")
    slot_count = groups * members
    tok_count = tokens.shape[0]
    assigns = 2 * tok_count
    capacity = 3 * tok_count // slot_count
    buffer_rows = slot_count * capacity
    flat_target = targets.reshape(-1)
    onehot = (flat_target[:, None] == jnp.arange(slot_count, dtype=jnp.int32)[None, :]).astype(
        jnp.int32
    )
    earlier = jnp.cumsum(onehot, axis=0) - onehot
    position = jnp.sum(earlier * onehot, axis=1)
    within = position < capacity
    dest_row = jnp.where(within, flat_target * capacity + position, buffer_rows)
    matched = dest_row[:, None] == jnp.arange(buffer_rows, dtype=jnp.int32)[None, :]
    filled = jnp.any(matched, axis=0)
    source_id = jnp.sum(
        jnp.where(matched, jnp.arange(assigns, dtype=jnp.int32)[:, None], 0), axis=0
    )
    scaled = (
        route_weight.reshape(-1)[:, None] * jnp.repeat(cotangent, 2, axis=0).astype(jnp.float32)
    ).astype(jnp.bfloat16)
    send_x = jnp.where(filled[:, None], tokens[source_id // 2], jnp.zeros((), jnp.bfloat16))
    send_dy = jnp.where(filled[:, None], scaled[source_id], jnp.zeros((), jnp.bfloat16))
    slot_x, slot_dy = to_slots(
        send_x.reshape(slot_count, capacity, D), send_dy.reshape(slot_count, capacity, D)
    )
    slot_x = slot_x.reshape(buffer_rows, D)
    slot_dy = slot_dy.reshape(buffer_rows, D)
    my_group = lax.axis_index("grp")
    group_expert = lax.dynamic_slice_in_dim(slot_expert, my_group * members, members)
    low_in = proj_in.astype(jnp.bfloat16)
    low_out = proj_out.astype(jnp.bfloat16)
    all_up, all_down = (
        lax.all_gather(low_in, "grp", axis=0, tiled=True),
        lax.all_gather(low_out, "grp", axis=0, tiled=True),
    )
    send_up = jnp.take(all_up, group_expert, axis=0)
    send_down = jnp.take(all_down, group_expert, axis=0)
    got_up, got_down = (
        lax.all_to_all(send_up, "dev", split_axis=0, concat_axis=0, tiled=True),
        lax.all_to_all(send_down, "dev", split_axis=0, concat_axis=0, tiled=True),
    )
    slot_up = got_up.reshape(D, 2 * FF)
    slot_down = got_down.reshape(FF, D)
    result, rows_dx, grad_up, grad_down = slot_pass(slot_x, slot_dy, slot_up, slot_down)
    back_out, back_dx = to_sources(
        result.reshape(slot_count, capacity, D), rows_dx.reshape(slot_count, capacity, D)
    )
    flat_out = back_out.reshape(buffer_rows, D)
    flat_dx = back_dx.reshape(buffer_rows, D)
    pick_row = jnp.where(within, flat_target * capacity + position, 0)
    assigned_out = jnp.where(
        within[:, None], flat_out[pick_row], jnp.zeros((), jnp.bfloat16)
    ).reshape(tok_count, 2, D)
    assigned_dx = jnp.where(
        within[:, None], flat_dx[pick_row], jnp.zeros((), jnp.bfloat16)
    ).reshape(tok_count, 2, D)
    out_float = assigned_out.astype(jnp.float32)
    mixed = (
        route_weight[:, 0:1] * out_float[:, 0] + route_weight[:, 1:2] * out_float[:, 1]
    ).astype(jnp.bfloat16)
    token_grad = (
        assigned_dx[:, 0].astype(jnp.float32) + assigned_dx[:, 1].astype(jnp.float32)
    ).astype(jnp.bfloat16)
    mix_grad = jnp.sum(cotangent.astype(jnp.float32)[:, None, :] * out_float, axis=2)
    rows_up, rows_down = (
        lax.all_to_all(
            grad_up.reshape(members, D // members, 2 * FF),
            "dev",
            split_axis=0,
            concat_axis=0,
            tiled=True,
        ),
        lax.all_to_all(
            grad_down.reshape(members, FF // members, D),
            "dev",
            split_axis=0,
            concat_axis=0,
            tiled=True,
        ),
    )
    holder = (group_expert[None, :] == jnp.arange(E, dtype=jnp.int32)[:, None]).astype(jnp.bfloat16)
    part_up = jnp.einsum("ed,drc->erc", holder, rows_up, preferred_element_type=jnp.float32)
    part_down = jnp.einsum("ed,drc->erc", holder, rows_down, preferred_element_type=jnp.float32)
    sum_up, sum_down = (
        lax.psum_scatter(
            part_up.astype(jnp.bfloat16), "grp", scatter_dimension=0, tiled=True
        ).astype(jnp.float32),
        lax.psum_scatter(
            part_down.astype(jnp.bfloat16), "grp", scatter_dimension=0, tiled=True
        ).astype(jnp.float32),
    )
    trained_in, mean_in, square_in = adam_step(proj_in, first_in, second_in, sum_up)
    trained_out, mean_out, square_out = adam_step(proj_out, first_out, second_out, sum_down)
    return (
        mixed,
        token_grad,
        mix_grad,
        trained_in,
        mean_in,
        square_in,
        trained_out,
        mean_out,
        square_out,
    )


def solution(mesh):
    in_specs = (
        P(("grp", "dev"), None),
        P(("grp", "dev"), None),
        P(("grp", "dev"), None),
        P(),
        P(("grp", "dev"), None),
        P("grp", "dev", None),
        P("grp", "dev", None),
        P("grp", "dev", None),
        P("grp", "dev", None),
        P("grp", "dev", None),
        P("grp", "dev", None),
    )
    out_specs = (
        P(("grp", "dev"), None),
        P(("grp", "dev"), None),
        P(("grp", "dev"), None),
        P("grp", "dev", None),
        P("grp", "dev", None),
        P("grp", "dev", None),
        P("grp", "dev", None),
        P("grp", "dev", None),
        P("grp", "dev", None),
    )
    return jax.shard_map(
        on_device, mesh=mesh, in_specs=in_specs, out_specs=out_specs, check_vma=False
    )
```

profile of v0, /device:TPU:1, one launch (start us, length us, event | category | flops | bytes accessed | tf_op | source)
XLA Modules:
  0.0 679.6 jit_solution(7755972250965304729)
XLA Ops:
  7.3 2.8 convert_element_type.80
  10.5 1.0 broadcast_in_dim.114
  11.6 2.4 convert_element_type.87
  14.4 0.2 fusion.22
  14.7 0.2 fusion.24
  15.0 1.8 multiply_convert_fusion
  16.8 3.1 gather_fusion.4
  19.9 4.0 gather.35
  24.1 0.2 broadcast_in_dim.101
  24.3 3.1 gather_fusion
  27.5 5.2 gather.29
  32.6 4.3 broadcast_select_fusion.2
  36.9 44.3 %all_to_all.40 = bf16[128,3,2048]{2,1,0:T(4,128)(2,1)S(1)} all-to-all(bf16[128,3,2048]{2,1,0:T(4,128)(2,1)S(1)} %get-tuple-element.59), channel_id=1, replica_groups=mesh['grp'=4,'dev'=32] {'grp','dev'}, dimensions={0} | all-to-all | bytes 3145728 | tf_op jit(solution)/shard_map/all_to_all | solution.py:62
  81.3 7.1 %all-to-all-start.4 = ((bf16[128,3,2048]{2,1,0:T(4,128)(2,1)}), bf16[128,3,2048]{2,1,0:T(4,128)(2,1)}, u32[]{:S(2)}, u32[]{:S(2)}) async-start(bf16[128,3,2048]{2,1,0:T(4,128)(2,1)} %get-tuple-element.58), calls=%async_computation.4 | async-start | bytes 4194304 | tf_op jit(solution)/shard_map/all_to_all | solution.py:63
  88.5 7.2 %gather_fusion.1 = bf16[32,64,2048]{2,1,0:T(8,128)(2,1)} fusion(bf16[16,64,2048]{2,1,0:T(8,128)(2,1)} %all-gather.3.cloned.1.call-done, s32[1024]{0:T(1024)S(1)} %pad_clamp_fusion.2), kind=kCustom, calls=%fused_computation.1 | custom fusion | bytes 16777344 | tf_op jit(solution)/shard_map/jit(_take)/gather | solution.py:127
  95.7 7.5 %broadcast_select_fusion = bf16[32,64,2048]{2,1,0:T(8,128)(2,1)} fusion(bf16[32,64,2048]{2,1,0:T(8,128)(2,1)} %gather_fusion.1, pred[32]{0:T(512)(128)(4,1)S(1)} %get-tuple-element.53), kind=kLoop, calls=%fused_computation.8 | loop fusion | flops 4194304 | bytes 16777248 | tf_op jit(solution)/shard_map/jit(_take)/select_n | solution.py:127
  103.2 15.0 %all-to-all-done.4 = bf16[128,3,2048]{2,1,0:T(4,128)(2,1)} async-done(((bf16[128,3,2048]{2,1,0:T(4,128)(2,1)}), bf16[128,3,2048]{2,1,0:T(4,128)(2,1)}, u32[]{:S(2)}, u32[]{:S(2)}) %all-to-all-start.4) | async-done | bytes 1572896 | tf_op jit(solution)/shard_map/all_to_all | solution.py:63
  118.2 5.0 all-to-all-start.1
  123.2 2.1 convert_element_type.82
  125.3 106.8 %all-gather.5.cloned.1.call-done = bf16[16,32,2048]{2,1,0:T(8,128)(2,1)} async-done(((bf16[4,32,2048]{2,1,0:T(8,128)(2,1)}), bf16[16,32,2048]{2,1,0:T(8,128)(2,1)}) %all-gather.5.cloned.1.call-update) | async-done | bytes 2097168 | tf_op jit(solution)/shard_map/all_gather | solution.py:125
  232.2 4.4 gather_fusion.2
  236.5 4.6 broadcast_select_fusion.1
  241.2 7.3 %all-to-all-done.1 = bf16[32,64,2048]{2,1,0:T(8,128)(2,1)} async-done(((bf16[32,64,2048]{2,1,0:T(8,128)(2,1)}), bf16[32,64,2048]{2,1,0:T(8,128)(2,1)}, u32[]{:S(2)}, u32[]{:S(2)}) %all-to-all-start.1) | async-done | bytes 8388640 | tf_op jit(solution)/shard_map/all_to_all | solution.py:130
  248.4 13.3 %all-to-all-start.2 = ((bf16[32,32,2048]{2,1,0:T(8,128)(2,1)}), bf16[32,32,2048]{2,1,0:T(8,128)(2,1)}, u32[]{:S(2)}, u32[]{:S(2)}) async-start(bf16[32,32,2048]{2,1,0:T(8,128)(2,1)} %broadcast_select_fusion.1), calls=%async_computation.2 | async-start | bytes 8388608 | tf_op jit(solution)/shard_map/all_to_all | solution.py:131
  261.7 2.5 reshape.237
  264.2 5.2 reshape.242
  269.3 8.5 %fusion.40 = f32[384,2048]{1,0:T(8,128)} fusion(bf16[384,2048]{1,0:T(8,128)(2,1)S(1)} %copy-done.5, bf16[2048,2048]{1,0:T(8,128)(2,1)} %bitcast.4), kind=kOutput, calls=%fused_computation.89 | convolution fusion | flops 3221225472 | bytes 13107200 | tf_op jit(solution)/shard_map/dot_general | solution.py:26
  277.8 38.0 %all-to-all-done.2 = bf16[32,32,2048]{2,1,0:T(8,128)(2,1)} async-done(((bf16[32,32,2048]{2,1,0:T(8,128)(2,1)}), bf16[32,32,2048]{2,1,0:T(8,128)(2,1)}, u32[]{:S(2)}, u32[]{:S(2)}) %all-to-all-start.2) | async-done | bytes 4194336 | tf_op jit(solution)/shard_map/all_to_all | solution.py:131
  315.9 7.2 %multiply_convert_fusion.2 = (bf16[384,1024]{1,0:T(8,128)(2,1)}, bf16[384,1024]{1,0:T(8,128)(2,1)}, bf16[384,1024]{1,0:T(8,128)(2,1)S(1)}) fusion(f32[384,2048]{1,0:T(8,128)} %fusion.40, bf16[384,2048]{1,0:T(8,128)(2,1)} %reshape.242, bf16[1024,2048]{1,0:T(8,128)(2,1)} %bitcast.5), kind=kOutput, calls=%fused_computation.30 | convolution fusion | flops 1616510976 | bytes 11272192 | tf_op jit(solution)/shard_map/dot_general | solution.py:32
  323.0 4.4 convolution_convert_fusion.1
  327.4 8.8 %all-to-all-start.7 = ((bf16[32,32,2048]{2,1,0:T(8,128)(2,1)}), bf16[32,32,2048]{2,1,0:T(8,128)(2,1)}, u32[]{:S(2)}, u32[]{:S(2)}) async-start(bf16[32,32,2048]{2,1,0:T(8,128)(2,1)} %bitcast.54), calls=%async_computation.8 | async-start | bytes 8388608 | tf_op jit(solution)/shard_map/all_to_all | solution.py:164
  336.2 8.1 %convolution_convert_fusion = bf16[2048,2048]{1,0:T(8,128)(2,1)} fusion(bf16[384,2048]{1,0:T(8,128)(2,1)S(1)} %copy-done.5, bf16[384,1024]{1,0:T(8,128)(2,1)} %get-tuple-element.56, bf16[384,1024]{1,0:T(8,128)(2,1)} %get-tuple-element.55), kind=kOutput, calls=%fused_computation.9 | convolution fusion | flops 3228565504 | bytes 11534336 | tf_op jit(solution)/shard_map/dot_general | solution.py:41
  344.3 45.0 %all-to-all-done.7 = bf16[32,32,2048]{2,1,0:T(8,128)(2,1)} async-done(((bf16[32,32,2048]{2,1,0:T(8,128)(2,1)}), bf16[32,32,2048]{2,1,0:T(8,128)(2,1)}, u32[]{:S(2)}, u32[]{:S(2)}) %all-to-all-start.7) | async-done | bytes 4194336 | tf_op jit(solution)/shard_map/all_to_all | solution.py:164
  389.3 9.3 %all-to-all-start.6 = ((bf16[32,64,2048]{2,1,0:T(8,128)(2,1)}), bf16[32,64,2048]{2,1,0:T(8,128)(2,1)}, u32[]{:S(2)}, u32[]{:S(2)}) async-start(bf16[32,64,2048]{2,1,0:T(8,128)(2,1)} %bitcast.53), calls=%async_computation.6 | async-start | bytes 16777216 | tf_op jit(solution)/shard_map/all_to_all | solution.py:157
  398.7 6.8 fusion.7
  405.5 2.5 copy.90
  408.0 8.8 %reduce-scatter.3.cloned.1.call-start = ((), (), s32[]{:S(2)}) async-start(), calls=%async_computation.12 | async-start | bytes 5242880 | tf_op jit(solution)/shard_map/reduce_scatter | solution.py:176
  416.8 103.2 %all-to-all-done.6 = bf16[32,64,2048]{2,1,0:T(8,128)(2,1)} async-done(((bf16[32,64,2048]{2,1,0:T(8,128)(2,1)}), bf16[32,64,2048]{2,1,0:T(8,128)(2,1)}, u32[]{:S(2)}, u32[]{:S(2)}) %all-to-all-start.6) | async-done | bytes 8388640 | tf_op jit(solution)/shard_map/all_to_all | solution.py:157
  520.0 12.5 %fusion.4 = bf16[16,64,2048]{2,0,1:T(8,128)(2,1)S(1)} fusion(bf16[32,64,2048]{2,1,0:T(8,128)(2,1)} %all-to-all-done.6, s32[32]{0:T(128)S(1)} %get-tuple-element.54), kind=kOutput, calls=%fused_computation.14 | convolution fusion | flops 136315392 | bytes 12583040 | tf_op jit(solution)/shard_map/ed,drc->erc/dot_general | solution.py:173
  532.5 4.3 copy.88
  536.8 7.5 %convolution_convert_fusion.2 = bf16[384,2048]{1,0:T(8,128)(2,1)S(1)} fusion(bf16[2048,2048]{1,0:T(8,128)(2,1)} %bitcast.4, bf16[384,1024]{1,0:T(8,128)(2,1)} %get-tuple-element.56, bf16[384,1024]{1,0:T(8,128)(2,1)} %get-tuple-element.55), kind=kOutput, calls=%fused_computation.17 | convolution fusion | flops 3225157632 | bytes 11534336 | tf_op jit(solution)/shard_map/dot_general | solution.py:38
  544.3 2.3 reshape.243
  546.7 24.6 %all-to-all-start.5 = ((bf16[128,3,2048]{2,1,0:T(4,128)(2,1)}), bf16[128,3,2048]{2,1,0:T(4,128)(2,1)S(1)}, u32[]{:S(2)}, u32[]{:S(2)}) async-start(bf16[128,3,2048]{2,1,0:T(4,128)(2,1)} %reshape.243), calls=%async_computation.5 | async-start | bytes 4194304 | tf_op jit(solution)/shard_map/all_to_all | solution.py:71
  571.2 5.4 convolution_convert_fusion.3
  576.7 5.2 reshape.240
  581.8 22.4 %all-to-all-done.5 = bf16[128,3,2048]{2,1,0:T(4,128)(2,1)S(1)} async-done(((bf16[128,3,2048]{2,1,0:T(4,128)(2,1)}), bf16[128,3,2048]{2,1,0:T(4,128)(2,1)S(1)}, u32[]{:S(2)}, u32[]{:S(2)}) %all-to-all-start.5) | async-done | bytes 1572896 | tf_op jit(solution)/shard_map/all_to_all | solution.py:71
  604.2 1.3 copy-done.3
  605.5 7.5 %all-to-all-start.3 = ((bf16[128,3,2048]{2,1,0:T(4,128)(2,1)}), bf16[128,3,2048]{2,1,0:T(4,128)(2,1)}, u32[]{:S(2)}, u32[]{:S(2)}) async-start(bf16[128,3,2048]{2,1,0:T(4,128)(2,1)} %reshape.240), calls=%async_computation.3 | async-start | bytes 4194304 | tf_op jit(solution)/shard_map/all_to_all | solution.py:70
  613.3 0.2 lt.62
  613.6 3.9 reshape.244
  617.5 1.4 gather_fusion.5
  618.9 1.5 gather.37
  620.4 25.2 %all-to-all-done.3 = bf16[128,3,2048]{2,1,0:T(4,128)(2,1)} async-done(((bf16[128,3,2048]{2,1,0:T(4,128)(2,1)}), bf16[128,3,2048]{2,1,0:T(4,128)(2,1)}, u32[]{:S(2)}, u32[]{:S(2)}) %all-to-all-start.3) | async-done | bytes 1572896 | tf_op jit(solution)/shard_map/all_to_all | solution.py:70
  645.6 3.9 reshape.241
  649.5 2.3 gather_fusion.3
  651.8 2.7 gather.33
  654.5 1.6 multiply_reduce_fusion
  656.1 0.1 reduce_sum.38
  656.3 0.6 copy.91
  656.9 2.9 copy_select_fusion
  659.8 0.9 fusion.20
  660.7 1.0 fusion.17
  661.7 4.4 multiply_subtract_fusion.1
  666.1 6.5 multiply_subtract_fusion
  (61 shorter events, 1.9 us)
Async XLA Ops:
  7.2 17.2 %copy-start = (bf16[128,2048]{1,0:T(8,128)(2,1)S(1)}, bf16[128,2048]{1,0:T(8,128)(2,1)}, u32[]{:S(2)}) copy-start(bf16[128,2048]{1,0:T(8,128)(2,1)} %param.11) | copy-start | bytes 1572868
  7.2 2.9 copy-start.8
  7.2 3.3 copy-start.7
  7.2 81.3 %all-gather.3.cloned.1.call-start = ((), (), s32[]{:S(2)}) async-start(), calls=%async_computation.10 | async-start | bytes 5242880 | tf_op jit(solution)/shard_map/all_gather | solution.py:124
  11.5 2.5 copy-start.9
  81.3 7.1 %copy-start.10 = (s32[128]{0:T(128)S(1)}, s32[128]{0:T(128)}, u32[]{:S(2)}) copy-start(s32[128]{0:T(128)} %param.14) | copy-start | bytes 1540
  81.3 37.0 %all-to-all-start.4 = ((bf16[128,3,2048]{2,1,0:T(4,128)(2,1)}), bf16[128,3,2048]{2,1,0:T(4,128)(2,1)}, u32[]{:S(2)}, u32[]{:S(2)}) async-start(bf16[128,3,2048]{2,1,0:T(4,128)(2,1)} %get-tuple-element.58), calls=%async_computation.4 | async-start | bytes 4194304 | tf_op jit(solution)/shard_map/all_to_all | solution.py:63
  118.2 130.2 %all-to-all-start.1 = ((bf16[32,64,2048]{2,1,0:T(8,128)(2,1)}), bf16[32,64,2048]{2,1,0:T(8,128)(2,1)}, u32[]{:S(2)}, u32[]{:S(2)}) async-start(bf16[32,64,2048]{2,1,0:T(8,128)(2,1)} %broadcast_select_fusion), calls=%async_computation.1 | async-start | bytes 16777216 | tf_op jit(solution)/shard_map/all_to_all | solution.py:130
  123.2 109.0 %all-gather.5.cloned.1.call-start = ((), (), s32[]{:S(2)}) async-start(), calls=%async_computation.11 | async-start | bytes 2621440 | tf_op jit(solution)/shard_map/all_gather | solution.py:125
  248.4 67.5 %all-to-all-start.2 = ((bf16[32,32,2048]{2,1,0:T(8,128)(2,1)}), bf16[32,32,2048]{2,1,0:T(8,128)(2,1)}, u32[]{:S(2)}, u32[]{:S(2)}) async-start(bf16[32,32,2048]{2,1,0:T(8,128)(2,1)} %broadcast_select_fusion.1), calls=%async_computation.2 | async-start | bytes 8388608 | tf_op jit(solution)/shard_map/all_to_all | solution.py:131
  264.2 5.2 copy-start.5
  315.9 7.2 %copy-start.6 = (bf16[384,2048]{1,0:T(8,128)(2,1)S(1)}, bf16[384,2048]{1,0:T(8,128)(2,1)}, u32[]{:S(2)}) copy-start(bf16[384,2048]{1,0:T(8,128)(2,1)} %reshape.242) | copy-start | bytes 4718596
  323.0 4.4 copy-start.11
  327.4 61.9 %all-to-all-start.7 = ((bf16[32,32,2048]{2,1,0:T(8,128)(2,1)}), bf16[32,32,2048]{2,1,0:T(8,128)(2,1)}, u32[]{:S(2)}, u32[]{:S(2)}) async-start(bf16[32,32,2048]{2,1,0:T(8,128)(2,1)} %bitcast.54), calls=%async_computation.8 | async-start | bytes 8388608 | tf_op jit(solution)/shard_map/all_to_all | solution.py:164
  389.3 130.7 %all-to-all-start.6 = ((bf16[32,64,2048]{2,1,0:T(8,128)(2,1)}), bf16[32,64,2048]{2,1,0:T(8,128)(2,1)}, u32[]{:S(2)}, u32[]{:S(2)}) async-start(bf16[32,64,2048]{2,1,0:T(8,128)(2,1)} %bitcast.53), calls=%async_computation.6 | async-start | bytes 16777216 | tf_op jit(solution)/shard_map/all_to_all | solution.py:157
  398.7 263.0 %reduce-scatter.5.cloned.1.call-start = ((), (), s32[]{:S(2)}) async-start(), calls=%async_computation.13 | async-start | bytes 2621440 | tf_op jit(solution)/shard_map/reduce_scatter | solution.py:179
  408.0 258.0 %reduce-scatter.3.cloned.1.call-start = ((), (), s32[]{:S(2)}) async-start(), calls=%async_computation.12 | async-start | bytes 5242880 | tf_op jit(solution)/shard_map/reduce_scatter | solution.py:176
  546.7 57.5 %all-to-all-start.5 = ((bf16[128,3,2048]{2,1,0:T(4,128)(2,1)}), bf16[128,3,2048]{2,1,0:T(4,128)(2,1)S(1)}, u32[]{:S(2)}, u32[]{:S(2)}) async-start(bf16[128,3,2048]{2,1,0:T(4,128)(2,1)} %reshape.243), calls=%async_computation.5 | async-start | bytes 4194304 | tf_op jit(solution)/shard_map/all_to_all | solution.py:71
  604.2 1.3 copy-start.3
  605.5 40.0 %all-to-all-start.3 = ((bf16[128,3,2048]{2,1,0:T(4,128)(2,1)}), bf16[128,3,2048]{2,1,0:T(4,128)(2,1)}, u32[]{:S(2)}, u32[]{:S(2)}) async-start(bf16[128,3,2048]{2,1,0:T(4,128)(2,1)} %reshape.240), calls=%async_computation.3 | async-start | bytes 4194304 | tf_op jit(solution)/shard_map/all_to_all | solution.py:70
  651.8 2.7 copy-start.2
  661.7 4.4 copy-start.4
  666.1 6.5 copy-start.1
Sparse Core Ops, SparseCore 0:
  10.3 72.6 all-gather.2
  126.3 105.8 all-gather.4
  408.2 106.6 reduce-scatter.4
  537.0 107.0 reduce-scatter.2
where the time goes:
time: 689 us; the launch traced here: 680 us
  waiting for transfers between devices  363 us (53%)
  starting transfers between devices  84.4 us (12%)
  local copies, waits for them, and re-layouts  71.8 us (10%)
  matrix products  60.3 us (9%)
  blocking collectives  44.3 us (6%)
  other arithmetic  41.2 us (6%)
  between operations  14.5 us (2%)
    all_gather x1, waiting for transfers between devices, on_device(): lax.all_gather(low_out, 'grp', axis=0, tiled=True)  107 us
    all_to_all x1, waiting for transfers between devices, on_device(): lax.all_to_all(grad_up.reshape(members, D // members, 2 * FF), 'dev', spl...  103 us
    all_to_all x1, waiting for transfers between devices, on_device(): lax.all_to_all(grad_down.reshape(members, FF // members, D), 'dev', split...  45 us
    all_to_all x1, blocking collectives, to_slots(): lax.all_to_all(payload_x, ('grp', 'dev'), split_axis=0, concat_axis=0, ti...  44.3 us
    all_to_all x1, waiting for transfers between devices, on_device(): lax.all_to_all(send_down, 'dev', split_axis=0, concat_axis=0, tiled=True)  38 us
    all_to_all x1, waiting for transfers between devices, to_sources(): lax.all_to_all(payload_out, ('grp', 'dev'), split_axis=0, concat_axis=0,...  25.2 us
    all_to_all x1, starting transfers between devices, to_sources(): lax.all_to_all(payload_dx, ('grp', 'dev'), split_axis=0, concat_axis=0, t...  24.6 us
    all_to_all x1, waiting for transfers between devices, to_sources(): lax.all_to_all(payload_dx, ('grp', 'dev'), split_axis=0, concat_axis=0, t...  22.4 us
  transfers between devices with their start and end apart: 11, of which 8 were waited for; matrix products, arithmetic and copies ran while one was open for 22% of the time, Pallas kernels for 0%

commit v1 on v0

v1 whole, which is shorter than its diff:
```python
import jax
import jax.numpy as jnp
from jax import lax
from jax.experimental import pallas as pl
from jax.experimental.pallas import tpu as pltpu
from jax.sharding import Mesh, PartitionSpec as P

D = 2048
FF = 1024
E = 16
CAP = 3
UNITS = 8
CHIPS = 64
ROWS = CHIPS * UNITS
HALF = 1024

BF = jnp.bfloat16
F32 = jnp.float32

beta_first = 0.9
beta_second = 0.95
learn_rate = 0.01
decay_rate = 0.1
adam_eps = 1e-08
bias_first = 1.0 - 0.9**10
bias_second = 1.0 - 0.95**10

CHIP_AXES = ("yl", "x", "z", "yh")
DEV_AXES = ("x", "z", "yh")
ALL_AXES = ("yl", "core", "x", "z", "yh")


def params(mib=48):
    return pltpu.CompilerParams(vmem_limit_bytes=mib * 2**20)


def adam_step(weight, moment, square, gradient):
    new_moment = beta_first * moment + (1.0 - beta_first) * gradient
    new_square = beta_second * square + (1.0 - beta_second) * gradient * gradient
    update = (
        new_moment / bias_first / (jnp.sqrt(new_square / bias_second) + adam_eps)
        + decay_rate * weight
    )
    return (weight - learn_rate * update, new_moment, new_square)


def dispatch_kernel(tcol, trow, ecol, erow, wrow, tok, cot, send, dest):
    sub = lax.broadcasted_iota(jnp.int32, (128, 128), 0).astype(F32)
    lane = lax.broadcasted_iota(jnp.int32, (128, 128), 1).astype(F32)
    one, zero = jnp.float32(1.0), jnp.float32(0.0)

    def down(mask, value):
        return jnp.sum(jnp.where(mask, value, zero), axis=0, keepdims=True)

    def across(mask, value):
        return jnp.sum(jnp.where(mask, value, zero), axis=1, keepdims=True)

    tc = [tcol[:, k : k + 1].astype(F32) for k in range(2)]
    tr = [trow[k : k + 1, :].astype(F32) for k in range(2)]
    ec, er = ecol[...].astype(F32), erow[...].astype(F32)
    chips_row = jnp.floor((CAP * down(ec == lane, one) + (UNITS - 1)) / UNITS)
    chips_col = jnp.floor((CAP * across(er == sub, one) + (UNITS - 1)) / UNITS)
    base_col = UNITS * across(lane < ec, chips_row) + CAP * across((ec == er) & (lane < sub), one)
    base_row = UNITS * down(sub < er, chips_col) + CAP * down((ec == er) & (sub < lane), one)
    dest_row = []
    for k in range(2):
        pos_row = down((tc[0] == tr[k]) & (sub < lane), one) + down((tc[1] == tr[k]) & (sub < lane), one)
        pos_col = across((tc[k] == tr[0]) & (lane < sub), one) + across((tc[k] == tr[1]) & (lane < sub), one)
        at_row = down(sub == tr[k], base_col)
        at_col = across(lane == tc[k], base_row)
        dest_row.append(jnp.where(pos_row < CAP, at_row + pos_row, 4.0 * ROWS))
        dest[:, k : k + 1] = jnp.where(pos_col < CAP, at_col + pos_col, 4.0 * ROWS)
    w0, w1 = wrow[0:1, :], wrow[1:2, :]
    for part in range(ROWS // 128):
        place = sub + 128.0 * part
        first, second = place == dest_row[0], place == dest_row[1]
        pick = jnp.where(first | second, one, zero).astype(BF)
        weight = across(first, w0) + across(second, w1)
        rows = slice(part * 128, part * 128 + 128)
        send[rows, :D] = jnp.dot(pick, tok[...], preferred_element_type=F32).astype(BF)
        send[rows, D:] = (jnp.dot(pick, cot[...], preferred_element_type=F32) * weight).astype(BF)


def dispatch(targets, slot_expert, route_weight, tokens, cotangent):
    return pl.pallas_call(
        dispatch_kernel,
        out_shape=(
            jax.ShapeDtypeStruct((ROWS, 2 * D), BF),
            jax.ShapeDtypeStruct((128, 2), F32),
        ),
        compiler_params=params(),
        name="dispatch",
    )(
        targets,
        targets.T,
        slot_expert.reshape(128, 1),
        slot_expert.reshape(1, 128),
        route_weight.T,
        tokens,
        cotangent,
    )


def combine_kernel(dest, weight, cot, back, mixed, grad, mix):
    place = lax.broadcasted_iota(jnp.int32, (128, ROWS), 1).astype(F32)
    first, second = place == dest[:, 0:1], place == dest[:, 1:2]
    one, zero = jnp.float32(1.0), jnp.float32(0.0)
    pick0 = jnp.where(first, one, zero).astype(BF)
    pick1 = jnp.where(second, one, zero).astype(BF)
    both = jnp.where(first | second, one, zero).astype(BF)
    w0, w1 = weight[:, 0:1], weight[:, 1:2]
    mix0 = jnp.zeros((128, 1), F32)
    mix1 = jnp.zeros((128, 1), F32)
    width = 512
    for c in range(D // width):
        cols = slice(c * width, (c + 1) * width)
        out0 = jnp.dot(pick0, back[:, cols], preferred_element_type=F32)
        out1 = jnp.dot(pick1, back[:, cols], preferred_element_type=F32)
        here = cot[:, cols].astype(F32)
        mixed[:, cols] = (w0 * out0 + w1 * out1).astype(BF)
        mix0 += jnp.sum(here * out0, axis=1, keepdims=True)
        mix1 += jnp.sum(here * out1, axis=1, keepdims=True)
        dcols = slice(D + c * width, D + (c + 1) * width)
        grad[:, cols] = jnp.dot(both, back[:, dcols], preferred_element_type=F32).astype(BF)
    mix[:, 0:1] = mix0
    mix[:, 1:2] = mix1


def combine(dest, route_weight, cotangent, back):
    return pl.pallas_call(
        combine_kernel,
        out_shape=(
            jax.ShapeDtypeStruct((128, D), BF),
            jax.ShapeDtypeStruct((128, D), BF),
            jax.ShapeDtypeStruct((128, 2), F32),
        ),
        compiler_params=params(),
        name="combine",
    )(dest, route_weight, cotangent, back)


def select_kernel(index, near, far, out):
    step = pl.program_id(0)
    for j in range(8):
        e = index[step * 8 + j]

        @pl.when(e < 8)
        def _():
            out[j] = near[jnp.minimum(e, 7)]

        @pl.when(e >= 8)
        def _():
            out[j] = far[jnp.maximum(e - 8, 0)]


def select_rows(index, near, far):
    n, r, c = near.shape
    return pl.pallas_call(
        select_kernel,
        grid_spec=pltpu.PrefetchScalarGridSpec(
            num_scalar_prefetch=1,
            grid=(4,),
            in_specs=[
                pl.BlockSpec((n, r, c), lambda i, s: (0, 0, 0)),
                pl.BlockSpec((n, r, c), lambda i, s: (0, 0, 0)),
            ],
            out_specs=pl.BlockSpec((8, r, c), lambda i, s: (i, 0, 0)),
        ),
        out_shape=jax.ShapeDtypeStruct((32, r, c), BF),
        compiler_params=params(),
        name="select_rows",
    )(index, near, far)


def sum_kernel(index, rows, out, total):
    total[...] = jnp.zeros_like(total)
    for d in range(32):
        e = index[d]
        total[e] += rows[d].astype(F32)
    out[...] = total[...].astype(BF)


def sum_rows(index, rows):
    n, r, c = rows.shape
    step = 16
    return pl.pallas_call(
        sum_kernel,
        grid_spec=pltpu.PrefetchScalarGridSpec(
            num_scalar_prefetch=1,
            grid=(r // step,),
            in_specs=[pl.BlockSpec((n, step, c), lambda i, s: (0, i, 0))],
            out_specs=pl.BlockSpec((E, step, c), lambda i, s: (0, i, 0)),
            scratch_shapes=[pltpu.VMEM((E, step, c), F32)],
        ),
        out_shape=jax.ShapeDtypeStruct((E, r, c), BF),
        compiler_params=params(),
        name="sum_rows",
    )(index, rows)


def dot(a, b):
    return jnp.dot(a, b, preferred_element_type=F32)


def dot_nt(a, b):
    return lax.dot_general(a, b, (((1,), (1,)), ((), ())), preferred_element_type=F32)


def dot_tn(a, b):
    return lax.dot_general(a, b, (((0,), (0,)), ((), ())), preferred_element_type=F32)


def over_core(v):
    return lax.ppermute(v, "core", [(0, 1), (1, 0)])


def over_y(v):
    return lax.ppermute(v, "yl", [(0, 1), (1, 0)])


def on_device(
    tokens,
    cotangent,
    route_weight,
    slot_expert,
    targets,
    proj_in,
    first_in,
    second_in,
    proj_out,
    first_out,
    second_out,
):
    core = lax.axis_index("core")
    yl = lax.axis_index("yl")
    is0 = core == 0

    def half_of(v, which):
        return lax.dynamic_slice_in_dim(v, which * HALF, HALF, axis=v.ndim - 1)

    near, far = [], []
    for w in (proj_in, proj_out):
        low = w.astype(BF)
        mine = half_of(low, core)
        theirs = over_core(half_of(low, 1 - core))
        both = jnp.concatenate([mine, theirs], axis=0)
        near.append(both)
        far.append(over_y(both))

    ids = jnp.arange(E, dtype=jnp.int32)
    count = jnp.sum((slot_expert[:, None] == ids[None, :]).astype(jnp.int32), axis=0)
    chips = (CAP * count + UNITS - 1) // UNITS
    start = jnp.sum(jnp.where(ids[:, None] < ids[None, :], chips[:, None], 0), axis=0)
    here = yl * 32 + jnp.arange(32, dtype=jnp.int32)
    expert = jnp.sum((start[None, :] <= here[:, None]).astype(jnp.int32), axis=1) - 1
    index = ((expert >> 3) ^ yl) * 8 + (((expert >> 2) & 1) ^ core) * 4 + (expert & 3)

    send, dest = dispatch(targets, slot_expert, route_weight, tokens, cotangent)
    got = lax.all_to_all(
        send.reshape(CHIPS, UNITS, 2 * D), CHIP_AXES, split_axis=0, concat_axis=0, tiled=True
    ).reshape(ROWS, 2 * D)
    x, dy = got[:, :D], got[:, D:]

    def spread(v):
        return lax.all_to_all(v, DEV_AXES, split_axis=0, concat_axis=0, tiled=True)

    own_in = spread(select_rows(index, near[0], far[0])).reshape(D, HALF)
    own_out = spread(select_rows(index, near[1], far[1])).reshape(FF, HALF)
    oth_in = over_core(own_in)
    oth_out = over_core(own_out)

    one, two = dot(x, own_in), dot(x, oth_in)
    gating = jnp.where(is0, one, two)
    upward = jnp.where(is0, two, one)
    logistic = jax.nn.sigmoid(gating)
    active = gating * logistic
    derivative = logistic * (1.0 + gating * (1.0 - logistic))
    hidden = (active * upward).astype(BF)

    dy_own, dy_oth = half_of(dy, core), half_of(dy, 1 - core)
    give_out = over_core(dot_tn(hidden, dy_oth).astype(BF))
    grad_out = (dot_tn(hidden, dy_own) + give_out.astype(F32)).astype(BF)
    rows_out = spread(grad_out.reshape(32, 32, HALF))

    dhidden = dot_nt(dy_own, own_out) + dot_nt(dy_oth, oth_out)
    d_gate = dhidden * upward * derivative
    d_up = dhidden * active
    d_own = jnp.where(is0, d_gate, d_up).astype(BF)
    d_oth = jnp.where(is0, d_up, d_gate).astype(BF)
    give_in = over_core(dot_tn(x, d_oth).astype(BF))
    grad_in = (dot_tn(x, d_own) + give_in.astype(F32)).astype(BF)
    rows_in = spread(grad_in.reshape(32, 64, HALF))

    res_own, res_oth = dot(hidden, own_out).astype(BF), dot(hidden, oth_out).astype(BF)
    rows_dx = (dot_nt(d_own, own_in) + dot_nt(d_oth, oth_in)).astype(BF)
    result = jnp.concatenate(
        [jnp.where(is0, res_own, res_oth), jnp.where(is0, res_oth, res_own), rows_dx], axis=1
    )
    back = lax.all_to_all(
        result.reshape(CHIPS, UNITS, 2 * D), CHIP_AXES, split_axis=0, concat_axis=0, tiled=True
    ).reshape(ROWS, 2 * D)
    mixed, token_grad, mix_grad = combine(dest, route_weight, cotangent, back)

    def collect(rows):
        part = sum_rows(index, rows)
        r = rows.shape[1]
        part = part.reshape(2, 2, 4, r, HALF)
        other = over_core(part[:, 1])
        ours = part[:, 0]
        come_ours, come_other = over_y(jnp.stack([ours[1], other[1]]))
        sum_ours = ours[0].astype(F32) + come_ours.astype(F32)
        sum_other = other[0].astype(F32) + come_other.astype(F32)
        return jnp.concatenate(
            [jnp.where(is0, sum_ours, sum_other), jnp.where(is0, sum_other, sum_ours)], axis=2
        )

    sum_out = collect(rows_out)
    sum_in = collect(rows_in)
    trained_in, mean_in, square_in = adam_step(proj_in, first_in, second_in, sum_in)
    trained_out, mean_out, square_out = adam_step(proj_out, first_out, second_out, sum_out)
    return (
        mixed,
        token_grad,
        mix_grad,
        trained_in,
        mean_in,
        square_in,
        trained_out,
        mean_out,
        square_out,
    )


def solution(mesh):
    fine = Mesh(mesh.devices.reshape(2, 2, 4, 4, 2), ALL_AXES)
    rows = P(ALL_AXES, None)
    state = P(("yl", "core"), DEV_AXES, None)
    in_specs = (rows, rows, rows, P(), rows) + (state,) * 6
    out_specs = (rows, rows, rows) + (state,) * 6
    return jax.shard_map(on_device, mesh=fine, in_specs=in_specs, out_specs=out_specs, check_vma=False)
```

time: 689 us -> 448 us (0.65)
  waiting for transfers between devices: 363 us -> 277 us
  local copies, waits for them, and re-layouts: 71.8 us -> 7.96 us
  blocking collectives: 44.3 us -> 0 us
  other arithmetic: 41.2 us -> 16.3 us
  Pallas kernels: 0 us -> 17.6 us
  between operations: 14.5 us -> 1.08 us
  starting transfers between devices: 84.4 us -> 72.9 us
  matrix products: 60.3 us -> 49.4 us
    all_gather x2 -> x0, waiting for transfers between devices: 107 us -> none  [the longest x1 107 us: on_device(): lax.all_gather(low_out, 'grp', axis=0, tiled=True)]
    ppermute x0 -> x12, waiting for transfers between devices: none -> 86.1 us  [the longest x4 72.3 us: over_y(): return lax.ppermute(v, 'yl', [(0, 1), (1, 0)])]
    all_to_all x7 -> x6, waiting for transfers between devices: 256 us -> 191 us  [the longest x4 109 us: spread(): return lax.all_to_all(v, DEV_AXES, split_axis=0, concat_axis=0, tiled=True)]
    all_to_all x1 -> x0, blocking collectives: 44.3 us -> none  [to_slots(): lax.all_to_all(payload_x, ('grp', 'dev'), split_axis=0, concat_axis=0, ti...]
    gather x10 -> x0, local copies, waits for them, and re-layouts: 34.9 us -> none  [the longest x2 8.3 us: on_device(): tokens[source_id // 2]]
    reshape x6 -> x1, local copies, waits for them, and re-layouts: 23 us -> 0.11 us  [dispatch(): slot_expert.reshape(128, 1)]
    pallas_call x0 -> x6, Pallas kernels: none -> 17.6 us  [the longest x2 5.92 us: sum_rows(): pl.pallas_call(sum_kernel, grid_spec=pltpu.PrefetchScalarGridSpec(num_sca...]
    all_to_all x7 -> x6, starting transfers between devices: 75.5 us -> 58.7 us  [the longest x4 37.7 us: spread(): return lax.all_to_all(v, DEV_AXES, split_axis=0, concat_axis=0, tiled=True)]
  transfers between devices with their start and end apart: 11 -> 18, of which waited for: 8 -> 13; matrix products, arithmetic and copies ran while one was open for 22% -> 10% of each run, Pallas kernels for 0% -> 3%
where the time goes in v1:
time: 448 us; the launch traced here: 442 us
  waiting for transfers between devices  277 us (62%)
  starting transfers between devices  72.9 us (16%)
  matrix products  49.4 us (11%)
  Pallas kernels  17.6 us (4%)
  other arithmetic  16.3 us (4%)
  local copies, waits for them, and re-layouts  7.96 us (2%)
    all_to_all x4, waiting for transfers between devices, spread(): return lax.all_to_all(v, DEV_AXES, split_axis=0, concat_axis=0, tiled=True)  109 us
    ppermute x4, waiting for transfers between devices, over_y(): return lax.ppermute(v, 'yl', [(0, 1), (1, 0)])  72.3 us
    all_to_all x1, waiting for transfers between devices, on_device(): lax.all_to_all(send.reshape(CHIPS, UNITS, 2 * D), CHIP_AXES, split_axis=0...  47 us
    all_to_all x4, starting transfers between devices, spread(): return lax.all_to_all(v, DEV_AXES, split_axis=0, concat_axis=0, tiled=True)  37.7 us
    all_to_all x1, waiting for transfers between devices, on_device(): lax.all_to_all(result.reshape(CHIPS, UNITS, 2 * D), CHIP_AXES, split_axis...  35.1 us
    dot_general x4, matrix products, dot_tn(): lax.dot_general(a, b, (((0,), (0,)), ((), ())), preferred_element_type=F32)  17.9 us
    dot_general x4, matrix products, dot(): return jnp.dot(a, b, preferred_element_type=F32)  16.1 us
    dot_general x4, matrix products, dot_nt(): lax.dot_general(a, b, (((1,), (1,)), ((), ())), preferred_element_type=F32)  15.4 us
  transfers between devices with their start and end apart: 18, of which 13 were waited for; matrix products, arithmetic and copies ran while one was open for 10% of the time, Pallas kernels for 3%

profile of v1, /device:TPU:1, one launch (start us, length us, event | category | flops | bytes accessed | tf_op | source)
XLA Modules:
  0.0 442.3 jit_solution(11090459782045329993)
XLA Ops:
  0.7 1.3 convert_element_type.92
  2.0 1.5 collective-permute-start.3
  3.5 0.1 convert_reduce_fusion.1
  3.6 1.0 collective-permute-done.3
  4.7 1.5 collective-permute-start.4
  6.4 11.6 %collective-permute-done.4.far = bf16[8,32,1024]{2,1,0:T(8,128)(2,1)S(1)} collective-permute-done((bf16[8,32,1024]{2,1,0:T(8,128)(2,1)S(1)}, bf16[8,32,1024]{2,1,0:T(8,128)(2,1)S(1)}, u32[]{:S(2)}, u32[]{:S(2)}) %collective-permute-start.4) | collective-permute-done | bytes 524320 | tf_op jit(solution)/shard_map/ppermute | solution.py:218
  17.9 2.6 select_rows.3
  20.5 10.9 %all-to-all-start.2 = ((bf16[32,32,1024]{2,1,0:T(8,128)(2,1)}), bf16[32,32,1024]{2,1,0:T(8,128)(2,1)}, u32[]{:S(2)}, u32[]{:S(2)}) async-start(bf16[32,32,1024]{2,1,0:T(8,128)(2,1)} %select_rows.3), calls=%async_computation.2 | async-start | bytes 4194304 | tf_op jit(solution)/shard_map/all_to_all | solution.py:265
  31.4 0.1 convert_element_type.90
  31.7 1.6 collective-permute-start
  33.2 1.5 collective-permute-done
  34.8 0.5 collective-permute-start.1
  35.3 41.4 %collective-permute-done.1.far = bf16[8,64,1024]{2,1,0:T(8,128)(2,1)S(1)} collective-permute-done((bf16[8,64,1024]{2,1,0:T(8,128)(2,1)S(1)}, bf16[8,64,1024]{2,1,0:T(8,128)(2,1)S(1)}, u32[]{:S(2)}, u32[]{:S(2)}) %collective-permute-start.1) | collective-permute-done | bytes 1048608 | tf_op jit(solution)/shard_map/ppermute | solution.py:218
  76.7 3.3 select_rows.2
  80.0 12.6 %all-to-all-start.1 = ((bf16[32,64,1024]{2,1,0:T(8,128)(2,1)}), bf16[32,64,1024]{2,1,0:T(8,128)(2,1)}, u32[]{:S(2)}, u32[]{:S(2)}) async-start(bf16[32,64,1024]{2,1,0:T(8,128)(2,1)} %select_rows.2), calls=%async_computation.1 | async-start | bytes 8388608 | tf_op jit(solution)/shard_map/all_to_all | solution.py:265
  92.7 0.1 copy.27.ecol
  92.8 0.1 copy.26.tcol
  92.9 1.5 dispatch.1
  94.4 2.0 copy-done
  96.5 49.6 %all-to-all-done.1 = bf16[32,64,1024]{2,1,0:T(8,128)(2,1)} async-done(((bf16[32,64,1024]{2,1,0:T(8,128)(2,1)}), bf16[32,64,1024]{2,1,0:T(8,128)(2,1)}, u32[]{:S(2)}, u32[]{:S(2)}) %all-to-all-start.1) | async-done | bytes 4194336 | tf_op jit(solution)/shard_map/all_to_all | solution.py:265
  146.1 9.9 %all-to-all-start = ((bf16[64,8,4096]{2,1,0:T(8,128)(2,1)}), bf16[64,8,4096]{2,1,0:T(8,128)(2,1)}, u32[]{:S(2)}, u32[]{:S(2)}) async-start(bf16[64,8,4096]{2,1,0:T(8,128)(2,1)} %bitcast.83), calls=%async_computation | async-start | bytes 8388608 | tf_op jit(solution)/shard_map/all_to_all | solution.py:259
  156.0 1.6 collective-permute-start.2
  157.6 0.3 collective-permute-start.5
  157.9 47.0 %all-to-all-done = bf16[64,8,4096]{2,1,0:T(8,128)(2,1)} async-done(((bf16[64,8,4096]{2,1,0:T(8,128)(2,1)}), bf16[64,8,4096]{2,1,0:T(8,128)(2,1)}, u32[]{:S(2)}, u32[]{:S(2)}) %all-to-all-start) | async-done | bytes 4194336 | tf_op jit(solution)/shard_map/all_to_all | solution.py:259
  204.8 1.7 slice.65
  206.6 1.3 fusion.13
  207.9 5.1 %fusion.7 = f32[512,1024]{1,0:T(8,128)S(1)} fusion(bf16[2048,1024]{1,0:T(8,128)(2,1)} %bitcast.6, bf16[512,4096]{1,0:T(8,128)(2,1)} %bitcast.5), kind=kOutput, calls=%fused_computation.26 | convolution fusion | flops 2147483648 | bytes 8388608 | tf_op jit(solution)/shard_map/dot_general | solution.py:202
  213.1 5.2 %fusion.5 = f32[512,1024]{1,0:T(8,128)S(1)} fusion(bf16[2048,1024]{1,0:T(8,128)(2,1)} %collective-permute-done.2, bf16[512,4096]{1,0:T(8,128)(2,1)} %bitcast.5), kind=kOutput, calls=%fused_computation.24 | convolution fusion | flops 2147483648 | bytes 8388608 | tf_op jit(solution)/shard_map/dot_general | solution.py:202
  218.2 4.9 %select_convert_fusion.1 = (bf16[512,1024]{1,0:T(8,128)(2,1)}, bf16[512,1024]{1,0:T(8,128)(2,1)S(1)}, bf16[512,1024]{1,0:T(8,128)(2,1)S(1)}) fusion(pred[]{:T(512)S(6)} %eq.16, f32[512,1024]{1,0:T(8,128)S(1)} %fusion.7, f32[512,1024]{1,0:T(8,128)S(1)} %fusion.5, f32[512,1024]{1,0:T(8,128)S(1)} %fusion.13, bf16[1024,1024]{1,0:T(8,128)(2,1)} %bitcast.7, ...), kind=kOutput, calls=%fused_computation.11 | convolution fusion | flops 1084227584 | bytes 12582917 | tf_op jit(solution)/shard_map/dot_general | solution.py:206
  223.1 6.4 %convolution_convert_fusion = bf16[2048,1024]{1,0:T(8,128)(2,1)} fusion(bf16[512,1024]{1,0:T(8,128)(2,1)S(1)} %get-tuple-element.44, bf16[512,4096]{1,0:T(8,128)(2,1)} %bitcast.5), kind=kOutput, calls=%fused_computation.4 | convolution fusion | flops 2149580800 | bytes 7340032 | tf_op jit(solution)/shard_map/dot_general | solution.py:210
  229.5 4.8 %collective-permute-start.6 = (bf16[2048,1024]{1,0:T(8,128)(2,1)}, bf16[2048,1024]{1,0:T(8,128)(2,1)}, u32[]{:S(2)}, u32[]{:S(2)}) collective-permute-start(bf16[2048,1024]{1,0:T(8,128)(2,1)} %convolution_convert_fusion), channel_id=1, source_target_pairs={{0,32},{32,0},{1,33},{33,1},{2,34},{34,2},{3,35},{35,3},{4,36},{36... | collective-permute-start | bytes 12582920 | tf_op jit(solution)/shard_map/ppermute | solution.py:214
  234.2 1.3 convolution_convert_fusion.1
  235.6 8.4 %collective-permute-done.9 = bf16[1024,1024]{1,0:T(8,128)(2,1)S(1)} collective-permute-done((bf16[1024,1024]{1,0:T(8,128)(2,1)S(1)}, bf16[1024,1024]{1,0:T(8,128)(2,1)S(1)}, u32[]{:S(2)}, u32[]{:S(2)}) %collective-permute-start.9) | collective-permute-done | bytes 2097184 | tf_op jit(solution)/shard_map/ppermute | solution.py:214
  244.0 2.6 add_convert_fusion.1
  246.7 7.3 %all-to-all-start.5 = ((bf16[32,32,1024]{2,1,0:T(8,128)(2,1)}), bf16[32,32,1024]{2,1,0:T(8,128)(2,1)S(1)}, u32[]{:S(2)}, u32[]{:S(2)}) async-start(bf16[32,32,1024]{2,1,0:T(8,128)(2,1)} %bitcast.89), calls=%async_computation.5 | async-start | bytes 4194304 | tf_op jit(solution)/shard_map/all_to_all | solution.py:265
  254.0 7.6 %add_convert_fusion = bf16[2048,1024]{1,0:T(8,128)(2,1)} fusion(bf16[2048,1024]{1,0:T(8,128)(2,1)} %collective-permute-done.6, bf16[512,1024]{1,0:T(8,128)(2,1)} %get-tuple-element.43, bf16[512,4096]{1,0:T(8,128)(2,1)} %bitcast.5), kind=kOutput, calls=%fused_computation | convolution fusion | flops 2153775104 | bytes 11534336 | tf_op jit(solution)/shard_map/dot_general | solution.py:210
  261.6 22.2 %all-to-all-done.5.rows = bf16[32,32,1024]{2,1,0:T(8,128)(2,1)S(1)} async-done(((bf16[32,32,1024]{2,1,0:T(8,128)(2,1)}), bf16[32,32,1024]{2,1,0:T(8,128)(2,1)S(1)}, u32[]{:S(2)}, u32[]{:S(2)}) %all-to-all-start.5) | async-done | bytes 2097184 | tf_op jit(solution)/shard_map/all_to_all | solution.py:265
  283.8 6.9 %all-to-all-start.4 = ((bf16[32,64,1024]{2,1,0:T(8,128)(2,1)}), bf16[32,64,1024]{2,1,0:T(8,128)(2,1)}, u32[]{:S(2)}, u32[]{:S(2)}) async-start(bf16[32,64,1024]{2,1,0:T(8,128)(2,1)} %bitcast.88), calls=%async_computation.4 | async-start | bytes 8388608 | tf_op jit(solution)/shard_map/all_to_all | solution.py:265
  290.6 2.9 convolution_convert_fusion.2
  293.5 3.0 broadcast_select_fusion.1
  296.5 4.7 %fusion.26 = f32[512,2048]{1,0:T(8,128)S(1)} fusion(bf16[512,1024]{1,0:T(8,128)(2,1)S(1)} %copy-done.18, bf16[2048,1024]{1,0:T(8,128)(2,1)} %collective-permute-done.2), kind=kOutput, calls=%fused_computation.81 | convolution fusion | flops 2147483648 | bytes 9437184 | tf_op jit(solution)/shard_map/dot_general | solution.py:206
  301.2 4.6 %add_convert_fusion.2 = bf16[512,2048]{1,0:T(8,128)(2,1)S(1)} fusion(f32[512,2048]{1,0:T(8,128)S(1)} %fusion.26, bf16[512,1024]{1,0:T(8,128)(2,1)S(1)} %copy-done.19, bf16[2048,1024]{1,0:T(8,128)(2,1)} %bitcast.6), kind=kOutput, calls=%fused_computation.3 | convolution fusion | flops 2149580800 | bytes 11534336 | tf_op jit(solution)/shard_map/dot_general | solution.py:206
  305.7 2.1 maximum_bitcast_fusion
  307.9 37.1 %all-to-all-done.4.rows = bf16[32,64,1024]{2,1,0:T(8,128)(2,1)} async-done(((bf16[32,64,1024]{2,1,0:T(8,128)(2,1)}), bf16[32,64,1024]{2,1,0:T(8,128)(2,1)}, u32[]{:S(2)}, u32[]{:S(2)}) %all-to-all-start.4) | async-done | bytes 4194336 | tf_op jit(solution)/shard_map/all_to_all | solution.py:265
  345.0 11.1 %all-to-all-start.3 = ((bf16[64,8,4096]{2,1,0:T(8,128)(2,1)}), bf16[64,8,4096]{2,1,0:T(8,128)(2,1)}, u32[]{:S(2)}, u32[]{:S(2)}) async-start(bf16[64,8,4096]{2,1,0:T(8,128)(2,1)} %maximum_bitcast_fusion), calls=%async_computation.3 | async-start | bytes 8388608 | tf_op jit(solution)/shard_map/all_to_all | solution.py:299
  356.1 1.6 sum_rows.3
  357.7 4.4 sum_rows.2
  362.1 1.0 collective-permute-start.7
  363.2 2.9 collective-permute-done.10
  366.1 0.8 copy-done.15
  366.9 0.8 pad_maximum_fusion.5
  367.8 1.4 collective-permute-start.11
  369.2 1.0 copy-done.13
  370.2 1.1 pad_maximum_fusion.2
  371.5 35.1 %all-to-all-done.3 = bf16[64,8,4096]{2,1,0:T(8,128)(2,1)} async-done(((bf16[64,8,4096]{2,1,0:T(8,128)(2,1)}), bf16[64,8,4096]{2,1,0:T(8,128)(2,1)}, u32[]{:S(2)}, u32[]{:S(2)}) %all-to-all-start.3) | async-done | bytes 4194336 | tf_op jit(solution)/shard_map/all_to_all | solution.py:299
  406.5 1.0 copy-done.2
  407.6 4.3 combine.1
  411.8 0.6 copy.31
  412.5 1.8 collective-permute-done.11
  414.3 1.3 bitcast_select_fusion.3
  415.6 3.6 multiply_subtract_fusion.1
  419.2 17.5 %collective-permute-done.8 = bf16[2,4,64,1024]{3,2,1,0:T(8,128)(2,1)} collective-permute-done((bf16[2,4,64,1024]{3,2,1,0:T(8,128)(2,1)}, bf16[2,4,64,1024]{3,2,1,0:T(8,128)(2,1)}, u32[]{:S(2)}, u32[]{:S(2)}) %collective-permute-start.8) | collective-permute-done | bytes 1048608 | tf_op jit(solution)/shard_map/ppermute | solution.py:218
  436.8 1.6 bitcast_select_fusion.1
  438.4 3.9 multiply_subtract_fusion
  (60 shorter events, 1.2 us)
Async XLA Ops:
  0.6 2.9 copy-start.6
  2.0 2.7 collective-permute-start.3
  4.7 13.2 %collective-permute-start.4 = (bf16[8,32,1024]{2,1,0:T(8,128)(2,1)S(1)}, bf16[8,32,1024]{2,1,0:T(8,128)(2,1)S(1)}, u32[]{:S(2)}, u32[]{:S(2)}) collective-permute-start(bf16[8,32,1024]{2,1,0:T(8,128)(2,1)S(1)} %pad_maximum_fusion.4.near), channel_id=1, source_target_pairs={{0,64},{64,0},{1,65},{65,1},{2,66},{66,2},{3,67},{67,3},{4,68},{68... | collective-permute-start | bytes 1572872 | tf_op jit(solution)/shard_map/ppermute | solution.py:218
  20.5 10.9 %copy-start.7 = (f32[4,64,2048]{2,1,0:T(8,128)S(1)}, f32[4,64,2048]{2,1,0:T(8,128)}, u32[]{:S(2)}) copy-start(f32[4,64,2048]{2,1,0:T(8,128)} %param.16) | copy-start | bytes 6291460
  20.5 59.5 %all-to-all-start.2 = ((bf16[32,32,1024]{2,1,0:T(8,128)(2,1)}), bf16[32,32,1024]{2,1,0:T(8,128)(2,1)}, u32[]{:S(2)}, u32[]{:S(2)}) async-start(bf16[32,32,1024]{2,1,0:T(8,128)(2,1)} %select_rows.3), calls=%async_computation.2 | async-start | bytes 4194304 | tf_op jit(solution)/shard_map/all_to_all | solution.py:265
  31.7 3.1 collective-permute-start
  34.8 41.8 %collective-permute-start.1 = (bf16[8,64,1024]{2,1,0:T(8,128)(2,1)S(1)}, bf16[8,64,1024]{2,1,0:T(8,128)(2,1)S(1)}, u32[]{:S(2)}, u32[]{:S(2)}) collective-permute-start(bf16[8,64,1024]{2,1,0:T(8,128)(2,1)S(1)} %pad_maximum_fusion.1.near), channel_id=1, source_target_pairs={{0,64},{64,0},{1,65},{65,1},{2,66},{66,2},{3,67},{67,3},{4,68},{68... | collective-permute-start | bytes 3145736 | tf_op jit(solution)/shard_map/ppermute | solution.py:218
  80.0 12.8 %copy-start.4 = (s32[128,2]{0,1:T(2,128)S(1)}, s32[128,2]{0,1:T(2,128)}, u32[]{:S(2)}) copy-start(s32[128,2]{0,1:T(2,128)} %param.15) | copy-start | bytes 3076
  80.0 12.9 %copy-start.1 = (bf16[128,2048]{1,0:T(8,128)(2,1)S(1)}, bf16[128,2048]{1,0:T(8,128)(2,1)}, u32[]{:S(2)}) copy-start(bf16[128,2048]{1,0:T(8,128)(2,1)} %cot.3) | copy-start | bytes 1572868
  80.0 12.9 %copy-start.3 = (bf16[128,2048]{1,0:T(8,128)(2,1)S(1)}, bf16[128,2048]{1,0:T(8,128)(2,1)}, u32[]{:S(2)}) copy-start(bf16[128,2048]{1,0:T(8,128)(2,1)} %tok.1) | copy-start | bytes 1572868
  80.0 12.9 %copy-start.5 = (f32[128,2]{0,1:T(2,128)S(1)}, f32[128,2]{0,1:T(2,128)}, u32[]{:S(2)}) copy-start(f32[128,2]{0,1:T(2,128)} %param.13) | copy-start | bytes 3076
  80.0 66.1 %all-to-all-start.1 = ((bf16[32,64,1024]{2,1,0:T(8,128)(2,1)}), bf16[32,64,1024]{2,1,0:T(8,128)(2,1)}, u32[]{:S(2)}, u32[]{:S(2)}) async-start(bf16[32,64,1024]{2,1,0:T(8,128)(2,1)} %select_rows.2), calls=%async_computation.1 | async-start | bytes 8388608 | tf_op jit(solution)/shard_map/all_to_all | solution.py:265
  94.4 2.0 copy-start
  146.1 58.7 %all-to-all-start = ((bf16[64,8,4096]{2,1,0:T(8,128)(2,1)}), bf16[64,8,4096]{2,1,0:T(8,128)(2,1)}, u32[]{:S(2)}, u32[]{:S(2)}) async-start(bf16[64,8,4096]{2,1,0:T(8,128)(2,1)} %bitcast.83), calls=%async_computation | async-start | bytes 8388608 | tf_op jit(solution)/shard_map/all_to_all | solution.py:259
  156.0 57.1 %collective-permute-start.2 = (bf16[2048,1024]{1,0:T(8,128)(2,1)}, bf16[2048,1024]{1,0:T(8,128)(2,1)}, u32[]{:S(2)}, u32[]{:S(2)}) collective-permute-start(bf16[2048,1024]{1,0:T(8,128)(2,1)} %bitcast.6), channel_id=1, source_target_pairs={{0,32},{32,0},{1,33},{33,1},{2,34},{34,2},{3,35},{35,3},{4,36},{36... | collective-permute-start | bytes 12582920 | tf_op jit(solution)/shard_map/ppermute | solution.py:214
  157.6 49.0 %collective-permute-start.5 = (bf16[1024,1024]{1,0:T(8,128)(2,1)}, bf16[1024,1024]{1,0:T(8,128)(2,1)S(1)}, u32[]{:S(2)}, u32[]{:S(2)}) collective-permute-start(bf16[1024,1024]{1,0:T(8,128)(2,1)} %bitcast.7), channel_id=1, source_target_pairs={{0,32},{32,0},{1,33},{33,1},{2,34},{34,2},{3,35},{35,3},{4,36},{36... | collective-permute-start | bytes 6291464 | tf_op jit(solution)/shard_map/ppermute | solution.py:214
  206.6 1.3 copy-start.16
  223.1 6.4 %copy-start.17 = (bf16[512,1024]{1,0:T(8,128)(2,1)}, bf16[512,1024]{1,0:T(8,128)(2,1)S(1)}, u32[]{:S(2)}) copy-start(bf16[512,1024]{1,0:T(8,128)(2,1)S(1)} %get-tuple-element.44) | copy-start | bytes 3145732
  229.5 24.5 %collective-permute-start.6 = (bf16[2048,1024]{1,0:T(8,128)(2,1)}, bf16[2048,1024]{1,0:T(8,128)(2,1)}, u32[]{:S(2)}, u32[]{:S(2)}) collective-permute-start(bf16[2048,1024]{1,0:T(8,128)(2,1)} %convolution_convert_fusion), channel_id=1, source_target_pairs={{0,32},{32,0},{1,33},{33,1},{2,34},{34,2},{3,35},{35,3},{4,36},{36... | collective-permute-start | bytes 12582920 | tf_op jit(solution)/shard_map/ppermute | solution.py:214
  235.6 8.5 %collective-permute-start.9 = (bf16[1024,1024]{1,0:T(8,128)(2,1)S(1)}, bf16[1024,1024]{1,0:T(8,128)(2,1)S(1)}, u32[]{:S(2)}, u32[]{:S(2)}) collective-permute-start(bf16[1024,1024]{1,0:T(8,128)(2,1)S(1)} %convolution_convert_fusion.1), channel_id=1, source_target_pairs={{0,32},{32,0},{1,33},{33,1},{2,34},{34,2},{3,35},{35,3},{4,36},{36... | collective-permute-start | bytes 6291464 | tf_op jit(solution)/shard_map/ppermute | solution.py:214
  246.7 37.1 %all-to-all-start.5 = ((bf16[32,32,1024]{2,1,0:T(8,128)(2,1)}), bf16[32,32,1024]{2,1,0:T(8,128)(2,1)S(1)}, u32[]{:S(2)}, u32[]{:S(2)}) async-start(bf16[32,32,1024]{2,1,0:T(8,128)(2,1)} %bitcast.89), calls=%async_computation.5 | async-start | bytes 4194304 | tf_op jit(solution)/shard_map/all_to_all | solution.py:265
  283.8 61.2 %all-to-all-start.4 = ((bf16[32,64,1024]{2,1,0:T(8,128)(2,1)}), bf16[32,64,1024]{2,1,0:T(8,128)(2,1)}, u32[]{:S(2)}, u32[]{:S(2)}) async-start(bf16[32,64,1024]{2,1,0:T(8,128)(2,1)} %bitcast.88), calls=%async_computation.4 | async-start | bytes 8388608 | tf_op jit(solution)/shard_map/all_to_all | solution.py:265
  293.5 3.0 copy-start.18
  296.5 4.7 %copy-start.19 = (bf16[512,1024]{1,0:T(8,128)(2,1)S(1)}, bf16[512,1024]{1,0:T(8,128)(2,1)}, u32[]{:S(2)}) copy-start(bf16[512,1024]{1,0:T(8,128)(2,1)} %get-tuple-element.43) | copy-start | bytes 3145732
  345.0 61.6 %all-to-all-start.3 = ((bf16[64,8,4096]{2,1,0:T(8,128)(2,1)}), bf16[64,8,4096]{2,1,0:T(8,128)(2,1)}, u32[]{:S(2)}, u32[]{:S(2)}) async-start(bf16[64,8,4096]{2,1,0:T(8,128)(2,1)} %maximum_bitcast_fusion), calls=%async_computation.3 | async-start | bytes 8388608 | tf_op jit(solution)/shard_map/all_to_all | solution.py:299
  362.1 7.1 %collective-permute-start.7 = (bf16[2,4,64,1024]{3,2,1,0:T(8,128)(2,1)S(1)}, bf16[2,4,64,1024]{3,2,1,0:T(8,128)(2,1)S(1)}, u32[]{:S(2)}, u32[]{:S(2)}) collective-permute-start(bf16[2,4,64,1024]{3,2,1,0:T(8,128)(2,1)S(1)} %slice_bitcast_fusion), channel_id=1, source_target_pairs={{0,32},{32,0},{1,33},{33,1},{2,34},{34,2},{3,35},{35,3},{4,36},{36... | collective-permute-start | bytes 3145736 | tf_op jit(solution)/shard_map/ppermute | solution.py:214
  363.1 3.0 collective-permute-start.10
  366.1 0.8 copy-start.15
  367.8 46.5 %collective-permute-start.11 = (bf16[2,4,32,1024]{3,2,1,0:T(8,128)(2,1)}, bf16[2,4,32,1024]{3,2,1,0:T(8,128)(2,1)}, u32[]{:S(2)}, u32[]{:S(2)}) collective-permute-start(bf16[2,4,32,1024]{3,2,1,0:T(8,128)(2,1)} %pad_maximum_fusion.5), channel_id=1, source_target_pairs={{0,64},{64,0},{1,65},{65,1},{2,66},{66,2},{3,67},{67,3},{4,68},{68... | collective-permute-start | bytes 1572872 | tf_op jit(solution)/shard_map/ppermute | solution.py:218
  369.2 1.0 copy-start.13
  371.3 65.5 %collective-permute-start.8 = (bf16[2,4,64,1024]{3,2,1,0:T(8,128)(2,1)}, bf16[2,4,64,1024]{3,2,1,0:T(8,128)(2,1)}, u32[]{:S(2)}, u32[]{:S(2)}) collective-permute-start(bf16[2,4,64,1024]{3,2,1,0:T(8,128)(2,1)} %pad_maximum_fusion.2), channel_id=1, source_target_pairs={{0,64},{64,0},{1,65},{65,1},{2,66},{66,2},{3,67},{67,3},{4,68},{68... | collective-permute-start | bytes 3145736 | tf_op jit(solution)/shard_map/ppermute | solution.py:218
  406.5 1.0 copy-start.2
  412.5 3.1 copy-start.9
  412.5 3.1 copy-start.12
  415.6 21.2 %copy-start.14 = (bf16[2,4,64,1024]{3,2,1,0:T(8,128)(2,1)S(1)}, bf16[2,4,64,1024]{3,2,1,0:T(8,128)(2,1)}, u32[]{:S(2)}) copy-start(bf16[2,4,64,1024]{3,2,1,0:T(8,128)(2,1)} %copy-done.13) | copy-start | bytes 3145732
  415.6 22.8 %copy-start.11 = (f32[4,64,2048]{2,1,0:T(8,128)S(1)}, f32[4,64,2048]{2,1,0:T(8,128)}, u32[]{:S(2)}) copy-start(f32[4,64,2048]{2,1,0:T(8,128)} %param.18) | copy-start | bytes 6291460
  419.2 19.2 %copy-start.8 = (f32[4,64,2048]{2,1,0:T(8,128)S(1)}, f32[4,64,2048]{2,1,0:T(8,128)}, u32[]{:S(2)}) copy-start(f32[4,64,2048]{2,1,0:T(8,128)} %param.16) | copy-start | bytes 6291460
  419.2 19.2 %copy-start.10 = (f32[4,64,2048]{2,1,0:T(8,128)S(1)}, f32[4,64,2048]{2,1,0:T(8,128)}, u32[]{:S(2)}) copy-start(f32[4,64,2048]{2,1,0:T(8,128)} %param.17) | copy-start | bytes 6291460

commit v2 on v1

v2 whole, which is shorter than its diff:
```python
import jax
import jax.numpy as jnp
from jax import lax
from jax.experimental import pallas as pl
from jax.experimental.pallas import tpu as pltpu
from jax.sharding import Mesh, PartitionSpec as P

D = 2048
FF = 1024
E = 16
CAP = 3
UNITS = 8
CHIPS = 64
ROWS = CHIPS * UNITS
HALF = 1024
HERE = 32
FAR = 4

BF = jnp.bfloat16
F32 = jnp.float32

beta_first = 0.9
beta_second = 0.95
learn_rate = 0.01
decay_rate = 0.1
adam_eps = 1e-08
bias_first = 1.0 - 0.9**10
bias_second = 1.0 - 0.95**10

CHIP_AXES = ("yl", "x", "z", "yh")
DEV_AXES = ("x", "z", "yh")
SEND_AXES = ("yh", "x", "z")
ALL_AXES = ("yl", "core", "x", "z", "yh")


def params(mib=48):
    return pltpu.CompilerParams(vmem_limit_bytes=mib * 2**20)


SHORT = pl.CostEstimate(flops=1, bytes_accessed=1, transcendentals=0)
LONG = pl.CostEstimate(flops=10**10, bytes_accessed=2 * 10**7, transcendentals=0)


def adam_step(weight, moment, square, gradient):
    new_moment = beta_first * moment + (1.0 - beta_first) * gradient
    new_square = beta_second * square + (1.0 - beta_second) * gradient * gradient
    update = (
        new_moment / bias_first / (jnp.sqrt(new_square / bias_second) + adam_eps)
        + decay_rate * weight
    )
    return (weight - learn_rate * update, new_moment, new_square)


def down(mask, value=1.0):
    return jnp.sum(jnp.where(mask, value, 0.0), axis=0, keepdims=True)


def across(mask, value=1.0):
    return jnp.sum(jnp.where(mask, value, 0.0), axis=1, keepdims=True)


def grids():
    sub = lax.broadcasted_iota(jnp.int32, (128, 128), 0).astype(F32)
    lane = lax.broadcasted_iota(jnp.int32, (128, 128), 1).astype(F32)
    return sub, lane


def plan_kernel(ecol, erow, plan, slot_rows, slot_cols):
    sub, lane = grids()
    ec, er = ecol[...].astype(F32), erow[...].astype(F32)

    chips_r = jnp.floor((CAP * down(ec == lane) + (UNITS - 1)) / UNITS)
    chips_c = jnp.floor((CAP * across(er == sub) + (UNITS - 1)) / UNITS)
    expert = (sub < E) & (lane < E)
    low_s, low_l = sub < E // 2, lane < E // 2
    same = expert & (low_s == low_l)
    ahead_r = same & ((chips_c > chips_r) | ((chips_c == chips_r) & (sub < lane)))
    ahead_c = same & ((chips_r > chips_c) | ((chips_r == chips_c) & (lane < sub)))
    rank_r = down(ahead_r)
    over_r = jnp.maximum(down(same, chips_c) - HERE, 0.0)
    over_c = jnp.maximum(across(same, chips_r) - HERE, 0.0)
    spill_r = jnp.clip(over_r - down(ahead_r, chips_c), 0.0, chips_r)
    spill_c = jnp.clip(over_c - across(ahead_c, chips_r), 0.0, chips_c)
    keep_r, keep_c = chips_r - spill_r, chips_c - spill_c
    across_y = expert & (low_s != low_l)
    kept_r = down(same & (sub < lane), keep_c)
    kept_c = across(same & (lane < sub), keep_r)
    spilt_r = down(across_y, keep_c) + down(same & (sub < lane), spill_c)
    spilt_c = across(across_y, keep_r) + across(same & (lane < sub), spill_r)
    y_r = jnp.where(low_l[0:1, :], 0.0, 1.0 * HERE)
    y_c = jnp.where(low_s[:, 0:1], 0.0, 1.0 * HERE)
    kept_r, kept_c = kept_r + y_r, kept_c + y_c
    spilt_r, spilt_c = spilt_r + (HERE - y_r), spilt_c + (HERE - y_c)
    for i, v in enumerate((rank_r, keep_r, spill_r, kept_r, spilt_r)):
        plan[i : i + 1, :] = v.astype(jnp.int32)

    mine_c, mine_r = ec == lane, er == sub
    slot_cols[:, 0:1] = CAP * across((ec == er) & (lane < sub))
    slot_rows[0:1, :] = CAP * down((ec == er) & (sub < lane))
    for i, (r, c) in enumerate(((keep_r, keep_c), (kept_r, kept_c), (spilt_r - keep_r, spilt_c - keep_c))):
        slot_cols[:, i + 1 : i + 2] = UNITS * across(mine_c, r)
        slot_rows[i + 1 : i + 2, :] = UNITS * down(mine_r, c)


def make_plan(slot_expert):
    return pl.pallas_call(
        plan_kernel,
        out_shape=(
            jax.ShapeDtypeStruct((8, 128), jnp.int32),
            jax.ShapeDtypeStruct((8, 128), F32),
            jax.ShapeDtypeStruct((128, 8), F32),
        ),
        compiler_params=params(),
        name="plan",
    )(slot_expert.reshape(128, 1), slot_expert.reshape(1, 128))


def dispatch_kernel(tcol, trow, slot_rows, slot_cols, wrow, tok, cot, send, dest):
    sub, lane = grids()
    tc = [tcol[:, k : k + 1].astype(F32) for k in range(2)]
    tr = [trow[k : k + 1, :].astype(F32) for k in range(2)]
    dest_row = []
    for k in range(2):
        at = sub == tr[k]
        pos = down((tc[0] == tr[k]) & (sub < lane)) + down((tc[1] == tr[k]) & (sub < lane))
        slot, limit, first, rest = (down(at, slot_cols[:, i : i + 1]) for i in range(4))
        unit = slot + pos
        row = unit + jnp.where(unit < limit, first, rest)
        dest_row.append(jnp.where(pos < CAP, row, 4.0 * ROWS))
        at = lane == tc[k]
        pos = across((tc[k] == tr[0]) & (lane < sub)) + across((tc[k] == tr[1]) & (lane < sub))
        slot, limit, first, rest = (across(at, slot_rows[i : i + 1, :]) for i in range(4))
        unit = slot + pos
        row = unit + jnp.where(unit < limit, first, rest)
        dest[:, k : k + 1] = jnp.where(pos < CAP, row, 4.0 * ROWS)

    w0, w1 = wrow[0:1, :], wrow[1:2, :]
    for part in range(ROWS // 128):
        place = sub + 128.0 * part
        first, second = place == dest_row[0], place == dest_row[1]
        pick = jnp.where(first | second, 1.0, 0.0).astype(BF)
        weight = across(first, w0) + across(second, w1)
        rows = slice(part * 128, part * 128 + 128)
        send[rows, :D] = jnp.dot(pick, tok[...], preferred_element_type=F32).astype(BF)
        send[rows, D:] = (jnp.dot(pick, cot[...], preferred_element_type=F32) * weight).astype(BF)


def dispatch(targets, slot_rows, slot_cols, route_weight, tokens, cotangent):
    return pl.pallas_call(
        dispatch_kernel,
        out_shape=(
            jax.ShapeDtypeStruct((ROWS, 2 * D), BF),
            jax.ShapeDtypeStruct((128, 2), F32),
        ),
        compiler_params=params(),
        name="dispatch",
    )(targets, targets.T, slot_rows, slot_cols, route_weight.T, tokens, cotangent)


def combine_kernel(dest, weight, cot, back, mixed, grad, mix):
    place = lax.broadcasted_iota(jnp.int32, (128, ROWS), 1).astype(F32)
    first, second = place == dest[:, 0:1], place == dest[:, 1:2]
    one, zero = jnp.float32(1.0), jnp.float32(0.0)
    pick0 = jnp.where(first, one, zero).astype(BF)
    pick1 = jnp.where(second, one, zero).astype(BF)
    both = jnp.where(first | second, one, zero).astype(BF)
    w0, w1 = weight[:, 0:1], weight[:, 1:2]
    mix0 = jnp.zeros((128, 1), F32)
    mix1 = jnp.zeros((128, 1), F32)
    width = 512
    for c in range(D // width):
        cols = slice(c * width, (c + 1) * width)
        out0 = jnp.dot(pick0, back[:, cols], preferred_element_type=F32)
        out1 = jnp.dot(pick1, back[:, cols], preferred_element_type=F32)
        here = cot[:, cols].astype(F32)
        mixed[:, cols] = (w0 * out0 + w1 * out1).astype(BF)
        mix0 += jnp.sum(here * out0, axis=1, keepdims=True)
        mix1 += jnp.sum(here * out1, axis=1, keepdims=True)
        dcols = slice(D + c * width, D + (c + 1) * width)
        grad[:, cols] = jnp.dot(both, back[:, dcols], preferred_element_type=F32).astype(BF)
    mix[:, 0:1] = mix0
    mix[:, 1:2] = mix1


def combine(dest, route_weight, cotangent, back):
    return pl.pallas_call(
        combine_kernel,
        out_shape=(
            jax.ShapeDtypeStruct((128, D), BF),
            jax.ShapeDtypeStruct((128, D), BF),
            jax.ShapeDtypeStruct((128, 2), F32),
        ),
        compiler_params=params(),
        name="combine",
    )(dest, route_weight, cotangent, back)


def prepare_kernel(core, w_in, w_out, mine, theirs):
    left_in, right_in = w_in[:, :, :HALF].astype(BF), w_in[:, :, HALF:].astype(BF)
    left_out, right_out = w_out[:, :, :HALF].astype(BF), w_out[:, :, HALF:].astype(BF)

    def put(left, right):
        left[:, :64], right[:, :64] = left_in, right_in
        left[:, 64:], right[:, 64:] = left_out, right_out

    @pl.when(core[0] == 0)
    def _():
        put(mine, theirs)

    @pl.when(core[0] != 0)
    def _():
        put(theirs, mine)


def prepare(core, w_in, w_out):
    n, r, c = w_in.shape
    ro = w_out.shape[1]
    half = pl.BlockSpec((1, r + ro, HALF), lambda i, s: (i, 0, 0))
    return pl.pallas_call(
        prepare_kernel,
        grid_spec=pltpu.PrefetchScalarGridSpec(
            num_scalar_prefetch=1,
            grid=(n,),
            in_specs=[
                pl.BlockSpec((1, r, c), lambda i, s: (i, 0, 0)),
                pl.BlockSpec((1, ro, c), lambda i, s: (i, 0, 0)),
            ],
            out_specs=[half, half],
        ),
        out_shape=[jax.ShapeDtypeStruct((n, r + ro, HALF), BF)] * 2,
        compiler_params=params(),
        name="prepare",
    )(core, w_in, w_out)


def copy_one(e, parts, out, j):
    for k, part in enumerate(parts):

        @pl.when((e >= 4 * k) & (e < 4 * k + 4))
        def _(k=k, part=part):
            out[j] = part[jnp.clip(e - 4 * k, 0, 3)]


def take_kernel(index, mine, theirs, out):
    for j in range(FAR):
        copy_one(index[j], (mine, theirs), out, j)


def take_rows(index, mine, theirs):
    n, r, c = mine.shape
    whole = pl.BlockSpec((n, r, c), lambda i, s: (0, 0, 0))
    return pl.pallas_call(
        take_kernel,
        grid_spec=pltpu.PrefetchScalarGridSpec(
            num_scalar_prefetch=1, grid=(1,), in_specs=[whole] * 2, out_specs=whole
        ),
        out_shape=jax.ShapeDtypeStruct((FAR, r, c), BF),
        compiler_params=params(),
        name="take_rows",
    )(index, mine, theirs)


def select_kernel(index, mine, theirs, far, out):
    step = pl.program_id(0)
    for j in range(8):
        copy_one(index[step * 8 + j], (mine, theirs, far), out, j)


def select_rows(index, mine, theirs, far, start, r):
    c = mine.shape[2]
    part = pl.BlockSpec((4, r, c), lambda i, s: (0, start // r, 0))
    return pl.pallas_call(
        select_kernel,
        grid_spec=pltpu.PrefetchScalarGridSpec(
            num_scalar_prefetch=1,
            grid=(4,),
            in_specs=[part] * 3,
            out_specs=pl.BlockSpec((8, r, c), lambda i, s: (i, 0, 0)),
        ),
        out_shape=jax.ShapeDtypeStruct((32, r, c), BF),
        compiler_params=params(),
        name="select_rows",
    )(index, mine, theirs, far)


def sum_kernel(index, rows, mine, theirs, far, total):
    total[...] = jnp.zeros_like(total)
    for d in range(32):
        e = index[d]
        total[e] += rows[d].astype(F32)
    mine[...] = total[:4].astype(BF)
    theirs[...] = total[4:8].astype(BF)
    far[...] = total[8:].astype(BF)


def sum_rows(index, rows):
    n, r, c = rows.shape
    step = 16
    return pl.pallas_call(
        sum_kernel,
        grid_spec=pltpu.PrefetchScalarGridSpec(
            num_scalar_prefetch=1,
            grid=(r // step,),
            in_specs=[pl.BlockSpec((n, step, c), lambda i, s: (0, i, 0))],
            out_specs=[pl.BlockSpec((4, step, c), lambda i, s: (0, i, 0))] * 3,
            scratch_shapes=[pltpu.VMEM((8 + FAR, step, c), F32)],
        ),
        out_shape=[jax.ShapeDtypeStruct((4, r, c), BF)] * 3,
        compiler_params=params(),
        cost_estimate=LONG,
        name="sum_rows",
    )(index, rows)


def adam_kernel(sel, weight, moment, square, near0, near1, far0, far1, new_w, new_m, new_s):
    has_far = (sel[1 + pl.program_id(0)] < FAR).astype(F32)
    for h in range(2):
        cols = slice(h * HALF, (h + 1) * HALF)
        own = sel[0] == h
        near = jnp.where(own, near0[...], near1[...]).astype(F32)
        far = jnp.where(own, far0[...], far1[...]).astype(F32)
        new_w[:, :, cols], new_m[:, :, cols], new_s[:, :, cols] = adam_step(
            weight[:, :, cols], moment[:, :, cols], square[:, :, cols], near + has_far * far
        )


def adam(sel, weight, moment, square, near0, near1, far0, far1):
    n, r, c = weight.shape
    state = pl.BlockSpec((1, r, c), lambda i, s: (i, 0, 0))
    near = pl.BlockSpec((1, r, HALF), lambda i, s: (i, 0, 0))
    far = pl.BlockSpec((1, r, HALF), lambda i, s: (jnp.minimum(s[1 + i], FAR - 1), 0, 0))
    return pl.pallas_call(
        adam_kernel,
        grid_spec=pltpu.PrefetchScalarGridSpec(
            num_scalar_prefetch=1,
            grid=(n,),
            in_specs=[state] * 3 + [near] * 2 + [far] * 2,
            out_specs=[state] * 3,
        ),
        out_shape=[jax.ShapeDtypeStruct((n, r, c), F32)] * 3,
        compiler_params=params(),
        cost_estimate=LONG,
        name="adam",
    )(sel, weight, moment, square, near0, near1, far0, far1)


def rows_of(w):
    return jnp.concatenate([w[y, i] for i in range(w.shape[1]) for y in range(2)], axis=0)


def put_rows(out, v):
    r = out.shape[2]
    for i in range(out.shape[1]):
        for y in range(2):
            out[y, i] = v[(2 * i + y) * r : (2 * i + y + 1) * r].astype(BF)


def call(kernel, core, args, in_specs, out_shape, out_specs, steps, name, cost=SHORT):
    return pl.pallas_call(
        kernel,
        grid_spec=pltpu.PrefetchScalarGridSpec(
            num_scalar_prefetch=1, grid=(steps,), in_specs=in_specs, out_specs=out_specs
        ),
        out_shape=out_shape,
        compiler_params=params(56),
        cost_estimate=cost,
        name=name,
    )(core, *args)


def hidden_kernel(core, x, own, oth, hidden, hidden_t, active, steep):
    one, two = dot(x[...], rows_of(own)), dot(x[...], rows_of(oth))
    is0 = core[0] == 0
    gating, upward = jnp.where(is0, one, two), jnp.where(is0, two, one)
    logistic = jax.nn.sigmoid(gating)
    act = gating * logistic
    hid = act * upward
    hidden[...] = hid.astype(BF)
    hidden_t[...] = hid.T.astype(BF)
    active[...] = act
    steep[...] = upward * (logistic * (1.0 + gating * (1.0 - logistic)))


def other_hidden_kernel(core, x, own, oth, hidden_t):
    one, two = dot(x[...], rows_of(own)), dot(x[...], rows_of(oth))
    is0 = core[0] == 0
    gating, upward = jnp.where(is0, one, two), jnp.where(is0, two, one)
    hidden_t[...] = (gating * jax.nn.sigmoid(gating) * upward).T.astype(BF)


def other_hidden_of(core, got, own, oth):
    w = pl.BlockSpec((2, 16, 64, 256), lambda j, s: (0, 0, 0, j))
    return call(
        other_hidden_kernel,
        core,
        (got, own, oth),
        [pl.BlockSpec((ROWS, D), lambda j, s: (0, 0)), w, w],
        jax.ShapeDtypeStruct((FF, ROWS), BF),
        pl.BlockSpec((256, ROWS), lambda j, s: (j, 0)),
        FF // 256,
        "other_hidden",
    )


def hidden_of(core, got, own, oth):
    w = pl.BlockSpec((2, 16, 64, 256), lambda j, s: (0, 0, 0, j))
    tile = pl.BlockSpec((ROWS, 256), lambda j, s: (0, j))
    return call(
        hidden_kernel,
        core,
        (got, own, oth),
        [pl.BlockSpec((ROWS, D), lambda j, s: (0, 0)), w, w],
        [
            jax.ShapeDtypeStruct((ROWS, FF), BF),
            jax.ShapeDtypeStruct((FF, ROWS), BF),
            jax.ShapeDtypeStruct((ROWS, FF), F32),
            jax.ShapeDtypeStruct((ROWS, FF), F32),
        ],
        [tile, pl.BlockSpec((256, ROWS), lambda j, s: (j, 0)), tile, tile],
        FF // 256,
        "hidden",
    )


def outer_kernel(core, a_t, a2_t, b, b2, out):
    put_rows(out, dot(a_t[...], b[...]) + dot(a2_t[...], b2[...]))


def outer(core, a_t, a2_t, b, b2, place, name):
    m, k = a_t.shape
    left = pl.BlockSpec((m, k), lambda j, s: (0, 0))
    right = pl.BlockSpec((k, 256), lambda j, s: (0, 4 * place(s[0]) + j))
    return call(
        outer_kernel,
        core,
        (a_t, a2_t, b, b2),
        [left, left, right, right],
        jax.ShapeDtypeStruct((2, 16, m // 32, HALF), BF),
        pl.BlockSpec((2, 16, m // 32, 256), lambda j, s: (0, 0, 0, j)),
        4,
        name,
    )


def flip_kernel(core, one, two, one_t, two_t):
    one_t[...] = one[...].T
    two_t[...] = two[...].T


def flip(core, one, two):
    rows = pl.BlockSpec((ROWS, 512), lambda j, s: (0, j))
    return call(
        flip_kernel,
        core,
        (one, two),
        [rows, rows],
        [jax.ShapeDtypeStruct((D, ROWS), BF)] * 2,
        [pl.BlockSpec((512, ROWS), lambda j, s: (j, 0))] * 2,
        4,
        "flip",
        LONG,
    )


def back_kernel(core, dy_own, dy_oth, own, oth, active, steep, d_own, d_oth):
    dhidden = dot_nt(dy_own[...], rows_of(own)) + dot_nt(dy_oth[...], rows_of(oth))
    d_gate = (dhidden * steep[...]).astype(BF)
    d_up = (dhidden * active[...]).astype(BF)
    is0 = core[0] == 0
    d_own[...] = jnp.where(is0, d_gate, d_up)
    d_oth[...] = jnp.where(is0, d_up, d_gate)


def back_of(core, got, own, oth, active, steep):
    w = pl.BlockSpec((2, 4, 32, HALF), lambda j, s: (0, j, 0, 0))
    tile = pl.BlockSpec((ROWS, 256), lambda j, s: (0, j))
    return call(
        back_kernel,
        core,
        (got, got, own, oth, active, steep),
        [
            pl.BlockSpec((ROWS, HALF), lambda j, s: (0, 2 + s[0])),
            pl.BlockSpec((ROWS, HALF), lambda j, s: (0, 3 - s[0])),
            w,
            w,
            tile,
            tile,
        ],
        [jax.ShapeDtypeStruct((ROWS, FF), BF)] * 2,
        [tile, tile],
        FF // 256,
        "back",
    )


def give_kernel(core, hidden, d_own, d_oth, own_out, oth_out, own_in, oth_in, out):
    step = pl.program_id(0)

    @pl.when(step == 0)
    def _():
        out[...] = dot(hidden[...], rows_of(own_out)).astype(BF)

    @pl.when(step == 1)
    def _():
        out[...] = dot(hidden[...], rows_of(oth_out)).astype(BF)

    @pl.when(step >= 2)
    def _():
        dx = dot_nt(d_own[...], rows_of(own_in)) + dot_nt(d_oth[...], rows_of(oth_in))
        out[...] = dx.astype(BF)


def give_of(core, hidden, d_own, d_oth, own_out, oth_out, own_in, oth_in):
    row = pl.BlockSpec((ROWS, FF), lambda j, s: (0, 0))
    w_out = pl.BlockSpec((2, 16, 32, HALF), lambda j, s: (0, 0, 0, 0))
    w_in = pl.BlockSpec((2, 8, 64, HALF), lambda j, s: (0, jnp.maximum(j - 2, 0), 0, 0))
    return call(
        give_kernel,
        core,
        (hidden, d_own, d_oth, own_out, oth_out, own_in, oth_in),
        [row, row, row, w_out, w_out, w_in, w_in],
        jax.ShapeDtypeStruct((ROWS, 2 * D), BF),
        pl.BlockSpec(
            (ROWS, HALF), lambda j, s: (0, jnp.where(j == 0, s[0], jnp.where(j == 1, 1 - s[0], j)))
        ),
        4,
        "give",
        LONG,
    )


def dot(a, b):
    return jnp.dot(a, b, preferred_element_type=F32)


def dot_nt(a, b):
    return lax.dot_general(a, b, (((1,), (1,)), ((), ())), preferred_element_type=F32)


def dot_tn(a, b):
    return lax.dot_general(a, b, (((0,), (0,)), ((), ())), preferred_element_type=F32)


def over_core(v):
    return lax.ppermute(v, "core", [(0, 1), (1, 0)])


def over_y(v):
    return lax.ppermute(v, "yl", [(0, 1), (1, 0)])


def on_device(
    tokens,
    cotangent,
    route_weight,
    slot_expert,
    targets,
    proj_in,
    first_in,
    second_in,
    proj_out,
    first_out,
    second_out,
):
    core = lax.axis_index("core")
    yl = lax.axis_index("yl")
    which = core[None].astype(jnp.int32)

    def after(v, *first):
        return lax.optimization_barrier((v, *first))[0]

    def spread(v):
        got = lax.all_to_all(v.reshape(32, *v.shape[-2:]), SEND_AXES, split_axis=0, concat_axis=0, tiled=True)
        return got.reshape(2, 16, *v.shape[-2:])

    def exchange(v):
        return lax.all_to_all(
            v.reshape(CHIPS, UNITS, 2 * D), CHIP_AXES, split_axis=0, concat_axis=0, tiled=True
        ).reshape(ROWS, 2 * D)

    plan, slot_rows, slot_cols = make_plan(slot_expert)

    rank, keep, spill, kept, spilt = (plan[i, :E] for i in range(5))
    ids = jnp.arange(E, dtype=jnp.int32)
    stored = (ids >> 3) == yl
    place = jnp.where(stored, (((ids >> 2) & 1) ^ core) * 4 + (ids & 3), 8 + rank)
    begin = jnp.where(stored, kept, spilt)
    length = jnp.where(stored, keep, spill)
    order = jnp.arange(HERE, dtype=jnp.int32)
    here = yl * HERE + ((order & 15) * 2 + (order >> 4))[:, None]
    index = jnp.sum(jnp.where((begin <= here) & (here < begin + length), place, 0), axis=1)
    ranked = stored & (rank == jnp.arange(FAR, dtype=jnp.int32)[:, None])
    largest = jnp.sum(jnp.where(ranked, place, 0), axis=1)
    own_rank = lax.dynamic_slice_in_dim(rank, (yl * 2 + core) * 4, 4)
    sel = jnp.concatenate([which, own_rank])

    mine, theirs = prepare(which, proj_in, proj_out)
    theirs = over_core(theirs)
    taken = take_rows(largest, mine, theirs)
    far = over_y(taken)
    send, dest = dispatch(targets, slot_rows, slot_cols, route_weight, after(tokens, taken), cotangent)
    got = exchange(after(send, far))
    for_in = select_rows(index, mine, theirs, far, 0, 64)
    for_out = select_rows(index, mine, theirs, far, 64, 32)
    for_in, for_out, got = lax.optimization_barrier((for_in, for_out, got))
    got2 = over_core(got)
    x_t, x2_t = flip(which, got, got2)
    own_in = spread(for_in)
    oth_in = over_core(own_in)
    own_out = spread(after(for_out, own_in))

    hidden, hidden_t, active, steep = hidden_of(which, got, own_in, oth_in)
    hidden2_t = other_hidden_of(which, got2, own_in, oth_in)
    grad_out = outer(which, hidden_t, hidden2_t, got, got2, lambda c: 2 + c, "outer_out")
    grad_out, own_out = lax.optimization_barrier((grad_out, own_out))
    oth_out = over_core(own_out)
    rows_out = spread(grad_out)

    d_own, d_oth = back_of(which, got, own_out, oth_out, after(active, grad_out), steep)
    d2_own = over_core(d_oth)
    grad_in = outer(which, x_t, x2_t, d_own, d2_own, lambda c: 0, "outer_in")
    rows_in = spread(after(grad_in, rows_out))

    def gather_sums(rows):
        near, near_other, spilled = sum_rows(index, rows.reshape(32, *rows.shape[2:]))
        return near, over_core(near_other), over_y(spilled)

    near0, near1, far_out = gather_sums(rows_out)
    trained_out, mean_out, square_out = adam(
        sel, proj_out, first_out, second_out, near0, near1, far_out, over_core(far_out)
    )
    result = give_of(which, hidden, d_own, d_oth, own_out, oth_out, own_in, oth_in)
    near0, near1, far_in = gather_sums(rows_in)
    back = exchange(after(result, far_in, far_out))
    trained_in, mean_in, square_in = adam(
        sel, proj_in, first_in, second_in, near0, near1, far_in, over_core(far_in)
    )
    mixed, token_grad, mix_grad = combine(dest, route_weight, cotangent, back)
    return (
        mixed,
        token_grad,
        mix_grad,
        trained_in,
        mean_in,
        square_in,
        trained_out,
        mean_out,
        square_out,
    )


def solution(mesh):
    fine = Mesh(mesh.devices.reshape(2, 2, 4, 4, 2), ALL_AXES)
    rows = P(ALL_AXES, None)
    state = P(("yl", "core"), DEV_AXES, None)
    in_specs = (rows, rows, rows, P(), rows) + (state,) * 6
    out_specs = (rows, rows, rows) + (state,) * 6
    return jax.shard_map(on_device, mesh=fine, in_specs=in_specs, out_specs=out_specs, check_vma=False)
```

time: 448 us -> 378 us (0.84)
  waiting for transfers between devices: 277 us -> 149 us
  Pallas kernels: 17.6 us -> 91.5 us
  blocking collectives: 0 us -> 57.2 us
  matrix products: 49.4 us -> 0 us
  other arithmetic: 16.3 us -> 0.9 us
  starting transfers between devices: 72.9 us -> 60.3 us
  local copies, waits for them, and re-layouts: 7.96 us -> 13.4 us
    pallas_call x0 -> x12, Pallas kernels: none -> 73.4 us  [the longest x7 58.4 us: call(): pl.pallas_call(kernel, grid_spec=pltpu.PrefetchScalarGridSpec(num_scalar_...]
    ppermute x4 -> x3, waiting for transfers between devices: 72.3 us -> 13 us  [over_y(): return lax.ppermute(v, 'yl', [(0, 1), (1, 0)])]
    all_to_all x0 -> x1, blocking collectives: none -> 57.2 us  [spread(): lax.all_to_all(v.reshape(32, *v.shape[-2:]), SEND_AXES, split_axis=0, con...]
    all_to_all x6 -> x5, waiting for transfers between devices: 191 us -> 135 us  [the longest x2 74.4 us: exchange(): lax.all_to_all(v.reshape(CHIPS, UNITS, 2 * D), CHIP_AXES, split_axis=0, c...]
    dot_general x12 -> x0, matrix products: 49.4 us -> none  [the longest x4 17.9 us: dot_tn(): lax.dot_general(a, b, (((0,), (0,)), ((), ())), preferred_element_type=F32)]
    all_to_all x6 -> x5, starting transfers between devices: 58.7 us -> 41.3 us  [the longest x3 21.7 us: spread(): lax.all_to_all(v.reshape(32, *v.shape[-2:]), SEND_AXES, split_axis=0, con...]
    ppermute x8 -> x9, waiting for transfers between devices: 13.8 us -> 1.07 us  [over_core(): return lax.ppermute(v, 'core', [(0, 1), (1, 0)])]
    unnamed x43 -> x51, local copies, waits for them, and re-layouts: 5.77 us -> 13.3 us
  transfers between devices with their start and end apart: 18 -> 17, of which waited for: 13 -> 9; matrix products, arithmetic and copies ran while one was open for 10% -> 0% of each run, Pallas kernels for 3% -> 23%
where the time goes in v2:
time: 378 us; the launch traced here: 373 us
  waiting for transfers between devices  149 us (39%)
  Pallas kernels  91.5 us (24%)
  starting transfers between devices  60.3 us (16%)
  blocking collectives  57.2 us (15%)
  local copies, waits for them, and re-layouts  13.4 us (4%)
    all_to_all x2, waiting for transfers between devices, exchange(): lax.all_to_all(v.reshape(CHIPS, UNITS, 2 * D), CHIP_AXES, split_axis=0, c...  74.4 us
    all_to_all x3, waiting for transfers between devices, spread(): lax.all_to_all(v.reshape(32, *v.shape[-2:]), SEND_AXES, split_axis=0, con...  60.7 us
    pallas_call x7, Pallas kernels, call(): pl.pallas_call(kernel, grid_spec=pltpu.PrefetchScalarGridSpec(num_scalar_...  58.4 us
    all_to_all x1, blocking collectives, spread(): lax.all_to_all(v.reshape(32, *v.shape[-2:]), SEND_AXES, split_axis=0, con...  57.2 us
    all_to_all x3, starting transfers between devices, spread(): lax.all_to_all(v.reshape(32, *v.shape[-2:]), SEND_AXES, split_axis=0, con...  21.7 us
    all_to_all x2, starting transfers between devices, exchange(): lax.all_to_all(v.reshape(CHIPS, UNITS, 2 * D), CHIP_AXES, split_axis=0, c...  19.5 us
    unnamed x51, local copies, waits for them, and re-layouts  13.3 us
    ppermute x3, waiting for transfers between devices, over_y(): return lax.ppermute(v, 'yl', [(0, 1), (1, 0)])  13 us
  transfers between devices with their start and end apart: 17, of which 9 were waited for; matrix products, arithmetic and copies ran while one was open for 0% of the time, Pallas kernels for 23%

profile of v2, /device:TPU:1, one launch (start us, length us, event | category | flops | bytes accessed | tf_op | source)
XLA Modules:
  0.0 373.5 jit_solution(708857374580088668)
XLA Ops:
  0.7 1.6 copy-done.2
  2.3 1.2 copy-done.4
  3.5 1.7 prepare.1
  5.1 1.4 collective-permute-start
  6.6 0.1 copy.24.ecol
  6.7 0.4 plan.1
  7.1 0.6 copy-done.7
  7.7 0.6 fusion.6
  8.3 0.1 select_reduce_fusion.1.index
  8.4 0.3 collective-permute-done.theirs
  8.7 1.5 take_rows.1
  10.2 1.4 collective-permute-start.1
  11.6 0.1 copy.25.tcol
  11.8 0.8 copy-done.8
  12.6 1.6 dispatch.1
  14.2 2.0 copy-done
  16.2 13.0 %collective-permute-done.1.far = bf16[4,96,1024]{2,1,0:T(8,128)(2,1)S(1)} collective-permute-done((bf16[4,96,1024]{2,1,0:T(8,128)(2,1)}, bf16[4,96,1024]{2,1,0:T(8,128)(2,1)S(1)}, u32[]{:S(2)}, u32[]{:S(2)}) %collective-permute-start.1) | collective-permute-done | bytes 786464 | tf_op jit(solution)/shard_map/ppermute | solution.py:549
  29.2 11.6 %all-to-all-start = ((bf16[64,8,4096]{2,1,0:T(8,128)(2,1)}), bf16[64,8,4096]{2,1,0:T(8,128)(2,1)}, u32[]{:S(2)}, u32[]{:S(2)}) async-start(bf16[64,8,4096]{2,1,0:T(8,128)(2,1)} %bitcast.21), calls=%async_computation | async-start | bytes 8388608 | tf_op jit(solution)/shard_map/all_to_all | solution.py:577
  40.9 0.1 select_reduce_fusion.index
  40.9 3.5 select_rows.2
  44.5 2.8 select_rows.3
  47.3 42.3 %all-to-all-done = bf16[64,8,4096]{2,1,0:T(8,128)(2,1)} async-done(((bf16[64,8,4096]{2,1,0:T(8,128)(2,1)}), bf16[64,8,4096]{2,1,0:T(8,128)(2,1)}, u32[]{:S(2)}, u32[]{:S(2)}) %all-to-all-start) | async-done | bytes 4194336 | tf_op jit(solution)/shard_map/all_to_all | solution.py:577
  89.6 57.2 %all_to_all.30 = bf16[32,64,1024]{2,1,0:T(8,128)(2,1)} all-to-all(bf16[32,64,1024]{2,1,0:T(8,128)(2,1)} %select_rows.2), channel_id=1, replica_groups=mesh['yl'=2,'core'=2,'x'=4,'z'=4,'yh'=2] {'yh','x','z'}, dimensions={0} | all-to-all | bytes 8388608 | tf_op jit(solution)/shard_map/all_to_all | solution.py:573
  146.8 4.7 %collective-permute-start.2 = (bf16[2,16,64,1024]{3,2,1,0:T(8,128)(2,1)}, bf16[2,16,64,1024]{3,2,1,0:T(8,128)(2,1)}, u32[]{:S(2)}, u32[]{:S(2)}) collective-permute-start(bf16[2,16,64,1024]{3,2,1,0:T(8,128)(2,1)} %bitcast.10.own.own_in), channel_id=1, source_target_pairs={{0,32},{32,0},{1,33},{33,1},{2,34},{34,2},{3,35},{35,3},{4,36},{36... | collective-permute-start | bytes 12582920 | tf_op jit(solution)/shard_map/ppermute | solution.py:545
  151.5 8.4 %all-to-all-start.2 = ((bf16[32,32,1024]{2,1,0:T(8,128)(2,1)}), bf16[32,32,1024]{2,1,0:T(8,128)(2,1)}, u32[]{:S(2)}, u32[]{:S(2)}) async-start(bf16[32,32,1024]{2,1,0:T(8,128)(2,1)} %select_rows.3), calls=%async_computation.2 | async-start | bytes 4194304 | tf_op jit(solution)/shard_map/all_to_all | solution.py:573
  159.9 9.8 %hidden.1 = (bf16[512,1024]{1,0:T(8,128)(2,1)}, bf16[1024,512]{1,0:T(8,128)(2,1)}, f32[512,1024]{1,0:T(8,128)}, f32[512,1024]{1,0:T(8,128)}) custom-call(s32[1]{0:T(128)} %bitcast.5.core, bf16[512,4096]{1,0:T(8,128)(2,1)} %bitcast.9.x.b.dy_own.dy_oth.one, bf16[2,16,64,1024]{3,2,1,0:T(8,128)(2,1)} %bitcast.10.own.own_in, ...), custom_call_target="tpu_custom_call" | custom-call | flops 1 | bytes 1 | tf_op jit(solution)/shard_map/hidden/pallas_call | solution.py:359
  169.7 8.8 %other_hidden.1.a2_t = bf16[1024,512]{1,0:T(8,128)(2,1)} custom-call(s32[1]{0:T(128)} %bitcast.5.core, bf16[512,4096]{1,0:T(8,128)(2,1)} %collective-permute-done.3.x.b2.two, bf16[2,16,64,1024]{3,2,1,0:T(8,128)(2,1)} %bitcast.10.own.own_in, bf16[2,16,64,1024]{3,2,1,0:T(8,128)(2,1)} %collective-permute-done.2.oth.oth_in), custom_call_target="tpu_custom_call" | custom-call | flops 1 | bytes 1 | tf_op jit(solution)/shard_map/other_hidden/pallas_call | solution.py:359
  178.5 6.0 %outer_out.1 = bf16[2,16,32,1024]{3,2,1,0:T(8,128)(2,1)} custom-call(s32[1]{0:T(128)} %bitcast.5.core, bf16[1024,512]{1,0:T(8,128)(2,1)} %get-tuple-element.61.a_t, bf16[1024,512]{1,0:T(8,128)(2,1)} %other_hidden.1.a2_t, bf16[512,4096]{1,0:T(8,128)(2,1)} %bitcast.9.x.b.dy_own.dy_oth.one, bf16[512,4096]{1,0:T(8,128)(2,1)} %collective-permute-done.3.x.b2.two), custom_call_target="tpu_custom_call" | custom-call | flops 1 | bytes 1 | tf_op jit(solution)/shard_map/outer_out/pallas_call | solution.py:359
  184.5 4.4 %all-to-all-done.2 = bf16[32,32,1024]{2,1,0:T(8,128)(2,1)} async-done(((bf16[32,32,1024]{2,1,0:T(8,128)(2,1)}), bf16[32,32,1024]{2,1,0:T(8,128)(2,1)}, u32[]{:S(2)}, u32[]{:S(2)}) %all-to-all-start.2) | async-done | bytes 2097184 | tf_op jit(solution)/shard_map/all_to_all | solution.py:573
  188.9 1.6 collective-permute-start.4
  190.5 6.4 %all-to-all-start.4 = ((bf16[32,32,1024]{2,1,0:T(8,128)(2,1)}), bf16[32,32,1024]{2,1,0:T(8,128)(2,1)S(1)}, u32[]{:S(2)}, u32[]{:S(2)}) async-start(bf16[32,32,1024]{2,1,0:T(8,128)(2,1)} %bitcast.27), calls=%async_computation.4 | async-start | bytes 4194304 | tf_op jit(solution)/shard_map/all_to_all | solution.py:573
  196.9 7.2 %back.1 = (bf16[512,1024]{1,0:T(8,128)(2,1)}, bf16[512,1024]{1,0:T(8,128)(2,1)}) custom-call(s32[1]{0:T(128)} %bitcast.5.core, bf16[512,4096]{1,0:T(8,128)(2,1)} %bitcast.9.x.b.dy_own.dy_oth.one, bf16[512,4096]{1,0:T(8,128)(2,1)} %bitcast.9.x.b.dy_own.dy_oth.one, bf16[2,16,32,1024]{3,2,1,0:T(8,128)(2,1)} %bitcast.11.own.own_out, ...), custom_call_target="tpu_custom_call" | custom-call | flops 1 | bytes 1 | tf_op jit(solution)/shard_map/back/pallas_call | solution.py:359
  204.1 0.3 collective-permute-start.5
  204.4 4.9 %flip.1 = (bf16[2048,512]{1,0:T(8,128)(2,1)}, bf16[2048,512]{1,0:T(8,128)(2,1)}) custom-call(s32[1]{0:T(128)} %bitcast.5.core, bf16[512,4096]{1,0:T(8,128)(2,1)} %bitcast.9.x.b.dy_own.dy_oth.one, bf16[512,4096]{1,0:T(8,128)(2,1)} %collective-permute-done.3.x.b2.two), custom_call_target="tpu_custom_call" | custom-call | flops 10000000000 | bytes 20000000 | tf_op jit(solution)/shard_map/flip/pallas_call | solution.py:359
  209.3 1.0 copy-done.20
  210.3 8.7 %outer_in.1 = bf16[2,16,64,1024]{3,2,1,0:T(8,128)(2,1)} custom-call(s32[1]{0:T(128)} %bitcast.5.core, bf16[2048,512]{1,0:T(8,128)(2,1)} %get-tuple-element.71.a_t, bf16[2048,512]{1,0:T(8,128)(2,1)} %get-tuple-element.72.a2_t, bf16[512,1024]{1,0:T(8,128)(2,1)} %get-tuple-element.69.d_own.b, bf16[512,1024]{1,0:T(8,128)(2,1)} %copy-done.20), custom_call_target="tpu_custom_call" | custom-call | flops 1 | bytes 1 | tf_op jit(solution)/shard_map/outer_in/pallas_call | solution.py:359
  218.9 7.3 %all-to-all-done.4.rows = bf16[32,32,1024]{2,1,0:T(8,128)(2,1)S(1)} async-done(((bf16[32,32,1024]{2,1,0:T(8,128)(2,1)}), bf16[32,32,1024]{2,1,0:T(8,128)(2,1)S(1)}, u32[]{:S(2)}, u32[]{:S(2)}) %all-to-all-start.4) | async-done | bytes 2097184 | tf_op jit(solution)/shard_map/all_to_all | solution.py:573
  226.2 6.9 %all-to-all-start.3 = ((bf16[32,64,1024]{2,1,0:T(8,128)(2,1)}), bf16[32,64,1024]{2,1,0:T(8,128)(2,1)}, u32[]{:S(2)}, u32[]{:S(2)}) async-start(bf16[32,64,1024]{2,1,0:T(8,128)(2,1)} %bitcast.26), calls=%async_computation.3 | async-start | bytes 8388608 | tf_op jit(solution)/shard_map/all_to_all | solution.py:573
  233.1 1.6 sum_rows.3
  234.7 0.7 copy-done.15
  235.4 0.7 copy-done.18
  236.1 0.9 collective-permute-start.7
  237.0 49.0 %all-to-all-done.3.rows = bf16[32,64,1024]{2,1,0:T(8,128)(2,1)} async-done(((bf16[32,64,1024]{2,1,0:T(8,128)(2,1)}), bf16[32,64,1024]{2,1,0:T(8,128)(2,1)}, u32[]{:S(2)}, u32[]{:S(2)}) %all-to-all-start.3) | async-done | bytes 4194336 | tf_op jit(solution)/shard_map/all_to_all | solution.py:573
  286.0 4.4 %sum_rows.2 = (bf16[4,64,1024]{2,1,0:T(8,128)(2,1)S(1)}, bf16[4,64,1024]{2,1,0:T(8,128)(2,1)S(1)}, bf16[4,64,1024]{2,1,0:T(8,128)(2,1)S(1)}) custom-call(s32[32]{0:T(128)S(1)} %select_reduce_fusion.index, bf16[32,64,1024]{2,1,0:T(8,128)(2,1)} %all-to-all-done.3.rows), custom_call_target="tpu_custom_call" | custom-call | flops 10000000000 | bytes 20000000 | tf_op jit(solution)/shard_map/sum_rows/pallas_call | solution.py:299
  290.4 0.8 copy-done.14
  291.2 0.8 copy-done.16
  292.0 5.3 %collective-permute-start.6 = (bf16[4,64,1024]{2,1,0:T(8,128)(2,1)S(1)}, bf16[4,64,1024]{2,1,0:T(8,128)(2,1)S(1)}, u32[]{:S(2)}, u32[]{:S(2)}) collective-permute-start(bf16[4,64,1024]{2,1,0:T(8,128)(2,1)S(1)} %get-tuple-element.73), channel_id=1, source_target_pairs={{0,64},{64,0},{1,65},{65,1},{2,66},{66,2},{3,67},{67,3},{4,68},{68... | collective-permute-start | bytes 1572872 | tf_op jit(solution)/shard_map/ppermute | solution.py:549
  297.3 13.0 %give.1 = bf16[512,4096]{1,0:T(8,128)(2,1)} custom-call(s32[1]{0:T(128)} %bitcast.5.core, bf16[512,1024]{1,0:T(8,128)(2,1)} %get-tuple-element.60.hidden, bf16[512,1024]{1,0:T(8,128)(2,1)} %get-tuple-element.69.d_own.b, bf16[512,1024]{1,0:T(8,128)(2,1)} %get-tuple-element.70.d_oth, bf16[2,16,32,1024]{3,2,1,0:T(8,128)(2,1)} %bitcast.11.own.own_out, ...), custom_call_target="tpu_custom_call" | custom-call | flops 10000000000 | bytes 20000000 | tf_op jit(solution)/shard_map/give/pallas_call | solution.py:359
  310.3 7.9 %all-to-all-start.5 = ((bf16[64,8,4096]{2,1,0:T(8,128)(2,1)}), bf16[64,8,4096]{2,1,0:T(8,128)(2,1)}, u32[]{:S(2)}, u32[]{:S(2)}) async-start(bf16[64,8,4096]{2,1,0:T(8,128)(2,1)} %bitcast.28), calls=%async_computation.5 | async-start | bytes 8388608 | tf_op jit(solution)/shard_map/all_to_all | solution.py:577
  318.2 2.9 collective-permute-start.10
  321.1 0.1 collective-permute-start.11
  321.2 0.1 copy.26.weight
  321.4 0.1 pad_add_fusion.sel
  321.5 0.4 collective-permute-start.8
  321.9 0.1 collective-permute-start.9
  322.0 0.6 collective-permute-done.10.near1
  322.6 0.2 collective-permute-done.11.far1
  322.8 1.2 copy-done.13
  324.0 0.9 copy-done.19
  325.0 4.8 %adam.3 = (f32[4,32,2048]{2,1,0:T(8,128)}, f32[4,32,2048]{2,1,0:T(8,128)}, f32[4,32,2048]{2,1,0:T(8,128)}) custom-call(s32[5]{0:T(128)S(1)} %pad_add_fusion.sel, f32[4,32,2048]{2,1,0:T(8,128)S(1)} %copy-done.5, f32[4,32,2048]{2,1,0:T(8,128)S(1)} %copy-done.12, f32[4,32,2048]{2,1,0:T(8,128)S(1)} %copy-done.13, bf16[4,32,1024]{2,1,0:T(8,128)(2,1)S(1)} %copy-done.19, ...), custom_call_target="tpu_custom_call" | custom-call | flops 10000000000 | bytes 20000000 | tf_op jit(solution)/shard_map/adam/pallas_call | solution.py:332
  329.8 6.7 %adam.2 = (f32[4,64,2048]{2,1,0:T(8,128)}, f32[4,64,2048]{2,1,0:T(8,128)}, f32[4,64,2048]{2,1,0:T(8,128)}) custom-call(s32[5]{0:T(128)S(1)} %pad_add_fusion.sel, f32[4,64,2048]{2,1,0:T(8,128)S(1)} %copy-done.3, f32[4,64,2048]{2,1,0:T(8,128)} %moment.2, f32[4,64,2048]{2,1,0:T(8,128)} %square.2, bf16[4,64,1024]{2,1,0:T(8,128)(2,1)S(1)} %copy-done.17, ...), custom_call_target="tpu_custom_call" | custom-call | flops 10000000000 | bytes 20000000 | tf_op jit(solution)/shard_map/adam/pallas_call | solution.py:332
  336.5 32.1 %all-to-all-done.5 = bf16[64,8,4096]{2,1,0:T(8,128)(2,1)} async-done(((bf16[64,8,4096]{2,1,0:T(8,128)(2,1)}), bf16[64,8,4096]{2,1,0:T(8,128)(2,1)}, u32[]{:S(2)}, u32[]{:S(2)}) %all-to-all-start.5) | async-done | bytes 4194336 | tf_op jit(solution)/shard_map/all_to_all | solution.py:577
  368.6 4.2 %combine.1 = (bf16[128,2048]{1,0:T(8,128)(2,1)}, bf16[128,2048]{1,0:T(8,128)(2,1)}, f32[128,2]{1,0:T(8,128)S(1)}) custom-call(f32[128,2]{1,0:T(8,128)S(1)} %get-tuple-element.55.dest, f32[128,2]{1,0:T(8,128)S(1)} %copy.26.weight, bf16[128,2048]{1,0:T(8,128)(2,1)S(1)} %copy-done.1, bf16[512,4096]{1,0:T(8,128)(2,1)} %bitcast.15.back), custom_call_target="tpu_custom_call" | custom-call | tf_op jit(solution)/shard_map/combine/pallas_call | solution.py:186
  372.8 0.6 copy.27
  (49 shorter events, 0.2 us)
Async XLA Ops:
  0.6 5.9 %copy-start.11 = (s32[128]{0:T(128)S(1)}, s32[128]{0:T(128)}, u32[]{:S(2)}) copy-start(s32[128]{0:T(128)} %param.14) | copy-start | bytes 1540
  0.7 1.6 copy-start.2
  2.3 1.2 copy-start.4
  3.5 8.1 %copy-start.9 = (s32[128,2]{0,1:T(2,128)S(1)}, s32[128,2]{0,1:T(2,128)}, u32[]{:S(2)}) copy-start(s32[128,2]{0,1:T(2,128)} %param.15) | copy-start | bytes 3076
  3.5 8.2 %copy-start.1 = (bf16[128,2048]{1,0:T(8,128)(2,1)S(1)}, bf16[128,2048]{1,0:T(8,128)(2,1)}, u32[]{:S(2)}) copy-start(bf16[128,2048]{1,0:T(8,128)(2,1)} %cot.3) | copy-start | bytes 1572868
  3.5 8.2 %copy-start.6 = (bf16[128,2048]{1,0:T(8,128)(2,1)S(1)}, bf16[128,2048]{1,0:T(8,128)(2,1)}, u32[]{:S(2)}) copy-start(bf16[128,2048]{1,0:T(8,128)(2,1)} %tok) | copy-start | bytes 1572868
  3.5 8.3 %copy-start.10 = (f32[128,2]{0,1:T(2,128)S(1)}, f32[128,2]{0,1:T(2,128)}, u32[]{:S(2)}) copy-start(f32[128,2]{0,1:T(2,128)} %param.13) | copy-start | bytes 3076
  5.1 3.6 collective-permute-start
  7.1 0.6 copy-start.7
  10.2 19.0 %collective-permute-start.1 = (bf16[4,96,1024]{2,1,0:T(8,128)(2,1)}, bf16[4,96,1024]{2,1,0:T(8,128)(2,1)S(1)}, u32[]{:S(2)}, u32[]{:S(2)}) collective-permute-start(bf16[4,96,1024]{2,1,0:T(8,128)(2,1)} %take_rows.1), channel_id=1, source_target_pairs={{0,64},{64,0},{1,65},{65,1},{2,66},{66,2},{3,67},{67,3},{4,68},{68... | collective-permute-start | bytes 2359304 | tf_op jit(solution)/shard_map/ppermute | solution.py:549
  11.7 0.8 copy-start.8
  14.2 2.0 copy-start
  29.2 11.6 %copy-start.21 = (s32[16]{0:T(128)S(1)}, s32[16]{0:T(128)}, u32[]{:S(2)}) copy-start(s32[16]{0:T(128)} %get-tuple-element.111) | copy-start | bytes 196
  29.2 11.7 %copy-start.22 = (s32[1,16]{1,0:T(1,128)S(1)}, s32[1,16]{1,0:T(1,128)}, u32[]{:S(2)}) copy-start(s32[1,16]{1,0:T(1,128)} %get-tuple-element.112) | copy-start | bytes 196
  29.2 60.4 %all-to-all-start = ((bf16[64,8,4096]{2,1,0:T(8,128)(2,1)}), bf16[64,8,4096]{2,1,0:T(8,128)(2,1)}, u32[]{:S(2)}, u32[]{:S(2)}) async-start(bf16[64,8,4096]{2,1,0:T(8,128)(2,1)} %bitcast.21), calls=%async_computation | async-start | bytes 8388608 | tf_op jit(solution)/shard_map/all_to_all | solution.py:577
  146.8 13.2 %collective-permute-start.2 = (bf16[2,16,64,1024]{3,2,1,0:T(8,128)(2,1)}, bf16[2,16,64,1024]{3,2,1,0:T(8,128)(2,1)}, u32[]{:S(2)}, u32[]{:S(2)}) collective-permute-start(bf16[2,16,64,1024]{3,2,1,0:T(8,128)(2,1)} %bitcast.10.own.own_in), channel_id=1, source_target_pairs={{0,32},{32,0},{1,33},{33,1},{2,34},{34,2},{3,35},{35,3},{4,36},{36... | collective-permute-start | bytes 12582920 | tf_op jit(solution)/shard_map/ppermute | solution.py:545
  151.5 18.3 %collective-permute-start.3 = (bf16[512,4096]{1,0:T(8,128)(2,1)}, bf16[512,4096]{1,0:T(8,128)(2,1)}, u32[]{:S(2)}, u32[]{:S(2)}) collective-permute-start(bf16[512,4096]{1,0:T(8,128)(2,1)} %bitcast.9.x.b.dy_own.dy_oth.one), channel_id=1, source_target_pairs={{0,32},{32,0},{1,33},{33,1},{2,34},{34,2},{3,35},{35,3},{4,36},{36... | collective-permute-start | bytes 12582920 | tf_op jit(solution)/shard_map/ppermute | solution.py:545
  151.5 37.5 %all-to-all-start.2 = ((bf16[32,32,1024]{2,1,0:T(8,128)(2,1)}), bf16[32,32,1024]{2,1,0:T(8,128)(2,1)}, u32[]{:S(2)}, u32[]{:S(2)}) async-start(bf16[32,32,1024]{2,1,0:T(8,128)(2,1)} %select_rows.3), calls=%async_computation.2 | async-start | bytes 4194304 | tf_op jit(solution)/shard_map/all_to_all | solution.py:573
  188.9 7.9 %collective-permute-start.4 = (bf16[2,16,32,1024]{3,2,1,0:T(8,128)(2,1)}, bf16[2,16,32,1024]{3,2,1,0:T(8,128)(2,1)}, u32[]{:S(2)}, u32[]{:S(2)}) collective-permute-start(bf16[2,16,32,1024]{3,2,1,0:T(8,128)(2,1)} %bitcast.11.own.own_out), channel_id=1, source_target_pairs={{0,32},{32,0},{1,33},{33,1},{2,34},{34,2},{3,35},{35,3},{4,36},{36... | collective-permute-start | bytes 6291464 | tf_op jit(solution)/shard_map/ppermute | solution.py:545
  190.5 35.7 %all-to-all-start.4 = ((bf16[32,32,1024]{2,1,0:T(8,128)(2,1)}), bf16[32,32,1024]{2,1,0:T(8,128)(2,1)S(1)}, u32[]{:S(2)}, u32[]{:S(2)}) async-start(bf16[32,32,1024]{2,1,0:T(8,128)(2,1)} %bitcast.27), calls=%async_computation.4 | async-start | bytes 4194304 | tf_op jit(solution)/shard_map/all_to_all | solution.py:573
  204.1 5.2 %collective-permute-start.5 = (bf16[512,1024]{1,0:T(8,128)(2,1)}, bf16[512,1024]{1,0:T(8,128)(2,1)S(1)}, u32[]{:S(2)}, u32[]{:S(2)}) collective-permute-start(bf16[512,1024]{1,0:T(8,128)(2,1)} %get-tuple-element.70.d_oth), channel_id=1, source_target_pairs={{0,32},{32,0},{1,33},{33,1},{2,34},{34,2},{3,35},{35,3},{4,36},{36... | collective-permute-start | bytes 3145736 | tf_op jit(solution)/shard_map/ppermute | solution.py:545
  209.3 1.0 copy-start.20
  226.2 59.8 %all-to-all-start.3 = ((bf16[32,64,1024]{2,1,0:T(8,128)(2,1)}), bf16[32,64,1024]{2,1,0:T(8,128)(2,1)}, u32[]{:S(2)}, u32[]{:S(2)}) async-start(bf16[32,64,1024]{2,1,0:T(8,128)(2,1)} %bitcast.26), calls=%async_computation.3 | async-start | bytes 8388608 | tf_op jit(solution)/shard_map/all_to_all | solution.py:573
  234.7 0.7 copy-start.15
  235.4 0.7 copy-start.18
  236.1 74.2 %collective-permute-start.7 = (bf16[4,32,1024]{2,1,0:T(8,128)(2,1)S(1)}, bf16[4,32,1024]{2,1,0:T(8,128)(2,1)S(1)}, u32[]{:S(2)}, u32[]{:S(2)}) collective-permute-start(bf16[4,32,1024]{2,1,0:T(8,128)(2,1)S(1)} %get-tuple-element.74), channel_id=1, source_target_pairs={{0,64},{64,0},{1,65},{65,1},{2,66},{66,2},{3,67},{67,3},{4,68},{68... | collective-permute-start | bytes 786440 | tf_op jit(solution)/shard_map/ppermute | solution.py:549
  290.4 0.8 copy-start.14
  291.2 0.8 copy-start.16
  292.0 18.3 %collective-permute-start.6 = (bf16[4,64,1024]{2,1,0:T(8,128)(2,1)S(1)}, bf16[4,64,1024]{2,1,0:T(8,128)(2,1)S(1)}, u32[]{:S(2)}, u32[]{:S(2)}) collective-permute-start(bf16[4,64,1024]{2,1,0:T(8,128)(2,1)S(1)} %get-tuple-element.73), channel_id=1, source_target_pairs={{0,64},{64,0},{1,65},{65,1},{2,66},{66,2},{3,67},{67,3},{4,68},{68... | collective-permute-start | bytes 1572872 | tf_op jit(solution)/shard_map/ppermute | solution.py:549
  310.3 11.1 %copy-start.23 = (s32[1,16]{1,0:T(1,128)S(1)}, s32[1,16]{1,0:T(1,128)}, u32[]{:S(2)}) copy-start(s32[1,16]{1,0:T(1,128)} %get-tuple-element.109) | copy-start | bytes 196
  310.3 12.5 %copy-start.5 = (f32[4,32,2048]{2,1,0:T(8,128)S(1)}, f32[4,32,2048]{2,1,0:T(8,128)}, u32[]{:S(2)}) copy-start(f32[4,32,2048]{2,1,0:T(8,128)} %weight.4) | copy-start | bytes 3145732
  310.3 12.5 %copy-start.12 = (f32[4,32,2048]{2,1,0:T(8,128)S(1)}, f32[4,32,2048]{2,1,0:T(8,128)}, u32[]{:S(2)}) copy-start(f32[4,32,2048]{2,1,0:T(8,128)} %moment.3) | copy-start | bytes 3145732
  310.3 58.3 %all-to-all-start.5 = ((bf16[64,8,4096]{2,1,0:T(8,128)(2,1)}), bf16[64,8,4096]{2,1,0:T(8,128)(2,1)}, u32[]{:S(2)}, u32[]{:S(2)}) async-start(bf16[64,8,4096]{2,1,0:T(8,128)(2,1)} %bitcast.28), calls=%async_computation.5 | async-start | bytes 8388608 | tf_op jit(solution)/shard_map/all_to_all | solution.py:577
  318.2 4.4 %collective-permute-start.10 = (bf16[4,32,1024]{2,1,0:T(8,128)(2,1)}, bf16[4,32,1024]{2,1,0:T(8,128)(2,1)}, u32[]{:S(2)}, u32[]{:S(2)}) collective-permute-start(bf16[4,32,1024]{2,1,0:T(8,128)(2,1)} %copy-done.15), channel_id=1, source_target_pairs={{0,32},{32,0},{1,33},{33,1},{2,34},{34,2},{3,35},{35,3},{4,36},{36... | collective-permute-start | bytes 786440 | tf_op jit(solution)/shard_map/ppermute | solution.py:545
  321.1 1.7 collective-permute-start.11
  321.5 8.3 %collective-permute-start.8 = (bf16[4,64,1024]{2,1,0:T(8,128)(2,1)}, bf16[4,64,1024]{2,1,0:T(8,128)(2,1)S(1)}, u32[]{:S(2)}, u32[]{:S(2)}) collective-permute-start(bf16[4,64,1024]{2,1,0:T(8,128)(2,1)} %copy-done.14), channel_id=1, source_target_pairs={{0,32},{32,0},{1,33},{33,1},{2,34},{34,2},{3,35},{35,3},{4,36},{36... | collective-permute-start | bytes 1572872 | tf_op jit(solution)/shard_map/ppermute | solution.py:545
  321.9 7.9 %collective-permute-start.9 = (bf16[4,64,1024]{2,1,0:T(8,128)(2,1)S(1)}, bf16[4,64,1024]{2,1,0:T(8,128)(2,1)S(1)}, u32[]{:S(2)}, u32[]{:S(2)}) collective-permute-start(bf16[4,64,1024]{2,1,0:T(8,128)(2,1)S(1)} %collective-permute-done.6.far0), channel_id=1, source_target_pairs={{0,32},{32,0},{1,33},{33,1},{2,34},{34,2},{3,35},{35,3},{4,36},{36... | collective-permute-start | bytes 1572872 | tf_op jit(solution)/shard_map/ppermute | solution.py:545
  322.8 1.2 copy-start.13
  324.0 0.9 copy-start.19
  325.0 4.8 %copy-start.3 = (f32[4,64,2048]{2,1,0:T(8,128)S(1)}, f32[4,64,2048]{2,1,0:T(8,128)}, u32[]{:S(2)}) copy-start(f32[4,64,2048]{2,1,0:T(8,128)} %weight.3) | copy-start | bytes 6291460
  325.0 4.8 %copy-start.17 = (bf16[4,64,1024]{2,1,0:T(8,128)(2,1)S(1)}, bf16[4,64,1024]{2,1,0:T(8,128)(2,1)}, u32[]{:S(2)}) copy-start(bf16[4,64,1024]{2,1,0:T(8,128)(2,1)} %copy-done.16) | copy-start | bytes 1572868

commit v3 on v2

--- a/solution.py
+++ b/solution.py
@@ -157,34 +157,41 @@
     )(targets, targets.T, slot_rows, slot_cols, route_weight.T, tokens, cotangent)
 
 
-def combine_kernel(dest, weight, cot, back, mixed, grad, mix):
+def combine_kernel(dest, weight, cot, out, dx, mixed, grad, mix):
+    step = pl.program_id(0)
     place = lax.broadcasted_iota(jnp.int32, (128, ROWS), 1).astype(F32)
     first, second = place == dest[:, 0:1], place == dest[:, 1:2]
-    one, zero = jnp.float32(1.0), jnp.float32(0.0)
-    pick0 = jnp.where(first, one, zero).astype(BF)
-    pick1 = jnp.where(second, one, zero).astype(BF)
-    both = jnp.where(first | second, one, zero).astype(BF)
-    w0, w1 = weight[:, 0:1], weight[:, 1:2]
-    mix0 = jnp.zeros((128, 1), F32)
-    mix1 = jnp.zeros((128, 1), F32)
+    pick0 = jnp.where(first, 1.0, 0.0).astype(BF)
+    pick1 = jnp.where(second, 1.0, 0.0).astype(BF)
+    both = jnp.where(first | second, 1.0, 0.0).astype(BF)
+    out0, out1 = dot(pick0, out[...]), dot(pick1, out[...])
+    here = cot[...].astype(F32)
+    mixed[...] = (weight[:, 0:1] * out0 + weight[:, 1:2] * out1).astype(BF)
+    grad[...] = dot(both, dx[...]).astype(BF)
+
+    @pl.when(step == 0)
+    def _():
+        mix[...] = jnp.zeros_like(mix)
+
+    mix[:, 0:1] += jnp.sum(here * out0, axis=1, keepdims=True)
+    mix[:, 1:2] += jnp.sum(here * out1, axis=1, keepdims=True)
+
+
+def combine(dest, route_weight, cotangent, back):
     width = 512
-    for c in range(D // width):
-        cols = slice(c * width, (c + 1) * width)
-        out0 = jnp.dot(pick0, back[:, cols], preferred_element_type=F32)
-        out1 = jnp.dot(pick1, back[:, cols], preferred_element_type=F32)
-        here = cot[:, cols].astype(F32)
-        mixed[:, cols] = (w0 * out0 + w1 * out1).astype(BF)
-        mix0 += jnp.sum(here * out0, axis=1, keepdims=True)
-        mix1 += jnp.sum(here * out1, axis=1, keepdims=True)
-        dcols = slice(D + c * width, D + (c + 1) * width)
-        grad[:, cols] = jnp.dot(both, back[:, dcols], preferred_element_type=F32).astype(BF)
-    mix[:, 0:1] = mix0
-    mix[:, 1:2] = mix1
-
-
-def combine(dest, route_weight, cotangent, back):
+    whole = pl.BlockSpec((128, 2), lambda j: (0, 0))
+    tile = pl.BlockSpec((128, width), lambda j: (0, j))
     return pl.pallas_call(
         combine_kernel,
+        grid=(D // width,),
+        in_specs=[
+            whole,
+            whole,
+            tile,
+            pl.BlockSpec((ROWS, width), lambda j: (0, j)),
+            pl.BlockSpec((ROWS, width), lambda j: (0, D // width + j)),
+        ],
+        out_specs=[tile, tile, whole],
         out_shape=(
             jax.ShapeDtypeStruct((128, D), BF),
             jax.ShapeDtypeStruct((128, D), BF),
@@ -192,7 +199,7 @@
         ),
         compiler_params=params(),
         name="combine",
-    )(dest, route_weight, cotangent, back)
+    )(dest, route_weight, cotangent, back, back)
 
 
 def prepare_kernel(core, w_in, w_out, mine, theirs):
@@ -234,125 +241,136 @@
 
 
 def copy_one(e, parts, out, j):
-    for k, part in enumerate(parts):
-
-        @pl.when((e >= 4 * k) & (e < 4 * k + 4))
-        def _(k=k, part=part):
-            out[j] = part[jnp.clip(e - 4 * k, 0, 3)]
-
-
-def take_kernel(index, mine, theirs, out):
+    start = 0
+    for part in parts:
+        n = part.shape[0]
+
+        @pl.when((e >= start) & (e < start + n))
+        def _(start=start, n=n, part=part):
+            out[j] = part[jnp.clip(e - start, 0, n - 1)]
+
+        start += n
+
+
+def take_kernel(index, mine, theirs, pair, cross):
     for j in range(FAR):
-        copy_one(index[j], (mine, theirs), out, j)
+        copy_one(index[j], (mine, theirs), (pair, cross)[j // 2], j % 2)
 
 
 def take_rows(index, mine, theirs):
     n, r, c = mine.shape
     whole = pl.BlockSpec((n, r, c), lambda i, s: (0, 0, 0))
+    two = pl.BlockSpec((2, r, c), lambda i, s: (0, 0, 0))
     return pl.pallas_call(
         take_kernel,
         grid_spec=pltpu.PrefetchScalarGridSpec(
-            num_scalar_prefetch=1, grid=(1,), in_specs=[whole] * 2, out_specs=whole
-        ),
-        out_shape=jax.ShapeDtypeStruct((FAR, r, c), BF),
+            num_scalar_prefetch=1, grid=(1,), in_specs=[whole] * 2, out_specs=[two] * 2
+        ),
+        out_shape=[jax.ShapeDtypeStruct((2, r, c), BF)] * 2,
         compiler_params=params(),
         name="take_rows",
     )(index, mine, theirs)
 
 
-def select_kernel(index, mine, theirs, far, out):
+def select_kernel(index, *refs):
     step = pl.program_id(0)
     for j in range(8):
-        copy_one(index[step * 8 + j], (mine, theirs, far), out, j)
-
-
-def select_rows(index, mine, theirs, far, start, r):
-    c = mine.shape[2]
-    part = pl.BlockSpec((4, r, c), lambda i, s: (0, start // r, 0))
+        copy_one(index[step * 8 + j], refs[:-1], refs[-1], j)
+
+
+def select_rows(index, parts, start, r):
+    c = parts[0].shape[2]
     return pl.pallas_call(
         select_kernel,
         grid_spec=pltpu.PrefetchScalarGridSpec(
             num_scalar_prefetch=1,
             grid=(4,),
-            in_specs=[part] * 3,
+            in_specs=[pl.BlockSpec((p.shape[0], r, c), lambda i, s: (0, start // r, 0)) for p in parts],
             out_specs=pl.BlockSpec((8, r, c), lambda i, s: (i, 0, 0)),
         ),
         out_shape=jax.ShapeDtypeStruct((32, r, c), BF),
         compiler_params=params(),
         name="select_rows",
-    )(index, mine, theirs, far)
-
-
-def sum_kernel(index, rows, mine, theirs, far, total):
+    )(index, *parts)
+
+
+def sum_kernel(index, rows, mine, theirs, pair, cross, total):
     total[...] = jnp.zeros_like(total)
     for d in range(32):
         e = index[d]
         total[e] += rows[d].astype(F32)
     mine[...] = total[:4].astype(BF)
     theirs[...] = total[4:8].astype(BF)
-    far[...] = total[8:].astype(BF)
+    pair[...] = total[8:10].astype(BF)
+    cross[...] = total[10:].astype(BF)
 
 
 def sum_rows(index, rows):
     n, r, c = rows.shape
     step = 16
+    counts = (4, 4, 2, 2)
     return pl.pallas_call(
         sum_kernel,
         grid_spec=pltpu.PrefetchScalarGridSpec(
             num_scalar_prefetch=1,
             grid=(r // step,),
             in_specs=[pl.BlockSpec((n, step, c), lambda i, s: (0, i, 0))],
-            out_specs=[pl.BlockSpec((4, step, c), lambda i, s: (0, i, 0))] * 3,
+            out_specs=[pl.BlockSpec((k, step, c), lambda i, s: (0, i, 0)) for k in counts],
             scratch_shapes=[pltpu.VMEM((8 + FAR, step, c), F32)],
         ),
-        out_shape=[jax.ShapeDtypeStruct((4, r, c), BF)] * 3,
+        out_shape=[jax.ShapeDtypeStruct((k, r, c), BF) for k in counts],
         compiler_params=params(),
         cost_estimate=LONG,
         name="sum_rows",
     )(index, rows)
 
 
-def adam_kernel(sel, weight, moment, square, near0, near1, far0, far1, new_w, new_m, new_s):
-    has_far = (sel[1 + pl.program_id(0)] < FAR).astype(F32)
+def adam_kernel(sel, weight, moment, square, *refs):
+    own, other = refs[:3], refs[3:6]
+    new_w, new_m, new_s = refs[6:]
+    rank = sel[1 + pl.program_id(0)]
     for h in range(2):
         cols = slice(h * HALF, (h + 1) * HALF)
-        own = sel[0] == h
-        near = jnp.where(own, near0[...], near1[...]).astype(F32)
-        far = jnp.where(own, far0[...], far1[...]).astype(F32)
+        mine = sel[0] == h
+        near, pair, cross = (jnp.where(mine, a[...], b[...]).astype(F32) for a, b in zip(own, other))
+        grad = near + jnp.where(rank < 2, pair, jnp.where(rank < FAR, cross, 0.0))
         new_w[:, :, cols], new_m[:, :, cols], new_s[:, :, cols] = adam_step(
-            weight[:, :, cols], moment[:, :, cols], square[:, :, cols], near + has_far * far
+            weight[:, :, cols], moment[:, :, cols], square[:, :, cols], grad
         )
 
 
-def adam(sel, weight, moment, square, near0, near1, far0, far1):
+def adam(sel, weight, moment, square, own, other):
     n, r, c = weight.shape
     state = pl.BlockSpec((1, r, c), lambda i, s: (i, 0, 0))
-    near = pl.BlockSpec((1, r, HALF), lambda i, s: (i, 0, 0))
-    far = pl.BlockSpec((1, r, HALF), lambda i, s: (jnp.minimum(s[1 + i], FAR - 1), 0, 0))
+    sums = [
+        pl.BlockSpec((1, r, HALF), lambda i, s: (i, 0, 0)),
+        pl.BlockSpec((1, r, HALF), lambda i, s: (jnp.clip(s[1 + i], 0, 1), 0, 0)),
+        pl.BlockSpec((1, r, HALF), lambda i, s: (jnp.clip(s[1 + i] - 2, 0, 1), 0, 0)),
+    ]
     return pl.pallas_call(
         adam_kernel,
         grid_spec=pltpu.PrefetchScalarGridSpec(
             num_scalar_prefetch=1,
             grid=(n,),
-            in_specs=[state] * 3 + [near] * 2 + [far] * 2,
+            in_specs=[state] * 3 + sums + sums,
             out_specs=[state] * 3,
         ),
         out_shape=[jax.ShapeDtypeStruct((n, r, c), F32)] * 3,
         compiler_params=params(),
         cost_estimate=LONG,
         name="adam",
-    )(sel, weight, moment, square, near0, near1, far0, far1)
-
-
-def rows_of(w):
-    return jnp.concatenate([w[y, i] for i in range(w.shape[1]) for y in range(2)], axis=0)
-
-
-def put_rows(out, v):
+    )(sel, weight, moment, square, *own, *other)
+
+
+def rows_of(w, flip):
+    return jnp.concatenate([w[y ^ flip, i] for i in range(w.shape[1]) for y in range(2)], axis=0)
+
+
+def put_rows(out, v, flip):
     r = out.shape[2]
     for i in range(out.shape[1]):
         for y in range(2):
-            out[y, i] = v[(2 * i + y) * r : (2 * i + y + 1) * r].astype(BF)
+            out[y ^ flip, i] = v[(2 * i + y) * r : (2 * i + y + 1) * r].astype(BF)
 
 
 def call(kernel, core, args, in_specs, out_shape, out_specs, steps, name, cost=SHORT):
@@ -369,7 +387,7 @@
 
 
 def hidden_kernel(core, x, own, oth, hidden, hidden_t, active, steep):
-    one, two = dot(x[...], rows_of(own)), dot(x[...], rows_of(oth))
+    one, two = dot(x[...], rows_of(own, core[1])), dot(x[...], rows_of(oth, core[1]))
     is0 = core[0] == 0
     gating, upward = jnp.where(is0, one, two), jnp.where(is0, two, one)
     logistic = jax.nn.sigmoid(gating)
@@ -382,7 +400,7 @@
 
 
 def other_hidden_kernel(core, x, own, oth, hidden_t):
-    one, two = dot(x[...], rows_of(own)), dot(x[...], rows_of(oth))
+    one, two = dot(x[...], rows_of(own, core[1])), dot(x[...], rows_of(oth, core[1]))
     is0 = core[0] == 0
     gating, upward = jnp.where(is0, one, two), jnp.where(is0, two, one)
     hidden_t[...] = (gating * jax.nn.sigmoid(gating) * upward).T.astype(BF)
@@ -423,7 +441,7 @@
 
 
 def outer_kernel(core, a_t, a2_t, b, b2, out):
-    put_rows(out, dot(a_t[...], b[...]) + dot(a2_t[...], b2[...]))
+    put_rows(out, dot(a_t[...], b[...]) + dot(a2_t[...], b2[...]), core[1])
 
 
 def outer(core, a_t, a2_t, b, b2, place, name):
@@ -463,7 +481,7 @@
 
 
 def back_kernel(core, dy_own, dy_oth, own, oth, active, steep, d_own, d_oth):
-    dhidden = dot_nt(dy_own[...], rows_of(own)) + dot_nt(dy_oth[...], rows_of(oth))
+    dhidden = dot_nt(dy_own[...], rows_of(own, core[1])) + dot_nt(dy_oth[...], rows_of(oth, core[1]))
     d_gate = (dhidden * steep[...]).astype(BF)
     d_up = (dhidden * active[...]).astype(BF)
     is0 = core[0] == 0
@@ -498,15 +516,15 @@
 
     @pl.when(step == 0)
     def _():
-        out[...] = dot(hidden[...], rows_of(own_out)).astype(BF)
+        out[...] = dot(hidden[...], rows_of(own_out, core[1])).astype(BF)
 
     @pl.when(step == 1)
     def _():
-        out[...] = dot(hidden[...], rows_of(oth_out)).astype(BF)
+        out[...] = dot(hidden[...], rows_of(oth_out, core[1])).astype(BF)
 
     @pl.when(step >= 2)
     def _():
-        dx = dot_nt(d_own[...], rows_of(own_in)) + dot_nt(d_oth[...], rows_of(oth_in))
+        dx = dot_nt(d_own[...], rows_of(own_in, core[1])) + dot_nt(d_oth[...], rows_of(oth_in, core[1]))
         out[...] = dx.astype(BF)
 
 
@@ -525,7 +543,6 @@
         ),
         4,
         "give",
-        LONG,
     )
 
 
@@ -545,8 +562,12 @@
     return lax.ppermute(v, "core", [(0, 1), (1, 0)])
 
 
-def over_y(v):
+def over_pair(v):
     return lax.ppermute(v, "yl", [(0, 1), (1, 0)])
+
+
+def over_cross(v):
+    return lax.ppermute(v, ("yl", "yh"), [(0, 3), (3, 0), (1, 2), (2, 1)])
 
 
 def on_device(
@@ -597,13 +618,16 @@
     mine, theirs = prepare(which, proj_in, proj_out)
     theirs = over_core(theirs)
     taken = take_rows(largest, mine, theirs)
-    far = over_y(taken)
-    send, dest = dispatch(targets, slot_rows, slot_cols, route_weight, after(tokens, taken), cotangent)
-    got = exchange(after(send, far))
-    for_in = select_rows(index, mine, theirs, far, 0, 64)
-    for_out = select_rows(index, mine, theirs, far, 64, 32)
+    far = (over_pair(taken[0]), over_cross(taken[1]))
+    send, dest = dispatch(targets, slot_rows, slot_cols, route_weight, after(tokens, *taken), cotangent)
+    got = exchange(after(send, *far))
+    for_in = select_rows(index, (mine, theirs, *far), 0, 64)
+    for_out = select_rows(index, (mine, theirs, *far), 64, 32)
     for_in, for_out, got = lax.optimization_barrier((for_in, for_out, got))
     got2 = over_core(got)
+    chip = lax.axis_index("yh") * 16 + lax.axis_index("x") * 4 + lax.axis_index("z")
+    crossed = (lax.dynamic_index_in_dim(index, chip, keepdims=False) >= 10).astype(jnp.int32)
+    which = jnp.stack([which[0], crossed])
     x_t, x2_t = flip(which, got, got2)
     own_in = spread(for_in)
     oth_in = over_core(own_in)
@@ -622,19 +646,17 @@
     rows_in = spread(after(grad_in, rows_out))
 
     def gather_sums(rows):
-        near, near_other, spilled = sum_rows(index, rows.reshape(32, *rows.shape[2:]))
-        return near, over_core(near_other), over_y(spilled)
-
-    near0, near1, far_out = gather_sums(rows_out)
-    trained_out, mean_out, square_out = adam(
-        sel, proj_out, first_out, second_out, near0, near1, far_out, over_core(far_out)
-    )
+        near, near_other, pair, cross = sum_rows(index, rows.reshape(32, *rows.shape[2:]))
+        pair, cross = over_pair(pair), over_cross(cross)
+        own, other = (near, pair, cross), (over_core(near_other), over_core(pair), over_core(cross))
+        return own, other
+
     result = give_of(which, hidden, d_own, d_oth, own_out, oth_out, own_in, oth_in)
-    near0, near1, far_in = gather_sums(rows_in)
-    back = exchange(after(result, far_in, far_out))
-    trained_in, mean_in, square_in = adam(
-        sel, proj_in, first_in, second_in, near0, near1, far_in, over_core(far_in)
-    )
+    own, other = gather_sums(after(rows_out, result))
+    trained_out, mean_out, square_out = adam(sel, proj_out, first_out, second_out, own, other)
+    own2, other2 = gather_sums(after(rows_in, result))
+    back = exchange(after(result, *own2[1:]))
+    trained_in, mean_in, square_in = adam(sel, proj_in, first_in, second_in, own2, other2)
     mixed, token_grad, mix_grad = combine(dest, route_weight, cotangent, back)
     return (
         mixed,

time: 378 us -> 391 us (1.034)
  waiting for transfers between devices: 149 us -> 135 us
  local copies, waits for them, and re-layouts: 13.4 us -> 21.4 us
  starting transfers between devices: 60.3 us -> 67.5 us
  Pallas kernels: 91.5 us -> 97.5 us
    ppermute x3 -> x6, waiting for transfers between devices: 13 us -> 48.5 us  [the longest x3 43.5 us: over_pair(): return lax.ppermute(v, 'yl', [(0, 1), (1, 0)])]
    all_to_all x2, waiting for transfers between devices: 74.4 us -> 42.8 us  [exchange(): lax.all_to_all(v.reshape(CHIPS, UNITS, 2 * D), CHIP_AXES, split_axis=0, c...]
    all_to_all x3, waiting for transfers between devices: 60.7 us -> 43.2 us  [spread(): lax.all_to_all(v.reshape(32, *v.shape[-2:]), SEND_AXES, split_axis=0, con...]
    unnamed x51 -> x65, local copies, waits for them, and re-layouts: 13.3 us -> 20.7 us
    pallas_call x7, Pallas kernels: 58.4 us -> 63.2 us  [call(): pl.pallas_call(kernel, grid_spec=pltpu.PrefetchScalarGridSpec(num_scalar_...]
    ppermute x9 -> x11, starting transfers between devices: 11.5 us -> 15.7 us  [over_core(): return lax.ppermute(v, 'core', [(0, 1), (1, 0)])]
    ppermute x3 -> x6, starting transfers between devices: 7.53 us -> 11.3 us  [the longest x3 7.67 us: over_pair(): return lax.ppermute(v, 'yl', [(0, 1), (1, 0)])]
  transfers between devices with their start and end apart: 17 -> 22, of which waited for: 9 -> 11; matrix products, arithmetic and copies ran while one was open for 0% -> 1% of each run, Pallas kernels for 23% -> 22%
where the time goes in v3:
time: 391 us; the launch traced here: 384 us
  waiting for transfers between devices  135 us (35%)
  Pallas kernels  97.5 us (25%)
  starting transfers between devices  67.5 us (17%)
  blocking collectives  59.5 us (15%)
  local copies, waits for them, and re-layouts  21.4 us (5%)
    pallas_call x7, Pallas kernels, call(): pl.pallas_call(kernel, grid_spec=pltpu.PrefetchScalarGridSpec(num_scalar_...  63.2 us
    all_to_all x1, blocking collectives, spread(): lax.all_to_all(v.reshape(32, *v.shape[-2:]), SEND_AXES, split_axis=0, con...  59.5 us
    ppermute x3, waiting for transfers between devices, over_pair(): return lax.ppermute(v, 'yl', [(0, 1), (1, 0)])  43.5 us
    all_to_all x3, waiting for transfers between devices, spread(): lax.all_to_all(v.reshape(32, *v.shape[-2:]), SEND_AXES, split_axis=0, con...  43.2 us
    all_to_all x2, waiting for transfers between devices, exchange(): lax.all_to_all(v.reshape(CHIPS, UNITS, 2 * D), CHIP_AXES, split_axis=0, c...  42.8 us
    unnamed x65, local copies, waits for them, and re-layouts  20.7 us
    all_to_all x2, starting transfers between devices, exchange(): lax.all_to_all(v.reshape(CHIPS, UNITS, 2 * D), CHIP_AXES, split_axis=0, c...  20.6 us
    all_to_all x3, starting transfers between devices, spread(): lax.all_to_all(v.reshape(32, *v.shape[-2:]), SEND_AXES, split_axis=0, con...  19.9 us
  transfers between devices with their start and end apart: 22, of which 11 were waited for; matrix products, arithmetic and copies ran while one was open for 1% of the time, Pallas kernels for 22%

profile of v3, /device:TPU:1, one launch (start us, length us, event | category | flops | bytes accessed | tf_op | source)
XLA Modules:
  0.0 384.1 jit_solution(10847082913570764848)
XLA Ops:
  0.7 1.6 copy-done.2
  2.3 1.2 copy-done.4
  3.5 1.7 prepare.1
  5.1 1.4 collective-permute-start
  7.1 0.6 copy-done.7
  7.7 0.6 fusion.6
  8.7 1.5 take_rows.1
  10.2 1.4 collective-permute-start.1
  11.6 1.9 collective-permute-start.2
  13.7 0.8 copy-done.8
  14.5 1.6 dispatch.1
  16.1 2.0 copy-done
  18.1 2.6 collective-permute-done.1.refs_2_
  20.8 2.3 collective-permute-done.2.refs_3_
  23.0 10.5 %all-to-all-start = ((bf16[64,8,4096]{2,1,0:T(8,128)(2,1)}), bf16[64,8,4096]{2,1,0:T(8,128)(2,1)}, u32[]{:S(2)}, u32[]{:S(2)}) async-start(bf16[64,8,4096]{2,1,0:T(8,128)(2,1)} %bitcast.25), calls=%async_computation | async-start | bytes 8388608 | tf_op jit(solution)/shard_map/all_to_all | solution.py:598
  33.7 2.9 select_rows.3
  36.6 3.6 select_rows.2
  40.2 42.8 %all-to-all-done = bf16[64,8,4096]{2,1,0:T(8,128)(2,1)} async-done(((bf16[64,8,4096]{2,1,0:T(8,128)(2,1)}), bf16[64,8,4096]{2,1,0:T(8,128)(2,1)}, u32[]{:S(2)}, u32[]{:S(2)}) %all-to-all-start) | async-done | bytes 4194336 | tf_op jit(solution)/shard_map/all_to_all | solution.py:598
  83.0 59.5 %all_to_all.30 = bf16[32,64,1024]{2,1,0:T(8,128)(2,1)} all-to-all(bf16[32,64,1024]{2,1,0:T(8,128)(2,1)} %select_rows.2), channel_id=1, replica_groups=mesh['yl'=2,'core'=2,'x'=4,'z'=4,'yh'=2] {'yh','x','z'}, dimensions={0} | all-to-all | bytes 8388608 | tf_op jit(solution)/shard_map/all_to_all | solution.py:594
  142.5 3.1 collective-permute-start.3
  145.6 4.9 %all-to-all-start.2 = ((bf16[32,32,1024]{2,1,0:T(8,128)(2,1)}), bf16[32,32,1024]{2,1,0:T(8,128)(2,1)}, u32[]{:S(2)}, u32[]{:S(2)}) async-start(bf16[32,32,1024]{2,1,0:T(8,128)(2,1)} %select_rows.3), calls=%async_computation.2 | async-start | bytes 4194304 | tf_op jit(solution)/shard_map/all_to_all | solution.py:594
  150.6 0.6 dynamic_slice.9
  152.8 10.5 %hidden.1 = (bf16[512,1024]{1,0:T(8,128)(2,1)}, bf16[1024,512]{1,0:T(8,128)(2,1)}, f32[512,1024]{1,0:T(8,128)}, f32[512,1024]{1,0:T(8,128)}) custom-call(s32[2]{0:T(128)} %pad_add_fusion.core, bf16[512,4096]{1,0:T(8,128)(2,1)} %bitcast.9.x.b.dy_own.dy_oth.one, bf16[2,16,64,1024]{3,2,1,0:T(8,128)(2,1)} %bitcast.10.own.own_in, ...), custom_call_target="tpu_custom_call" | custom-call | flops 1 | bytes 1 | tf_op jit(solution)/shard_map/hidden/pallas_call | solution.py:377
  163.3 9.4 %other_hidden.1.a2_t = bf16[1024,512]{1,0:T(8,128)(2,1)} custom-call(s32[2]{0:T(128)} %pad_add_fusion.core, bf16[512,4096]{1,0:T(8,128)(2,1)} %collective-permute-done.4.x.b2.two, bf16[2,16,64,1024]{3,2,1,0:T(8,128)(2,1)} %bitcast.10.own.own_in, bf16[2,16,64,1024]{3,2,1,0:T(8,128)(2,1)} %collective-permute-done.3.oth.oth_in), custom_call_target="tpu_custom_call" | custom-call | flops 1 | bytes 1 | tf_op jit(solution)/shard_map/other_hidden/pallas_call | solution.py:377
  172.7 6.7 %outer_out.1 = bf16[2,16,32,1024]{3,2,1,0:T(8,128)(2,1)} custom-call(s32[2]{0:T(128)} %pad_add_fusion.core, bf16[1024,512]{1,0:T(8,128)(2,1)} %get-tuple-element.70.a_t, bf16[1024,512]{1,0:T(8,128)(2,1)} %other_hidden.1.a2_t, bf16[512,4096]{1,0:T(8,128)(2,1)} %bitcast.9.x.b.dy_own.dy_oth.one, bf16[512,4096]{1,0:T(8,128)(2,1)} %collective-permute-done.4.x.b2.two), custom_call_target="tpu_custom_call" | custom-call | flops 1 | bytes 1 | tf_op jit(solution)/shard_map/outer_out/pallas_call | solution.py:377
  179.6 1.6 collective-permute-start.5
  181.2 8.3 %all-to-all-start.3 = ((bf16[32,32,1024]{2,1,0:T(8,128)(2,1)}), bf16[32,32,1024]{2,1,0:T(8,128)(2,1)}, u32[]{:S(2)}, u32[]{:S(2)}) async-start(bf16[32,32,1024]{2,1,0:T(8,128)(2,1)} %bitcast.32), calls=%async_computation.3 | async-start | bytes 4194304 | tf_op jit(solution)/shard_map/all_to_all | solution.py:594
  189.5 1.3 copy-done.26
  190.8 7.9 %back.1 = (bf16[512,1024]{1,0:T(8,128)(2,1)}, bf16[512,1024]{1,0:T(8,128)(2,1)}) custom-call(s32[2]{0:T(128)} %pad_add_fusion.core, bf16[512,4096]{1,0:T(8,128)(2,1)} %bitcast.9.x.b.dy_own.dy_oth.one, bf16[512,4096]{1,0:T(8,128)(2,1)} %bitcast.9.x.b.dy_own.dy_oth.one, bf16[2,16,32,1024]{3,2,1,0:T(8,128)(2,1)} %bitcast.11.own.own_out, ...), custom_call_target="tpu_custom_call" | custom-call | flops 1 | bytes 1 | tf_op jit(solution)/shard_map/back/pallas_call | solution.py:377
  199.0 5.6 %flip.1 = (bf16[2048,512]{1,0:T(8,128)(2,1)}, bf16[2048,512]{1,0:T(8,128)(2,1)}) custom-call(s32[2]{0:T(128)} %pad_add_fusion.core, bf16[512,4096]{1,0:T(8,128)(2,1)} %bitcast.9.x.b.dy_own.dy_oth.one, bf16[512,4096]{1,0:T(8,128)(2,1)} %collective-permute-done.4.x.b2.two), custom_call_target="tpu_custom_call" | custom-call | flops 10000000000 | bytes 20000000 | tf_op jit(solution)/shard_map/flip/pallas_call | solution.py:377
  204.6 1.0 copy-done.27
  205.6 9.4 %outer_in.1 = bf16[2,16,64,1024]{3,2,1,0:T(8,128)(2,1)} custom-call(s32[2]{0:T(128)} %pad_add_fusion.core, bf16[2048,512]{1,0:T(8,128)(2,1)} %get-tuple-element.80.a_t, bf16[2048,512]{1,0:T(8,128)(2,1)} %get-tuple-element.81.a2_t, bf16[512,1024]{1,0:T(8,128)(2,1)} %get-tuple-element.78.d_own.b, bf16[512,1024]{1,0:T(8,128)(2,1)} %copy-done.27), custom_call_target="tpu_custom_call" | custom-call | flops 1 | bytes 1 | tf_op jit(solution)/shard_map/outer_in/pallas_call | solution.py:377
  214.9 3.8 %all-to-all-done.3 = bf16[32,32,1024]{2,1,0:T(8,128)(2,1)} async-done(((bf16[32,32,1024]{2,1,0:T(8,128)(2,1)}), bf16[32,32,1024]{2,1,0:T(8,128)(2,1)}, u32[]{:S(2)}, u32[]{:S(2)}) %all-to-all-start.3) | async-done | bytes 2097184 | tf_op jit(solution)/shard_map/all_to_all | solution.py:594
  218.8 6.7 %all-to-all-start.4 = ((bf16[32,64,1024]{2,1,0:T(8,128)(2,1)}), bf16[32,64,1024]{2,1,0:T(8,128)(2,1)}, u32[]{:S(2)}, u32[]{:S(2)}) async-start(bf16[32,64,1024]{2,1,0:T(8,128)(2,1)} %bitcast.30), calls=%async_computation.4 | async-start | bytes 8388608 | tf_op jit(solution)/shard_map/all_to_all | solution.py:594
  225.5 13.7 %give.1 = bf16[512,4096]{1,0:T(8,128)(2,1)} custom-call(s32[2]{0:T(128)} %pad_add_fusion.core, bf16[512,1024]{1,0:T(8,128)(2,1)} %get-tuple-element.69.hidden, bf16[512,1024]{1,0:T(8,128)(2,1)} %get-tuple-element.78.d_own.b, bf16[512,1024]{1,0:T(8,128)(2,1)} %get-tuple-element.79.d_oth, bf16[2,16,32,1024]{3,2,1,0:T(8,128)(2,1)} %bitcast.11.own.own_out, ...), custom_call_target="tpu_custom_call" | custom-call | flops 1 | bytes 1 | tf_op jit(solution)/shard_map/give/pallas_call | solution.py:377
  239.2 39.2 %all-to-all-done.4 = bf16[32,64,1024]{2,1,0:T(8,128)(2,1)} async-done(((bf16[32,64,1024]{2,1,0:T(8,128)(2,1)}), bf16[32,64,1024]{2,1,0:T(8,128)(2,1)}, u32[]{:S(2)}, u32[]{:S(2)}) %all-to-all-start.4) | async-done | bytes 4194336 | tf_op jit(solution)/shard_map/all_to_all | solution.py:594
  278.3 5.1 %sum_rows.2 = (bf16[4,64,1024]{2,1,0:T(8,128)(2,1)S(1)}, bf16[4,64,1024]{2,1,0:T(8,128)(2,1)}, bf16[2,64,1024]{2,1,0:T(8,128)(2,1)S(1)}, bf16[2,64,1024]{2,1,0:T(8,128)(2,1)S(1)}) custom-call(s32[32]{0:T(128)S(1)} %select_reduce_fusion.index, bf16[32,64,1024]{2,1,0:T(8,128)(2,1)} %bitcast.16.rows), custom_call_target="tpu_custom_call" | custom-call | flops 10000000000 | bytes 20000000 | tf_op jit(solution)/shard_map/sum_rows/pallas_call | solution.py:312
  283.4 0.8 copy-done.22
  284.2 5.3 %collective-permute-start.7 = (bf16[2,64,1024]{2,1,0:T(8,128)(2,1)S(1)}, bf16[2,64,1024]{2,1,0:T(8,128)(2,1)S(1)}, u32[]{:S(2)}, u32[]{:S(2)}) collective-permute-start(bf16[2,64,1024]{2,1,0:T(8,128)(2,1)S(1)} %get-tuple-element.84), channel_id=1, source_target_pairs={{0,64},{64,0},{1,65},{65,1},{2,66},{66,2},{3,67},{67,3},{4,68},{68... | collective-permute-start | bytes 786440 | tf_op jit(solution)/shard_map/ppermute | solution.py:566
  289.5 3.8 collective-permute-done.7.refs_1_
  293.2 2.7 collective-permute-done.8.refs_2_
  295.9 10.1 %all-to-all-start.5 = ((bf16[64,8,4096]{2,1,0:T(8,128)(2,1)}), bf16[64,8,4096]{2,1,0:T(8,128)(2,1)}, u32[]{:S(2)}, u32[]{:S(2)}) async-start(bf16[64,8,4096]{2,1,0:T(8,128)(2,1)} %bitcast.31), calls=%async_computation.5 | async-start | bytes 8388608 | tf_op jit(solution)/shard_map/all_to_all | solution.py:598
  306.0 2.5 sum_rows.3
  308.6 0.7 copy-done.24
  309.3 1.0 collective-permute-start.12
  310.3 1.7 collective-permute-start.13
  312.0 3.7 collective-permute-start.14
  315.7 37.1 %collective-permute-done.12.refs_1_ = bf16[2,32,1024]{2,1,0:T(8,128)(2,1)S(1)} collective-permute-done((bf16[2,32,1024]{2,1,0:T(8,128)(2,1)S(1)}, bf16[2,32,1024]{2,1,0:T(8,128)(2,1)S(1)}, u32[]{:S(2)}, u32[]{:S(2)}) %collective-permute-start.12) | collective-permute-done | bytes 131104 | tf_op jit(solution)/shard_map/ppermute | solution.py:566
  352.8 4.5 %collective-permute-start.15 = (bf16[2,32,1024]{2,1,0:T(8,128)(2,1)S(1)}, bf16[2,32,1024]{2,1,0:T(8,128)(2,1)S(1)}, u32[]{:S(2)}, u32[]{:S(2)}) collective-permute-start(bf16[2,32,1024]{2,1,0:T(8,128)(2,1)S(1)} %collective-permute-done.12.refs_1_), channel_id=1, source_target_pairs={{0,32},{32,0},{1,33},{33,1},{2,34},{34,2},{3,35},{35,3},{4,36},{36... | collective-permute-start | bytes 393224 | tf_op jit(solution)/shard_map/ppermute | solution.py:562
  357.3 0.7 copy-done.16
  358.9 0.7 copy-done.18
  360.0 0.7 copy-done.20
  360.6 0.7 copy-done.14
  361.3 1.2 copy-done.12
  362.6 1.2 copy-done.13
  363.8 0.9 copy-done.15
  364.7 0.9 copy-done.17
  365.6 0.9 copy-done.19
  366.5 0.9 copy-done.21
  367.4 0.9 copy-done.25
  368.4 3.2 adam.3
  371.7 6.9 %adam.2 = (f32[4,64,2048]{2,1,0:T(8,128)}, f32[4,64,2048]{2,1,0:T(8,128)}, f32[4,64,2048]{2,1,0:T(8,128)}) custom-call(s32[5]{0:T(128)S(1)} %pad_add_fusion.1.sel, f32[4,64,2048]{2,1,0:T(8,128)S(1)} %copy-done.3, f32[4,64,2048]{2,1,0:T(8,128)} %moment.2, f32[4,64,2048]{2,1,0:T(8,128)} %square.2, bf16[4,64,1024]{2,1,0:T(8,128)(2,1)S(1)} %copy-done.23, ...), custom_call_target="tpu_custom_call" | custom-call | flops 10000000000 | bytes 20000000 | tf_op jit(solution)/shard_map/adam/pallas_call | solution.py:350
  378.5 4.9 %combine.1 = (bf16[128,2048]{1,0:T(8,128)(2,1)}, bf16[128,2048]{1,0:T(8,128)(2,1)}, f32[128,2]{1,0:T(8,128)S(1)}) custom-call(f32[128,2]{1,0:T(8,128)S(1)} %get-tuple-element.64.dest, f32[128,2]{1,0:T(8,128)S(1)} %copy.26.weight, bf16[128,2048]{1,0:T(8,128)(2,1)S(1)} %copy-done.1, bf16[512,4096]{1,0:T(8,128)(2,1)} %bitcast.18.out.dx, ...), custom_call_target="tpu_custom_call" | custom-call | tf_op jit(solution)/shard_map/combine/pallas_call | solution.py:184
  383.4 0.6 copy.27
  (75 shorter events, 3.9 us)
Async XLA Ops:
  0.6 5.9 %copy-start.11 = (s32[128]{0:T(128)S(1)}, s32[128]{0:T(128)}, u32[]{:S(2)}) copy-start(s32[128]{0:T(128)} %param.14) | copy-start | bytes 1540
  0.7 1.6 copy-start.2
  2.3 1.2 copy-start.4
  3.5 10.0 %copy-start.9 = (s32[128,2]{0,1:T(2,128)S(1)}, s32[128,2]{0,1:T(2,128)}, u32[]{:S(2)}) copy-start(s32[128,2]{0,1:T(2,128)} %param.15) | copy-start | bytes 3076
  3.5 10.1 %copy-start.1 = (bf16[128,2048]{1,0:T(8,128)(2,1)S(1)}, bf16[128,2048]{1,0:T(8,128)(2,1)}, u32[]{:S(2)}) copy-start(bf16[128,2048]{1,0:T(8,128)(2,1)} %cot.3) | copy-start | bytes 1572868
  3.5 10.1 %copy-start.6 = (bf16[128,2048]{1,0:T(8,128)(2,1)S(1)}, bf16[128,2048]{1,0:T(8,128)(2,1)}, u32[]{:S(2)}) copy-start(bf16[128,2048]{1,0:T(8,128)(2,1)} %tok) | copy-start | bytes 1572868
  3.5 10.2 %copy-start.10 = (f32[128,2]{0,1:T(2,128)S(1)}, f32[128,2]{0,1:T(2,128)}, u32[]{:S(2)}) copy-start(f32[128,2]{0,1:T(2,128)} %param.13) | copy-start | bytes 3076
  5.1 3.6 collective-permute-start
  7.1 0.6 copy-start.7
  10.2 10.5 %collective-permute-start.1 = (bf16[2,96,1024]{2,1,0:T(8,128)(2,1)}, bf16[2,96,1024]{2,1,0:T(8,128)(2,1)S(1)}, u32[]{:S(2)}, u32[]{:S(2)}) collective-permute-start(bf16[2,96,1024]{2,1,0:T(8,128)(2,1)} %get-tuple-element.61), channel_id=1, source_target_pairs={{0,64},{64,0},{1,65},{65,1},{2,66},{66,2},{3,67},{67,3},{4,68},{68... | collective-permute-start | bytes 1179656 | tf_op jit(solution)/shard_map/ppermute | solution.py:566
  11.6 11.4 %collective-permute-start.2 = (bf16[2,96,1024]{2,1,0:T(8,128)(2,1)}, bf16[2,96,1024]{2,1,0:T(8,128)(2,1)S(1)}, u32[]{:S(2)}, u32[]{:S(2)}) collective-permute-start(bf16[2,96,1024]{2,1,0:T(8,128)(2,1)} %get-tuple-element.62), channel_id=1, source_target_pairs={{0,65},{65,0},{1,64},{64,1},{2,67},{67,2},{3,66},{66,3},{4,69},{69... | collective-permute-start | bytes 1179656 | tf_op jit(solution)/shard_map/ppermute | solution.py:570
  13.6 0.8 copy-start.8
  16.1 2.0 copy-start
  23.0 10.5 %copy-start.28 = (s32[16]{0:T(128)S(1)}, s32[16]{0:T(128)}, u32[]{:S(2)}) copy-start(s32[16]{0:T(128)} %get-tuple-element.125) | copy-start | bytes 196
  23.0 10.5 %copy-start.29 = (s32[1,16]{1,0:T(1,128)S(1)}, s32[1,16]{1,0:T(1,128)}, u32[]{:S(2)}) copy-start(s32[1,16]{1,0:T(1,128)} %get-tuple-element.126) | copy-start | bytes 196
  23.0 60.0 %all-to-all-start = ((bf16[64,8,4096]{2,1,0:T(8,128)(2,1)}), bf16[64,8,4096]{2,1,0:T(8,128)(2,1)}, u32[]{:S(2)}, u32[]{:S(2)}) async-start(bf16[64,8,4096]{2,1,0:T(8,128)(2,1)} %bitcast.25), calls=%async_computation | async-start | bytes 8388608 | tf_op jit(solution)/shard_map/all_to_all | solution.py:598
  142.5 10.3 %collective-permute-start.3 = (bf16[2,16,64,1024]{3,2,1,0:T(8,128)(2,1)}, bf16[2,16,64,1024]{3,2,1,0:T(8,128)(2,1)}, u32[]{:S(2)}, u32[]{:S(2)}) collective-permute-start(bf16[2,16,64,1024]{3,2,1,0:T(8,128)(2,1)} %bitcast.10.own.own_in), channel_id=1, source_target_pairs={{0,32},{32,0},{1,33},{33,1},{2,34},{34,2},{3,35},{35,3},{4,36},{36... | collective-permute-start | bytes 12582920 | tf_op jit(solution)/shard_map/ppermute | solution.py:562
  145.6 17.6 %collective-permute-start.4 = (bf16[512,4096]{1,0:T(8,128)(2,1)}, bf16[512,4096]{1,0:T(8,128)(2,1)}, u32[]{:S(2)}, u32[]{:S(2)}) collective-permute-start(bf16[512,4096]{1,0:T(8,128)(2,1)} %bitcast.9.x.b.dy_own.dy_oth.one), channel_id=1, source_target_pairs={{0,32},{32,0},{1,33},{33,1},{2,34},{34,2},{3,35},{35,3},{4,36},{36... | collective-permute-start | bytes 12582920 | tf_op jit(solution)/shard_map/ppermute | solution.py:562
  145.6 34.0 %all-to-all-start.2 = ((bf16[32,32,1024]{2,1,0:T(8,128)(2,1)}), bf16[32,32,1024]{2,1,0:T(8,128)(2,1)}, u32[]{:S(2)}, u32[]{:S(2)}) async-start(bf16[32,32,1024]{2,1,0:T(8,128)(2,1)} %select_rows.3), calls=%async_computation.2 | async-start | bytes 4194304 | tf_op jit(solution)/shard_map/all_to_all | solution.py:594
  179.6 9.9 %collective-permute-start.5 = (bf16[2,16,32,1024]{3,2,1,0:T(8,128)(2,1)}, bf16[2,16,32,1024]{3,2,1,0:T(8,128)(2,1)S(1)}, u32[]{:S(2)}, u32[]{:S(2)}) collective-permute-start(bf16[2,16,32,1024]{3,2,1,0:T(8,128)(2,1)} %bitcast.11.own.own_out), channel_id=1, source_target_pairs={{0,32},{32,0},{1,33},{33,1},{2,34},{34,2},{3,35},{35,3},{4,36},{36... | collective-permute-start | bytes 6291464 | tf_op jit(solution)/shard_map/ppermute | solution.py:562
  181.2 37.6 %all-to-all-start.3 = ((bf16[32,32,1024]{2,1,0:T(8,128)(2,1)}), bf16[32,32,1024]{2,1,0:T(8,128)(2,1)}, u32[]{:S(2)}, u32[]{:S(2)}) async-start(bf16[32,32,1024]{2,1,0:T(8,128)(2,1)} %bitcast.32), calls=%async_computation.3 | async-start | bytes 4194304 | tf_op jit(solution)/shard_map/all_to_all | solution.py:594
  189.5 1.3 copy-start.26
  198.7 5.9 %collective-permute-start.6 = (bf16[512,1024]{1,0:T(8,128)(2,1)}, bf16[512,1024]{1,0:T(8,128)(2,1)S(1)}, u32[]{:S(2)}, u32[]{:S(2)}) collective-permute-start(bf16[512,1024]{1,0:T(8,128)(2,1)} %get-tuple-element.79.d_oth), channel_id=1, source_target_pairs={{0,32},{32,0},{1,33},{33,1},{2,34},{34,2},{3,35},{35,3},{4,36},{36... | collective-permute-start | bytes 3145736 | tf_op jit(solution)/shard_map/ppermute | solution.py:562
  204.6 1.0 copy-start.27
  218.8 59.6 %all-to-all-start.4 = ((bf16[32,64,1024]{2,1,0:T(8,128)(2,1)}), bf16[32,64,1024]{2,1,0:T(8,128)(2,1)}, u32[]{:S(2)}, u32[]{:S(2)}) async-start(bf16[32,64,1024]{2,1,0:T(8,128)(2,1)} %bitcast.30), calls=%async_computation.4 | async-start | bytes 8388608 | tf_op jit(solution)/shard_map/all_to_all | solution.py:594
  283.4 0.8 copy-start.22
  284.2 9.0 %collective-permute-start.7 = (bf16[2,64,1024]{2,1,0:T(8,128)(2,1)S(1)}, bf16[2,64,1024]{2,1,0:T(8,128)(2,1)S(1)}, u32[]{:S(2)}, u32[]{:S(2)}) collective-permute-start(bf16[2,64,1024]{2,1,0:T(8,128)(2,1)S(1)} %get-tuple-element.84), channel_id=1, source_target_pairs={{0,64},{64,0},{1,65},{65,1},{2,66},{66,2},{3,67},{67,3},{4,68},{68... | collective-permute-start | bytes 786440 | tf_op jit(solution)/shard_map/ppermute | solution.py:566
  289.5 6.4 %collective-permute-start.8 = (bf16[2,64,1024]{2,1,0:T(8,128)(2,1)S(1)}, bf16[2,64,1024]{2,1,0:T(8,128)(2,1)S(1)}, u32[]{:S(2)}, u32[]{:S(2)}) collective-permute-start(bf16[2,64,1024]{2,1,0:T(8,128)(2,1)S(1)} %get-tuple-element.85), channel_id=1, source_target_pairs={{0,65},{65,0},{1,64},{64,1},{2,67},{67,2},{3,66},{66,3},{4,69},{69... | collective-permute-start | bytes 786440 | tf_op jit(solution)/shard_map/ppermute | solution.py:570
  295.9 82.6 %all-to-all-start.5 = ((bf16[64,8,4096]{2,1,0:T(8,128)(2,1)}), bf16[64,8,4096]{2,1,0:T(8,128)(2,1)}, u32[]{:S(2)}, u32[]{:S(2)}) async-start(bf16[64,8,4096]{2,1,0:T(8,128)(2,1)} %bitcast.31), calls=%async_computation.5 | async-start | bytes 8388608 | tf_op jit(solution)/shard_map/all_to_all | solution.py:598
  306.0 52.0 %copy-start.30 = (s32[1,16]{1,0:T(1,128)S(1)}, s32[1,16]{1,0:T(1,128)}, u32[]{:S(2)}) copy-start(s32[1,16]{1,0:T(1,128)} %get-tuple-element.123) | copy-start | bytes 196
  306.0 55.3 %copy-start.5 = (f32[4,32,2048]{2,1,0:T(8,128)S(1)}, f32[4,32,2048]{2,1,0:T(8,128)}, u32[]{:S(2)}) copy-start(f32[4,32,2048]{2,1,0:T(8,128)} %weight.4) | copy-start | bytes 3145732
  308.6 0.7 copy-start.24
  309.3 43.6 %collective-permute-start.12 = (bf16[2,32,1024]{2,1,0:T(8,128)(2,1)S(1)}, bf16[2,32,1024]{2,1,0:T(8,128)(2,1)S(1)}, u32[]{:S(2)}, u32[]{:S(2)}) collective-permute-start(bf16[2,32,1024]{2,1,0:T(8,128)(2,1)S(1)} %get-tuple-element.97), channel_id=1, source_target_pairs={{0,64},{64,0},{1,65},{65,1},{2,66},{66,2},{3,67},{67,3},{4,68},{68... | collective-permute-start | bytes 393224 | tf_op jit(solution)/shard_map/ppermute | solution.py:566
  310.3 47.0 %collective-permute-start.13 = (bf16[2,32,1024]{2,1,0:T(8,128)(2,1)S(1)}, bf16[2,32,1024]{2,1,0:T(8,128)(2,1)S(1)}, u32[]{:S(2)}, u32[]{:S(2)}) collective-permute-start(bf16[2,32,1024]{2,1,0:T(8,128)(2,1)S(1)} %get-tuple-element.98), channel_id=1, source_target_pairs={{0,65},{65,0},{1,64},{64,1},{2,67},{67,2},{3,66},{66,3},{4,69},{69... | collective-permute-start | bytes 393224 | tf_op jit(solution)/shard_map/ppermute | solution.py:570
  312.0 48.6 %collective-permute-start.14 = (bf16[4,32,1024]{2,1,0:T(8,128)(2,1)S(1)}, bf16[4,32,1024]{2,1,0:T(8,128)(2,1)S(1)}, u32[]{:S(2)}, u32[]{:S(2)}) collective-permute-start(bf16[4,32,1024]{2,1,0:T(8,128)(2,1)S(1)} %get-tuple-element.99), channel_id=1, source_target_pairs={{0,32},{32,0},{1,33},{33,1},{2,34},{34,2},{3,35},{35,3},{4,36},{36... | collective-permute-start | bytes 786440 | tf_op jit(solution)/shard_map/ppermute | solution.py:562
  352.8 6.0 %collective-permute-start.15 = (bf16[2,32,1024]{2,1,0:T(8,128)(2,1)S(1)}, bf16[2,32,1024]{2,1,0:T(8,128)(2,1)S(1)}, u32[]{:S(2)}, u32[]{:S(2)}) collective-permute-start(bf16[2,32,1024]{2,1,0:T(8,128)(2,1)S(1)} %collective-permute-done.12.refs_1_), channel_id=1, source_target_pairs={{0,32},{32,0},{1,33},{33,1},{2,34},{34,2},{3,35},{35,3},{4,36},{36... | collective-permute-start | bytes 393224 | tf_op jit(solution)/shard_map/ppermute | solution.py:562
  357.3 2.6 collective-permute-start.16
  357.3 0.7 copy-start.16
  358.3 13.4 %collective-permute-start.9 = (bf16[4,64,1024]{2,1,0:T(8,128)(2,1)}, bf16[4,64,1024]{2,1,0:T(8,128)(2,1)S(1)}, u32[]{:S(2)}, u32[]{:S(2)}) collective-permute-start(bf16[4,64,1024]{2,1,0:T(8,128)(2,1)} %get-tuple-element.91), channel_id=1, source_target_pairs={{0,32},{32,0},{1,33},{33,1},{2,34},{34,2},{3,35},{35,3},{4,36},{36... | collective-permute-start | bytes 1572872 | tf_op jit(solution)/shard_map/ppermute | solution.py:562
  358.8 12.8 %collective-permute-start.10 = (bf16[2,64,1024]{2,1,0:T(8,128)(2,1)S(1)}, bf16[2,64,1024]{2,1,0:T(8,128)(2,1)S(1)}, u32[]{:S(2)}, u32[]{:S(2)}) collective-permute-start(bf16[2,64,1024]{2,1,0:T(8,128)(2,1)S(1)} %collective-permute-done.7.refs_1_), channel_id=1, source_target_pairs={{0,32},{32,0},{1,33},{33,1},{2,34},{34,2},{3,35},{35,3},{4,36},{36... | collective-permute-start | bytes 786440 | tf_op jit(solution)/shard_map/ppermute | solution.py:562
  358.9 0.7 copy-start.18
  359.5 12.1 %collective-permute-start.11 = (bf16[2,64,1024]{2,1,0:T(8,128)(2,1)S(1)}, bf16[2,64,1024]{2,1,0:T(8,128)(2,1)S(1)}, u32[]{:S(2)}, u32[]{:S(2)}) collective-permute-start(bf16[2,64,1024]{2,1,0:T(8,128)(2,1)S(1)} %collective-permute-done.8.refs_2_), channel_id=1, source_target_pairs={{0,32},{32,0},{1,33},{33,1},{2,34},{34,2},{3,35},{35,3},{4,36},{36... | collective-permute-start | bytes 786440 | tf_op jit(solution)/shard_map/ppermute | solution.py:562
  360.0 0.7 copy-start.20
  360.6 0.7 copy-start.14
  361.3 1.2 copy-start.12
  362.6 1.2 copy-start.13
  363.8 0.9 copy-start.15
  364.7 0.9 copy-start.17
  365.6 0.9 copy-start.19
  366.5 0.9 copy-start.21
  367.4 0.9 copy-start.25
  368.4 3.3 copy-start.3
  368.4 3.3 copy-start.23

commit v4 on v3

--- a/solution.py
+++ b/solution.py
@@ -237,7 +237,7 @@
         out_shape=[jax.ShapeDtypeStruct((n, r + ro, HALF), BF)] * 2,
         compiler_params=params(),
         name="prepare",
-    )(core, w_in, w_out)
+    )(core, pltpu.with_memory_space_constraint(w_in, pltpu.HBM), pltpu.with_memory_space_constraint(w_out, pltpu.HBM))
 
 
 def copy_one(e, parts, out, j):
@@ -654,8 +654,8 @@
     result = give_of(which, hidden, d_own, d_oth, own_out, oth_out, own_in, oth_in)
     own, other = gather_sums(after(rows_out, result))
     trained_out, mean_out, square_out = adam(sel, proj_out, first_out, second_out, own, other)
-    own2, other2 = gather_sums(after(rows_in, result))
-    back = exchange(after(result, *own2[1:]))
+    own2, other2 = gather_sums(after(rows_in, result, *own))
+    back = exchange(after(result, *own[1:], *own2[1:]))
     trained_in, mean_in, square_in = adam(sel, proj_in, first_in, second_in, own2, other2)
     mixed, token_grad, mix_grad = combine(dest, route_weight, cotangent, back)
     return (

time: 391 us -> 369 us (0.944)
  waiting for transfers between devices: 135 us -> 121 us
  local copies, waits for them, and re-layouts: 21.4 us -> 10.5 us
    all_to_all x3, waiting for transfers between devices: 43.2 us -> 2.85 us  [spread(): lax.all_to_all(v.reshape(32, *v.shape[-2:]), SEND_AXES, split_axis=0, con...]
    all_to_all x2, waiting for transfers between devices: 42.8 us -> 74.1 us  [exchange(): lax.all_to_all(v.reshape(CHIPS, UNITS, 2 * D), CHIP_AXES, split_axis=0, c...]
    unnamed x65 -> x53, local copies, waits for them, and re-layouts: 20.7 us -> 9.7 us
    ppermute x3, waiting for transfers between devices: 43.5 us -> 36.8 us  [over_pair(): return lax.ppermute(v, 'yl', [(0, 1), (1, 0)])]
    ppermute x11, starting transfers between devices: 15.7 us -> 11 us  [over_core(): return lax.ppermute(v, 'core', [(0, 1), (1, 0)])]
  transfers between devices with their start and end apart: 22 -> 22, of which waited for: 11 -> 11; matrix products, arithmetic and copies ran while one was open for 1% -> 1% of each run, Pallas kernels for 22% -> 24%
where the time goes in v4:
time: 369 us; the launch traced here: 364 us
  waiting for transfers between devices  121 us (33%)
  Pallas kernels  100 us (27%)
  starting transfers between devices  70 us (19%)
  blocking collectives  59.4 us (16%)
  local copies, waits for them, and re-layouts  10.5 us (3%)
    all_to_all x2, waiting for transfers between devices, exchange(): lax.all_to_all(v.reshape(CHIPS, UNITS, 2 * D), CHIP_AXES, split_axis=0, c...  74.1 us
    pallas_call x7, Pallas kernels, call(): pl.pallas_call(kernel, grid_spec=pltpu.PrefetchScalarGridSpec(num_scalar_...  63.2 us
    all_to_all x1, blocking collectives, spread(): lax.all_to_all(v.reshape(32, *v.shape[-2:]), SEND_AXES, split_axis=0, con...  59.4 us
    ppermute x3, waiting for transfers between devices, over_pair(): return lax.ppermute(v, 'yl', [(0, 1), (1, 0)])  36.8 us
    all_to_all x2, starting transfers between devices, exchange(): lax.all_to_all(v.reshape(CHIPS, UNITS, 2 * D), CHIP_AXES, split_axis=0, c...  22 us
    all_to_all x3, starting transfers between devices, spread(): lax.all_to_all(v.reshape(32, *v.shape[-2:]), SEND_AXES, split_axis=0, con...  21.2 us
    pallas_call x2, Pallas kernels, adam(): pl.pallas_call(adam_kernel, grid_spec=pltpu.PrefetchScalarGridSpec(num_sc...  11.6 us
    ppermute x11, starting transfers between devices, over_core(): return lax.ppermute(v, 'core', [(0, 1), (1, 0)])  11 us
  transfers between devices with their start and end apart: 22, of which 11 were waited for; matrix products, arithmetic and copies ran while one was open for 1% of the time, Pallas kernels for 24%

profile of v4, /device:TPU:1, one launch (start us, length us, event | category | flops | bytes accessed | tf_op | source)
XLA Modules:
  0.0 363.9 jit_solution(8107387082616211421)
XLA Ops:
  0.7 3.9 %prepare.1 = (bf16[4,96,1024]{2,1,0:T(8,128)(2,1)S(1)}, bf16[4,96,1024]{2,1,0:T(8,128)(2,1)}) custom-call(s32[1]{0:T(128)} %bitcast.5.core, f32[4,64,2048]{2,1,0:T(8,128)} %weight.3, f32[4,32,2048]{2,1,0:T(8,128)} %weight.4), custom_call_target="tpu_custom_call" | custom-call | tf_op jit(solution)/shard_map/prepare/pallas_call | solution.py:226
  4.6 1.4 collective-permute-start
  6.1 0.4 plan.1
  6.5 0.6 copy-done.5
  7.2 0.6 fusion.6
  7.7 0.1 select_reduce_fusion.1.index
  7.9 0.3 collective-permute-done.theirs.refs_1_
  8.1 1.5 take_rows.1
  9.7 1.4 collective-permute-start.1
  11.0 1.9 collective-permute-start.2
  13.1 0.8 copy-done.6
  13.9 1.6 dispatch.1
  15.6 2.0 copy-done
  17.6 2.6 collective-permute-done.1.refs_2_
  20.2 2.3 collective-permute-done.2.refs_3_
  22.5 10.5 %all-to-all-start = ((bf16[64,8,4096]{2,1,0:T(8,128)(2,1)}), bf16[64,8,4096]{2,1,0:T(8,128)(2,1)}, u32[]{:S(2)}, u32[]{:S(2)}) async-start(bf16[64,8,4096]{2,1,0:T(8,128)(2,1)} %bitcast.25), calls=%async_computation | async-start | bytes 8388608 | tf_op jit(solution)/shard_map/all_to_all | solution.py:598
  33.1 2.9 select_rows.3
  36.1 3.6 select_rows.2
  39.6 42.8 %all-to-all-done = bf16[64,8,4096]{2,1,0:T(8,128)(2,1)} async-done(((bf16[64,8,4096]{2,1,0:T(8,128)(2,1)}), bf16[64,8,4096]{2,1,0:T(8,128)(2,1)}, u32[]{:S(2)}, u32[]{:S(2)}) %all-to-all-start) | async-done | bytes 4194336 | tf_op jit(solution)/shard_map/all_to_all | solution.py:598
  82.4 59.4 %all_to_all.30 = bf16[32,64,1024]{2,1,0:T(8,128)(2,1)} all-to-all(bf16[32,64,1024]{2,1,0:T(8,128)(2,1)} %select_rows.2), channel_id=1, replica_groups=mesh['yl'=2,'core'=2,'x'=4,'z'=4,'yh'=2] {'yh','x','z'}, dimensions={0} | all-to-all | bytes 8388608 | tf_op jit(solution)/shard_map/all_to_all | solution.py:594
  141.9 3.2 collective-permute-start.3
  145.1 4.8 %all-to-all-start.2 = ((bf16[32,32,1024]{2,1,0:T(8,128)(2,1)}), bf16[32,32,1024]{2,1,0:T(8,128)(2,1)S(1)}, u32[]{:S(2)}, u32[]{:S(2)}) async-start(bf16[32,32,1024]{2,1,0:T(8,128)(2,1)} %select_rows.3), calls=%async_computation.2 | async-start | bytes 4194304 | tf_op jit(solution)/shard_map/all_to_all | solution.py:594
  149.9 0.6 dynamic_slice.9
  151.1 0.6 pad_add_fusion.core
  151.7 0.5 collective-permute-done.3.oth.oth_in
  152.2 10.5 %hidden.1 = (bf16[512,1024]{1,0:T(8,128)(2,1)}, bf16[1024,512]{1,0:T(8,128)(2,1)}, f32[512,1024]{1,0:T(8,128)}, f32[512,1024]{1,0:T(8,128)}) custom-call(s32[2]{0:T(128)} %pad_add_fusion.core, bf16[512,4096]{1,0:T(8,128)(2,1)} %bitcast.9.x.b.dy_own.dy_oth.one, bf16[2,16,64,1024]{3,2,1,0:T(8,128)(2,1)} %bitcast.10.own.own_in, ...), custom_call_target="tpu_custom_call" | custom-call | flops 1 | bytes 1 | tf_op jit(solution)/shard_map/hidden/pallas_call | solution.py:377
  162.7 9.4 %other_hidden.1.a2_t = bf16[1024,512]{1,0:T(8,128)(2,1)} custom-call(s32[2]{0:T(128)} %pad_add_fusion.core, bf16[512,4096]{1,0:T(8,128)(2,1)} %collective-permute-done.4.x.b2.two, bf16[2,16,64,1024]{3,2,1,0:T(8,128)(2,1)} %bitcast.10.own.own_in, bf16[2,16,64,1024]{3,2,1,0:T(8,128)(2,1)} %collective-permute-done.3.oth.oth_in), custom_call_target="tpu_custom_call" | custom-call | flops 1 | bytes 1 | tf_op jit(solution)/shard_map/other_hidden/pallas_call | solution.py:377
  172.2 6.7 %outer_out.1 = bf16[2,16,32,1024]{3,2,1,0:T(8,128)(2,1)} custom-call(s32[2]{0:T(128)} %pad_add_fusion.core, bf16[1024,512]{1,0:T(8,128)(2,1)} %get-tuple-element.70.a_t, bf16[1024,512]{1,0:T(8,128)(2,1)} %other_hidden.1.a2_t, bf16[512,4096]{1,0:T(8,128)(2,1)} %bitcast.9.x.b.dy_own.dy_oth.one, bf16[512,4096]{1,0:T(8,128)(2,1)} %collective-permute-done.4.x.b2.two), custom_call_target="tpu_custom_call" | custom-call | flops 1 | bytes 1 | tf_op jit(solution)/shard_map/outer_out/pallas_call | solution.py:377
  178.9 1.6 collective-permute-start.5
  180.5 8.6 %all-to-all-start.3 = ((bf16[32,32,1024]{2,1,0:T(8,128)(2,1)}), bf16[32,32,1024]{2,1,0:T(8,128)(2,1)}, u32[]{:S(2)}, u32[]{:S(2)}) async-start(bf16[32,32,1024]{2,1,0:T(8,128)(2,1)} %bitcast.35), calls=%async_computation.3 | async-start | bytes 4194304 | tf_op jit(solution)/shard_map/all_to_all | solution.py:594
  189.1 7.9 %back.1 = (bf16[512,1024]{1,0:T(8,128)(2,1)}, bf16[512,1024]{1,0:T(8,128)(2,1)}) custom-call(s32[2]{0:T(128)} %pad_add_fusion.core, bf16[512,4096]{1,0:T(8,128)(2,1)} %bitcast.9.x.b.dy_own.dy_oth.one, bf16[512,4096]{1,0:T(8,128)(2,1)} %bitcast.9.x.b.dy_own.dy_oth.one, bf16[2,16,32,1024]{3,2,1,0:T(8,128)(2,1)} %bitcast.31, ...), custom_call_target="tpu_custom_call" | custom-call | flops 1 | bytes 1 | tf_op jit(solution)/shard_map/back/pallas_call | solution.py:377
  197.0 1.3 collective-permute-start.8
  198.3 5.6 %flip.1 = (bf16[2048,512]{1,0:T(8,128)(2,1)}, bf16[2048,512]{1,0:T(8,128)(2,1)}) custom-call(s32[2]{0:T(128)} %pad_add_fusion.core, bf16[512,4096]{1,0:T(8,128)(2,1)} %bitcast.9.x.b.dy_own.dy_oth.one, bf16[512,4096]{1,0:T(8,128)(2,1)} %collective-permute-done.4.x.b2.two), custom_call_target="tpu_custom_call" | custom-call | flops 10000000000 | bytes 20000000 | tf_op jit(solution)/shard_map/flip/pallas_call | solution.py:377
  203.9 1.0 copy-done.21
  204.9 9.4 %outer_in.1 = bf16[2,16,64,1024]{3,2,1,0:T(8,128)(2,1)} custom-call(s32[2]{0:T(128)} %pad_add_fusion.core, bf16[2048,512]{1,0:T(8,128)(2,1)} %get-tuple-element.83.a_t, bf16[2048,512]{1,0:T(8,128)(2,1)} %get-tuple-element.84.a2_t, bf16[512,1024]{1,0:T(8,128)(2,1)} %get-tuple-element.78.d_own.b, bf16[512,1024]{1,0:T(8,128)(2,1)} %copy-done.21), custom_call_target="tpu_custom_call" | custom-call | flops 1 | bytes 1 | tf_op jit(solution)/shard_map/outer_in/pallas_call | solution.py:377
  214.2 2.8 all-to-all-done.3
  217.0 7.9 %all-to-all-start.4 = ((bf16[32,64,1024]{2,1,0:T(8,128)(2,1)}), bf16[32,64,1024]{2,1,0:T(8,128)(2,1)}, u32[]{:S(2)}, u32[]{:S(2)}) async-start(bf16[32,64,1024]{2,1,0:T(8,128)(2,1)} %bitcast.33), calls=%async_computation.4 | async-start | bytes 8388608 | tf_op jit(solution)/shard_map/all_to_all | solution.py:594
  224.9 13.7 %give.1 = bf16[512,4096]{1,0:T(8,128)(2,1)} custom-call(s32[2]{0:T(128)} %pad_add_fusion.core, bf16[512,1024]{1,0:T(8,128)(2,1)} %get-tuple-element.69.hidden, bf16[512,1024]{1,0:T(8,128)(2,1)} %get-tuple-element.78.d_own.b, bf16[512,1024]{1,0:T(8,128)(2,1)} %get-tuple-element.79.d_oth, bf16[2,16,32,1024]{3,2,1,0:T(8,128)(2,1)} %bitcast.32, ...), custom_call_target="tpu_custom_call" | custom-call | flops 1 | bytes 1 | tf_op jit(solution)/shard_map/give/pallas_call | solution.py:377
  238.6 2.5 sum_rows.2
  241.1 0.7 copy-done.18
  241.8 2.7 collective-permute-start.6
  244.5 2.1 collective-permute-start.7
  246.6 33.8 %collective-permute-done.6.refs_1_ = bf16[2,32,1024]{2,1,0:T(8,128)(2,1)} collective-permute-done((bf16[2,32,1024]{2,1,0:T(8,128)(2,1)S(1)}, bf16[2,32,1024]{2,1,0:T(8,128)(2,1)}, u32[]{:S(2)}, u32[]{:S(2)}) %collective-permute-start.6) | collective-permute-done | bytes 131104 | tf_op jit(solution)/shard_map/ppermute | solution.py:566
  280.5 4.2 %sum_rows.3 = (bf16[4,64,1024]{2,1,0:T(8,128)(2,1)S(1)}, bf16[4,64,1024]{2,1,0:T(8,128)(2,1)S(1)}, bf16[2,64,1024]{2,1,0:T(8,128)(2,1)S(1)}, bf16[2,64,1024]{2,1,0:T(8,128)(2,1)S(1)}) custom-call(s32[32]{0:T(128)S(1)} %select_reduce_fusion.index, bf16[32,64,1024]{2,1,0:T(8,128)(2,1)} %bitcast.17.rows), custom_call_target="tpu_custom_call" | custom-call | flops 10000000000 | bytes 20000000 | tf_op jit(solution)/shard_map/sum_rows/pallas_call | solution.py:312
  284.7 0.8 copy-done.16
  285.5 4.4 %collective-permute-start.9 = (bf16[2,64,1024]{2,1,0:T(8,128)(2,1)S(1)}, bf16[2,64,1024]{2,1,0:T(8,128)(2,1)S(1)}, u32[]{:S(2)}, u32[]{:S(2)}) collective-permute-start(bf16[2,64,1024]{2,1,0:T(8,128)(2,1)S(1)} %get-tuple-element.88), channel_id=1, source_target_pairs={{0,64},{64,0},{1,65},{65,1},{2,66},{66,2},{3,67},{67,3},{4,68},{68... | collective-permute-start | bytes 786440 | tf_op jit(solution)/shard_map/ppermute | solution.py:566
  289.9 3.4 collective-permute-start.10
  293.3 0.3 collective-permute-done.9.refs_1_
  293.7 3.4 collective-permute-done.10.refs_2_
  297.1 0.7 copy-done.14
  297.8 11.4 %all-to-all-start.5 = ((bf16[64,8,4096]{2,1,0:T(8,128)(2,1)}), bf16[64,8,4096]{2,1,0:T(8,128)(2,1)}, u32[]{:S(2)}, u32[]{:S(2)}) async-start(bf16[64,8,4096]{2,1,0:T(8,128)(2,1)} %bitcast.34), calls=%async_computation.5 | async-start | bytes 8388608 | tf_op jit(solution)/shard_map/all_to_all | solution.py:598
  309.2 2.0 collective-permute-start.14
  311.3 0.4 collective-permute-start.16
  312.0 0.1 collective-permute-start.11
  312.1 0.4 collective-permute-start.12
  312.6 0.4 collective-permute-done.15.refs_4_
  312.9 0.4 collective-permute-start.13
  313.3 1.2 copy-done.11
  314.6 0.9 copy-done.19
  315.5 4.8 %adam.3 = (f32[4,32,2048]{2,1,0:T(8,128)}, f32[4,32,2048]{2,1,0:T(8,128)}, f32[4,32,2048]{2,1,0:T(8,128)}) custom-call(s32[5]{0:T(128)S(1)} %pad_add_fusion.1.sel, f32[4,32,2048]{2,1,0:T(8,128)S(1)} %copy-done.3, f32[4,32,2048]{2,1,0:T(8,128)S(1)} %copy-done.10, f32[4,32,2048]{2,1,0:T(8,128)S(1)} %copy-done.11, bf16[4,32,1024]{2,1,0:T(8,128)(2,1)S(1)} %copy-done.19, ...), custom_call_target="tpu_custom_call" | custom-call | flops 10000000000 | bytes 20000000 | tf_op jit(solution)/shard_map/adam/pallas_call | solution.py:350
  320.3 6.9 %adam.2 = (f32[4,64,2048]{2,1,0:T(8,128)}, f32[4,64,2048]{2,1,0:T(8,128)}, f32[4,64,2048]{2,1,0:T(8,128)}) custom-call(s32[5]{0:T(128)S(1)} %pad_add_fusion.1.sel, f32[4,64,2048]{2,1,0:T(8,128)S(1)} %copy-done.2, f32[4,64,2048]{2,1,0:T(8,128)} %moment.2, f32[4,64,2048]{2,1,0:T(8,128)} %square.2, bf16[4,64,1024]{2,1,0:T(8,128)(2,1)S(1)} %copy-done.17, ...), custom_call_target="tpu_custom_call" | custom-call | flops 10000000000 | bytes 20000000 | tf_op jit(solution)/shard_map/adam/pallas_call | solution.py:350
  327.2 31.3 %all-to-all-done.5 = bf16[64,8,4096]{2,1,0:T(8,128)(2,1)} async-done(((bf16[64,8,4096]{2,1,0:T(8,128)(2,1)}), bf16[64,8,4096]{2,1,0:T(8,128)(2,1)}, u32[]{:S(2)}, u32[]{:S(2)}) %all-to-all-start.5) | async-done | bytes 4194336 | tf_op jit(solution)/shard_map/all_to_all | solution.py:598
  358.5 4.8 %combine.1 = (bf16[128,2048]{1,0:T(8,128)(2,1)}, bf16[128,2048]{1,0:T(8,128)(2,1)}, f32[128,2]{1,0:T(8,128)S(1)}) custom-call(f32[128,2]{1,0:T(8,128)S(1)} %get-tuple-element.64.dest, f32[128,2]{1,0:T(8,128)S(1)} %copy.26.weight, bf16[128,2048]{1,0:T(8,128)(2,1)S(1)} %copy-done.1, bf16[512,4096]{1,0:T(8,128)(2,1)} %bitcast.19.out.dx, ...), custom_call_target="tpu_custom_call" | custom-call | tf_op jit(solution)/shard_map/combine/pallas_call | solution.py:184
  363.3 0.6 copy.27
  (63 shorter events, 0.9 us)
Async XLA Ops:
  0.6 5.4 %copy-start.9 = (s32[128]{0:T(128)S(1)}, s32[128]{0:T(128)}, u32[]{:S(2)}) copy-start(s32[128]{0:T(128)} %param.14) | copy-start | bytes 1540
  0.7 12.3 %copy-start.7 = (s32[128,2]{0,1:T(2,128)S(1)}, s32[128,2]{0,1:T(2,128)}, u32[]{:S(2)}) copy-start(s32[128,2]{0,1:T(2,128)} %param.15) | copy-start | bytes 3076
  0.7 12.4 %copy-start.1 = (bf16[128,2048]{1,0:T(8,128)(2,1)S(1)}, bf16[128,2048]{1,0:T(8,128)(2,1)}, u32[]{:S(2)}) copy-start(bf16[128,2048]{1,0:T(8,128)(2,1)} %cot.3) | copy-start | bytes 1572868
  0.7 12.4 %copy-start.4 = (bf16[128,2048]{1,0:T(8,128)(2,1)S(1)}, bf16[128,2048]{1,0:T(8,128)(2,1)}, u32[]{:S(2)}) copy-start(bf16[128,2048]{1,0:T(8,128)(2,1)} %tok) | copy-start | bytes 1572868
  0.7 12.4 %copy-start.8 = (f32[128,2]{0,1:T(2,128)S(1)}, f32[128,2]{0,1:T(2,128)}, u32[]{:S(2)}) copy-start(f32[128,2]{0,1:T(2,128)} %param.13) | copy-start | bytes 3076
  4.6 3.6 collective-permute-start
  6.5 0.6 copy-start.5
  9.7 10.5 %collective-permute-start.1 = (bf16[2,96,1024]{2,1,0:T(8,128)(2,1)}, bf16[2,96,1024]{2,1,0:T(8,128)(2,1)S(1)}, u32[]{:S(2)}, u32[]{:S(2)}) collective-permute-start(bf16[2,96,1024]{2,1,0:T(8,128)(2,1)} %get-tuple-element.61), channel_id=1, source_target_pairs={{0,64},{64,0},{1,65},{65,1},{2,66},{66,2},{3,67},{67,3},{4,68},{68... | collective-permute-start | bytes 1179656 | tf_op jit(solution)/shard_map/ppermute | solution.py:566
  11.0 11.4 %collective-permute-start.2 = (bf16[2,96,1024]{2,1,0:T(8,128)(2,1)}, bf16[2,96,1024]{2,1,0:T(8,128)(2,1)S(1)}, u32[]{:S(2)}, u32[]{:S(2)}) collective-permute-start(bf16[2,96,1024]{2,1,0:T(8,128)(2,1)} %get-tuple-element.62), channel_id=1, source_target_pairs={{0,65},{65,0},{1,64},{64,1},{2,67},{67,2},{3,66},{66,3},{4,69},{69... | collective-permute-start | bytes 1179656 | tf_op jit(solution)/shard_map/ppermute | solution.py:570
  13.1 0.8 copy-start.6
  15.6 2.0 copy-start
  22.5 10.5 %copy-start.22 = (s32[16]{0:T(128)S(1)}, s32[16]{0:T(128)}, u32[]{:S(2)}) copy-start(s32[16]{0:T(128)} %get-tuple-element.125) | copy-start | bytes 196
  22.5 10.5 %copy-start.23 = (s32[1,16]{1,0:T(1,128)S(1)}, s32[1,16]{1,0:T(1,128)}, u32[]{:S(2)}) copy-start(s32[1,16]{1,0:T(1,128)} %get-tuple-element.126) | copy-start | bytes 196
  22.5 60.0 %all-to-all-start = ((bf16[64,8,4096]{2,1,0:T(8,128)(2,1)}), bf16[64,8,4096]{2,1,0:T(8,128)(2,1)}, u32[]{:S(2)}, u32[]{:S(2)}) async-start(bf16[64,8,4096]{2,1,0:T(8,128)(2,1)} %bitcast.25), calls=%async_computation | async-start | bytes 8388608 | tf_op jit(solution)/shard_map/all_to_all | solution.py:598
  141.9 10.3 %collective-permute-start.3 = (bf16[2,16,64,1024]{3,2,1,0:T(8,128)(2,1)}, bf16[2,16,64,1024]{3,2,1,0:T(8,128)(2,1)}, u32[]{:S(2)}, u32[]{:S(2)}) collective-permute-start(bf16[2,16,64,1024]{3,2,1,0:T(8,128)(2,1)} %bitcast.10.own.own_in), channel_id=1, source_target_pairs={{0,32},{32,0},{1,33},{33,1},{2,34},{34,2},{3,35},{35,3},{4,36},{36... | collective-permute-start | bytes 12582920 | tf_op jit(solution)/shard_map/ppermute | solution.py:562
  145.1 17.6 %collective-permute-start.4 = (bf16[512,4096]{1,0:T(8,128)(2,1)}, bf16[512,4096]{1,0:T(8,128)(2,1)}, u32[]{:S(2)}, u32[]{:S(2)}) collective-permute-start(bf16[512,4096]{1,0:T(8,128)(2,1)} %bitcast.9.x.b.dy_own.dy_oth.one), channel_id=1, source_target_pairs={{0,32},{32,0},{1,33},{33,1},{2,34},{34,2},{3,35},{35,3},{4,36},{36... | collective-permute-start | bytes 12582920 | tf_op jit(solution)/shard_map/ppermute | solution.py:562
  145.1 33.8 %all-to-all-start.2 = ((bf16[32,32,1024]{2,1,0:T(8,128)(2,1)}), bf16[32,32,1024]{2,1,0:T(8,128)(2,1)S(1)}, u32[]{:S(2)}, u32[]{:S(2)}) async-start(bf16[32,32,1024]{2,1,0:T(8,128)(2,1)} %select_rows.3), calls=%async_computation.2 | async-start | bytes 4194304 | tf_op jit(solution)/shard_map/all_to_all | solution.py:594
  178.9 1.6 copy-start.20
  178.9 10.2 %collective-permute-start.5 = (bf16[2,16,32,1024]{3,2,1,0:T(8,128)(2,1)S(1)}, bf16[2,16,32,1024]{3,2,1,0:T(8,128)(2,1)}, u32[]{:S(2)}, u32[]{:S(2)}) collective-permute-start(bf16[2,16,32,1024]{3,2,1,0:T(8,128)(2,1)S(1)} %bitcast.30), channel_id=1, source_target_pairs={{0,32},{32,0},{1,33},{33,1},{2,34},{34,2},{3,35},{35,3},{4,36},{36... | collective-permute-start | bytes 6291464 | tf_op jit(solution)/shard_map/ppermute | solution.py:562
  180.5 36.5 %all-to-all-start.3 = ((bf16[32,32,1024]{2,1,0:T(8,128)(2,1)}), bf16[32,32,1024]{2,1,0:T(8,128)(2,1)}, u32[]{:S(2)}, u32[]{:S(2)}) async-start(bf16[32,32,1024]{2,1,0:T(8,128)(2,1)} %bitcast.35), calls=%async_computation.3 | async-start | bytes 4194304 | tf_op jit(solution)/shard_map/all_to_all | solution.py:594
  197.0 6.9 %collective-permute-start.8 = (bf16[512,1024]{1,0:T(8,128)(2,1)}, bf16[512,1024]{1,0:T(8,128)(2,1)S(1)}, u32[]{:S(2)}, u32[]{:S(2)}) collective-permute-start(bf16[512,1024]{1,0:T(8,128)(2,1)} %get-tuple-element.79.d_oth), channel_id=1, source_target_pairs={{0,32},{32,0},{1,33},{33,1},{2,34},{34,2},{3,35},{35,3},{4,36},{36... | collective-permute-start | bytes 3145736 | tf_op jit(solution)/shard_map/ppermute | solution.py:562
  203.9 1.0 copy-start.21
  217.0 63.4 %all-to-all-start.4 = ((bf16[32,64,1024]{2,1,0:T(8,128)(2,1)}), bf16[32,64,1024]{2,1,0:T(8,128)(2,1)}, u32[]{:S(2)}, u32[]{:S(2)}) async-start(bf16[32,64,1024]{2,1,0:T(8,128)(2,1)} %bitcast.33), calls=%async_computation.4 | async-start | bytes 8388608 | tf_op jit(solution)/shard_map/all_to_all | solution.py:594
  241.1 0.7 copy-start.18
  241.8 38.6 %collective-permute-start.6 = (bf16[2,32,1024]{2,1,0:T(8,128)(2,1)S(1)}, bf16[2,32,1024]{2,1,0:T(8,128)(2,1)}, u32[]{:S(2)}, u32[]{:S(2)}) collective-permute-start(bf16[2,32,1024]{2,1,0:T(8,128)(2,1)S(1)} %get-tuple-element.81), channel_id=1, source_target_pairs={{0,64},{64,0},{1,65},{65,1},{2,66},{66,2},{3,67},{67,3},{4,68},{68... | collective-permute-start | bytes 393224 | tf_op jit(solution)/shard_map/ppermute | solution.py:566
  244.5 35.9 %collective-permute-start.7 = (bf16[2,32,1024]{2,1,0:T(8,128)(2,1)S(1)}, bf16[2,32,1024]{2,1,0:T(8,128)(2,1)}, u32[]{:S(2)}, u32[]{:S(2)}) collective-permute-start(bf16[2,32,1024]{2,1,0:T(8,128)(2,1)S(1)} %get-tuple-element.82), channel_id=1, source_target_pairs={{0,65},{65,0},{1,64},{64,1},{2,67},{67,2},{3,66},{66,3},{4,69},{69... | collective-permute-start | bytes 393224 | tf_op jit(solution)/shard_map/ppermute | solution.py:570
  284.7 0.8 copy-start.16
  285.5 8.2 %collective-permute-start.9 = (bf16[2,64,1024]{2,1,0:T(8,128)(2,1)S(1)}, bf16[2,64,1024]{2,1,0:T(8,128)(2,1)S(1)}, u32[]{:S(2)}, u32[]{:S(2)}) collective-permute-start(bf16[2,64,1024]{2,1,0:T(8,128)(2,1)S(1)} %get-tuple-element.88), channel_id=1, source_target_pairs={{0,64},{64,0},{1,65},{65,1},{2,66},{66,2},{3,67},{67,3},{4,68},{68... | collective-permute-start | bytes 786440 | tf_op jit(solution)/shard_map/ppermute | solution.py:566
  289.9 7.2 %collective-permute-start.10 = (bf16[2,64,1024]{2,1,0:T(8,128)(2,1)S(1)}, bf16[2,64,1024]{2,1,0:T(8,128)(2,1)S(1)}, u32[]{:S(2)}, u32[]{:S(2)}) collective-permute-start(bf16[2,64,1024]{2,1,0:T(8,128)(2,1)S(1)} %get-tuple-element.89), channel_id=1, source_target_pairs={{0,65},{65,0},{1,64},{64,1},{2,67},{67,2},{3,66},{66,3},{4,69},{69... | collective-permute-start | bytes 786440 | tf_op jit(solution)/shard_map/ppermute | solution.py:570
  293.7 3.4 copy-start.12
  297.1 0.7 copy-start.14
  297.8 14.0 %copy-start.24 = (s32[1,16]{1,0:T(1,128)S(1)}, s32[1,16]{1,0:T(1,128)}, u32[]{:S(2)}) copy-start(s32[1,16]{1,0:T(1,128)} %get-tuple-element.123) | copy-start | bytes 196
  297.8 15.5 %copy-start.3 = (f32[4,32,2048]{2,1,0:T(8,128)S(1)}, f32[4,32,2048]{2,1,0:T(8,128)}, u32[]{:S(2)}) copy-start(f32[4,32,2048]{2,1,0:T(8,128)} %weight.4) | copy-start | bytes 3145732
  297.8 15.5 %copy-start.10 = (f32[4,32,2048]{2,1,0:T(8,128)S(1)}, f32[4,32,2048]{2,1,0:T(8,128)}, u32[]{:S(2)}) copy-start(f32[4,32,2048]{2,1,0:T(8,128)} %moment.3) | copy-start | bytes 3145732
  297.8 60.7 %all-to-all-start.5 = ((bf16[64,8,4096]{2,1,0:T(8,128)(2,1)}), bf16[64,8,4096]{2,1,0:T(8,128)(2,1)}, u32[]{:S(2)}, u32[]{:S(2)}) async-start(bf16[64,8,4096]{2,1,0:T(8,128)(2,1)} %bitcast.34), calls=%async_computation.5 | async-start | bytes 8388608 | tf_op jit(solution)/shard_map/all_to_all | solution.py:598
  309.2 4.1 %collective-permute-start.14 = (bf16[4,32,1024]{2,1,0:T(8,128)(2,1)S(1)}, bf16[4,32,1024]{2,1,0:T(8,128)(2,1)}, u32[]{:S(2)}, u32[]{:S(2)}) collective-permute-start(bf16[4,32,1024]{2,1,0:T(8,128)(2,1)S(1)} %get-tuple-element.99), channel_id=1, source_target_pairs={{0,32},{32,0},{1,33},{33,1},{2,34},{34,2},{3,35},{35,3},{4,36},{36... | collective-permute-start | bytes 786440 | tf_op jit(solution)/shard_map/ppermute | solution.py:562
  311.2 1.7 collective-permute-start.15
  311.3 2.0 collective-permute-start.16
  312.0 8.3 %copy-start.2 = (f32[4,64,2048]{2,1,0:T(8,128)S(1)}, f32[4,64,2048]{2,1,0:T(8,128)}, u32[]{:S(2)}) copy-start(f32[4,64,2048]{2,1,0:T(8,128)} %weight.3) | copy-start | bytes 6291460
  312.0 8.3 %collective-permute-start.11 = (bf16[4,64,1024]{2,1,0:T(8,128)(2,1)S(1)}, bf16[4,64,1024]{2,1,0:T(8,128)(2,1)S(1)}, u32[]{:S(2)}, u32[]{:S(2)}) collective-permute-start(bf16[4,64,1024]{2,1,0:T(8,128)(2,1)S(1)} %get-tuple-element.95), channel_id=1, source_target_pairs={{0,32},{32,0},{1,33},{33,1},{2,34},{34,2},{3,35},{35,3},{4,36},{36... | collective-permute-start | bytes 1572872 | tf_op jit(solution)/shard_map/ppermute | solution.py:562
  312.1 8.1 %collective-permute-start.12 = (bf16[2,64,1024]{2,1,0:T(8,128)(2,1)}, bf16[2,64,1024]{2,1,0:T(8,128)(2,1)S(1)}, u32[]{:S(2)}, u32[]{:S(2)}) collective-permute-start(bf16[2,64,1024]{2,1,0:T(8,128)(2,1)} %copy-done.12), channel_id=1, source_target_pairs={{0,32},{32,0},{1,33},{33,1},{2,34},{34,2},{3,35},{35,3},{4,36},{36... | collective-permute-start | bytes 786440 | tf_op jit(solution)/shard_map/ppermute | solution.py:562
  312.9 7.3 %collective-permute-start.13 = (bf16[2,64,1024]{2,1,0:T(8,128)(2,1)}, bf16[2,64,1024]{2,1,0:T(8,128)(2,1)S(1)}, u32[]{:S(2)}, u32[]{:S(2)}) collective-permute-start(bf16[2,64,1024]{2,1,0:T(8,128)(2,1)} %copy-done.14), channel_id=1, source_target_pairs={{0,32},{32,0},{1,33},{33,1},{2,34},{34,2},{3,35},{35,3},{4,36},{36... | collective-permute-start | bytes 786440 | tf_op jit(solution)/shard_map/ppermute | solution.py:562
  313.3 1.2 copy-start.11
  314.6 0.9 copy-start.19
  315.5 4.8 %copy-start.13 = (bf16[2,64,1024]{2,1,0:T(8,128)(2,1)S(1)}, bf16[2,64,1024]{2,1,0:T(8,128)(2,1)}, u32[]{:S(2)}) copy-start(bf16[2,64,1024]{2,1,0:T(8,128)(2,1)} %copy-done.12) | copy-start | bytes 786436
  315.5 4.8 %copy-start.15 = (bf16[2,64,1024]{2,1,0:T(8,128)(2,1)S(1)}, bf16[2,64,1024]{2,1,0:T(8,128)(2,1)}, u32[]{:S(2)}) copy-start(bf16[2,64,1024]{2,1,0:T(8,128)(2,1)} %copy-done.14) | copy-start | bytes 786436
  315.5 4.8 %copy-start.17 = (bf16[4,64,1024]{2,1,0:T(8,128)(2,1)S(1)}, bf16[4,64,1024]{2,1,0:T(8,128)(2,1)}, u32[]{:S(2)}) copy-start(bf16[4,64,1024]{2,1,0:T(8,128)(2,1)} %copy-done.16) | copy-start | bytes 1572868

commit v5 on v4

--- a/solution.py
+++ b/solution.py
@@ -157,49 +157,56 @@
     )(targets, targets.T, slot_rows, slot_cols, route_weight.T, tokens, cotangent)
 
 
-def combine_kernel(dest, weight, cot, out, dx, mixed, grad, mix):
-    step = pl.program_id(0)
+def picks(dest):
     place = lax.broadcasted_iota(jnp.int32, (128, ROWS), 1).astype(F32)
-    first, second = place == dest[:, 0:1], place == dest[:, 1:2]
+    return place == dest[:, 0:1], place == dest[:, 1:2]
+
+
+def mix_kernel(dest, weight, cot, out, mixed, mix):
+    first, second = picks(dest)
     pick0 = jnp.where(first, 1.0, 0.0).astype(BF)
     pick1 = jnp.where(second, 1.0, 0.0).astype(BF)
-    both = jnp.where(first | second, 1.0, 0.0).astype(BF)
-    out0, out1 = dot(pick0, out[...]), dot(pick1, out[...])
-    here = cot[...].astype(F32)
-    mixed[...] = (weight[:, 0:1] * out0 + weight[:, 1:2] * out1).astype(BF)
-    grad[...] = dot(both, dx[...]).astype(BF)
-
-    @pl.when(step == 0)
-    def _():
-        mix[...] = jnp.zeros_like(mix)
-
-    mix[:, 0:1] += jnp.sum(here * out0, axis=1, keepdims=True)
-    mix[:, 1:2] += jnp.sum(here * out1, axis=1, keepdims=True)
-
-
-def combine(dest, route_weight, cotangent, back):
-    width = 512
-    whole = pl.BlockSpec((128, 2), lambda j: (0, 0))
-    tile = pl.BlockSpec((128, width), lambda j: (0, j))
-    return pl.pallas_call(
-        combine_kernel,
-        grid=(D // width,),
-        in_specs=[
-            whole,
-            whole,
-            tile,
-            pl.BlockSpec((ROWS, width), lambda j: (0, j)),
-            pl.BlockSpec((ROWS, width), lambda j: (0, D // width + j)),
-        ],
-        out_specs=[tile, tile, whole],
+    w0, w1 = weight[:, 0:1], weight[:, 1:2]
+    mix0 = jnp.zeros((128, 1), F32)
+    mix1 = jnp.zeros((128, 1), F32)
+    for c in range(0, D, 512):
+        cols = slice(c, c + 512)
+        out0, out1 = dot(pick0, out[:, cols]), dot(pick1, out[:, cols])
+        here = cot[:, cols].astype(F32)
+        mixed[:, cols] = (w0 * out0 + w1 * out1).astype(BF)
+        mix0 += jnp.sum(here * out0, axis=1, keepdims=True)
+        mix1 += jnp.sum(here * out1, axis=1, keepdims=True)
+    mix[:, 0:1] = mix0
+    mix[:, 1:2] = mix1
+
+
+def mix_results(dest, route_weight, cotangent, back):
+    return pl.pallas_call(
+        mix_kernel,
         out_shape=(
             jax.ShapeDtypeStruct((128, D), BF),
-            jax.ShapeDtypeStruct((128, D), BF),
             jax.ShapeDtypeStruct((128, 2), F32),
         ),
         compiler_params=params(),
-        name="combine",
-    )(dest, route_weight, cotangent, back, back)
+        cost_estimate=LONG,
+        name="mix_results",
+    )(dest, route_weight, cotangent, back)
+
+
+def add_kernel(dest, dx, grad):
+    first, second = picks(dest)
+    both = jnp.where(first | second, 1.0, 0.0).astype(BF)
+    for c in range(0, D, 512):
+        grad[:, c : c + 512] = dot(both, dx[:, c : c + 512]).astype(BF)
+
+
+def add_gradients(dest, back):
+    return pl.pallas_call(
+        add_kernel,
+        out_shape=jax.ShapeDtypeStruct((128, D), BF),
+        compiler_params=params(),
+        name="add_gradients",
+    )(dest, back)
 
 
 def prepare_kernel(core, w_in, w_out, mine, theirs):
@@ -511,38 +518,51 @@
     )
 
 
-def give_kernel(core, hidden, d_own, d_oth, own_out, oth_out, own_in, oth_in, out):
+def result_kernel(core, hidden, own, oth, out):
     step = pl.program_id(0)
 
     @pl.when(step == 0)
     def _():
-        out[...] = dot(hidden[...], rows_of(own_out, core[1])).astype(BF)
+        out[...] = dot(hidden[...], rows_of(own, core[1])).astype(BF)
 
     @pl.when(step == 1)
     def _():
-        out[...] = dot(hidden[...], rows_of(oth_out, core[1])).astype(BF)
-
-    @pl.when(step >= 2)
-    def _():
-        dx = dot_nt(d_own[...], rows_of(own_in, core[1])) + dot_nt(d_oth[...], rows_of(oth_in, core[1]))
-        out[...] = dx.astype(BF)
-
-
-def give_of(core, hidden, d_own, d_oth, own_out, oth_out, own_in, oth_in):
+        out[...] = dot(hidden[...], rows_of(oth, core[1])).astype(BF)
+
+
+def result_of(core, hidden, own, oth):
+    w = pl.BlockSpec((2, 16, 32, HALF), lambda j, s: (0, 0, 0, 0))
+    return call(
+        result_kernel,
+        core,
+        (hidden, own, oth),
+        [pl.BlockSpec((ROWS, FF), lambda j, s: (0, 0)), w, w],
+        jax.ShapeDtypeStruct((ROWS, D), BF),
+        pl.BlockSpec((ROWS, HALF), lambda j, s: (0, jnp.where(j == 0, s[0], 1 - s[0]))),
+        2,
+        "result",
+        LONG,
+    )
+
+
+def dx_kernel(core, d_own, d_oth, own, oth, out):
+    dx = dot_nt(d_own[...], rows_of(own, core[1])) + dot_nt(d_oth[...], rows_of(oth, core[1]))
+    out[...] = dx.astype(BF)
+
+
+def dx_of(core, d_own, d_oth, own, oth):
     row = pl.BlockSpec((ROWS, FF), lambda j, s: (0, 0))
-    w_out = pl.BlockSpec((2, 16, 32, HALF), lambda j, s: (0, 0, 0, 0))
-    w_in = pl.BlockSpec((2, 8, 64, HALF), lambda j, s: (0, jnp.maximum(j - 2, 0), 0, 0))
+    w = pl.BlockSpec((2, 4, 64, HALF), lambda j, s: (0, j, 0, 0))
     return call(
-        give_kernel,
+        dx_kernel,
         core,
-        (hidden, d_own, d_oth, own_out, oth_out, own_in, oth_in),
-        [row, row, row, w_out, w_out, w_in, w_in],
-        jax.ShapeDtypeStruct((ROWS, 2 * D), BF),
-        pl.BlockSpec(
-            (ROWS, HALF), lambda j, s: (0, jnp.where(j == 0, s[0], jnp.where(j == 1, 1 - s[0], j)))
-        ),
+        (d_own, d_oth, own, oth),
+        [row, row, w, w],
+        jax.ShapeDtypeStruct((ROWS, D), BF),
+        pl.BlockSpec((ROWS, 512), lambda j, s: (0, j)),
         4,
-        "give",
+        "dx",
+        LONG,
     )
 
 
@@ -552,10 +572,6 @@
 
 def dot_nt(a, b):
     return lax.dot_general(a, b, (((1,), (1,)), ((), ())), preferred_element_type=F32)
-
-
-def dot_tn(a, b):
-    return lax.dot_general(a, b, (((0,), (0,)), ((), ())), preferred_element_type=F32)
 
 
 def over_core(v):
@@ -596,8 +612,8 @@
 
     def exchange(v):
         return lax.all_to_all(
-            v.reshape(CHIPS, UNITS, 2 * D), CHIP_AXES, split_axis=0, concat_axis=0, tiled=True
-        ).reshape(ROWS, 2 * D)
+            v.reshape(CHIPS, UNITS, -1), CHIP_AXES, split_axis=0, concat_axis=0, tiled=True
+        ).reshape(v.shape)
 
     plan, slot_rows, slot_cols = make_plan(slot_expert)
 
@@ -651,13 +667,18 @@
         own, other = (near, pair, cross), (over_core(near_other), over_core(pair), over_core(cross))
         return own, other
 
-    result = give_of(which, hidden, d_own, d_oth, own_out, oth_out, own_in, oth_in)
-    own, other = gather_sums(after(rows_out, result))
+    result = result_of(which, hidden, own_out, oth_out)
+    rows_dx = dx_of(which, d_own, d_oth, own_in, oth_in)
+    own, other = gather_sums(after(rows_out, result, rows_dx))
     trained_out, mean_out, square_out = adam(sel, proj_out, first_out, second_out, own, other)
-    own2, other2 = gather_sums(after(rows_in, result, *own))
-    back = exchange(after(result, *own[1:], *own2[1:]))
+    rows_in = after(rows_in, result, rows_dx, *own)
+    back = exchange(after(result, rows_in))
+    own2, other2 = gather_sums(rows_in)
+    mixed, mix_grad = mix_results(dest, route_weight, cotangent, back)
+    back_dx = exchange(after(rows_dx, back))
+    own2 = (after(own2[0], back), *own2[1:])
     trained_in, mean_in, square_in = adam(sel, proj_in, first_in, second_in, own2, other2)
-    mixed, token_grad, mix_grad = combine(dest, route_weight, cotangent, back)
+    token_grad = add_gradients(dest, back_dx)
     return (
         mixed,
         token_grad,

time: 369 us -> 363 us (0.984)
  waiting for transfers between devices: 121 us -> 106 us
  starting transfers between devices: 70 us -> 75.2 us
    all_to_all x2 -> x3, waiting for transfers between devices: 74.1 us -> 63.1 us  [exchange(): lax.all_to_all(v.reshape(CHIPS, UNITS, -1), CHIP_AXES, split_axis=0, conc...]
    all_to_all x2 -> x3, starting transfers between devices: 22 us -> 32 us  [exchange(): lax.all_to_all(v.reshape(CHIPS, UNITS, -1), CHIP_AXES, split_axis=0, conc...]
    ppermute x3, waiting for transfers between devices: 36.8 us -> 29.4 us  [over_pair(): return lax.ppermute(v, 'yl', [(0, 1), (1, 0)])]
    unnamed x53 -> x49, local copies, waits for them, and re-layouts: 9.7 us -> 12.8 us
    pallas_call x7 -> x8, Pallas kernels: 63.2 us -> 65.7 us  [call(): pl.pallas_call(kernel, grid_spec=pltpu.PrefetchScalarGridSpec(num_scalar_...]
  transfers between devices with their start and end apart: 22 -> 23, of which waited for: 11 -> 11; matrix products, arithmetic and copies ran while one was open for 1% -> 1% of each run, Pallas kernels for 24% -> 26%
where the time goes in v5:
time: 363 us; the launch traced here: 359 us
  waiting for transfers between devices  106 us (29%)
  Pallas kernels  101 us (28%)
  starting transfers between devices  75.2 us (21%)
  blocking collectives  59.4 us (16%)
  local copies, waits for them, and re-layouts  13.6 us (4%)
    pallas_call x8, Pallas kernels, call(): pl.pallas_call(kernel, grid_spec=pltpu.PrefetchScalarGridSpec(num_scalar_...  65.7 us
    all_to_all x3, waiting for transfers between devices, exchange(): lax.all_to_all(v.reshape(CHIPS, UNITS, -1), CHIP_AXES, split_axis=0, conc...  63.1 us
    all_to_all x1, blocking collectives, spread(): lax.all_to_all(v.reshape(32, *v.shape[-2:]), SEND_AXES, split_axis=0, con...  59.4 us
    all_to_all x3, starting transfers between devices, exchange(): lax.all_to_all(v.reshape(CHIPS, UNITS, -1), CHIP_AXES, split_axis=0, conc...  32 us
    ppermute x3, waiting for transfers between devices, over_pair(): return lax.ppermute(v, 'yl', [(0, 1), (1, 0)])  29.4 us
    all_to_all x3, starting transfers between devices, spread(): lax.all_to_all(v.reshape(32, *v.shape[-2:]), SEND_AXES, split_axis=0, con...  19.8 us
    unnamed x49, local copies, waits for them, and re-layouts  12.8 us
    pallas_call x2, Pallas kernels, adam(): pl.pallas_call(adam_kernel, grid_spec=pltpu.PrefetchScalarGridSpec(num_sc...  11.9 us
  transfers between devices with their start and end apart: 23, of which 11 were waited for; matrix products, arithmetic and copies ran while one was open for 1% of the time, Pallas kernels for 26%

profile of v5, /device:TPU:1, one launch (start us, length us, event | category | flops | bytes accessed | tf_op | source)
XLA Modules:
  0.0 358.6 jit_solution(4576359648139945204)
XLA Ops:
  0.7 3.9 %prepare.1 = (bf16[4,96,1024]{2,1,0:T(8,128)(2,1)S(1)}, bf16[4,96,1024]{2,1,0:T(8,128)(2,1)}) custom-call(s32[1]{0:T(128)} %bitcast.5.core, f32[4,64,2048]{2,1,0:T(8,128)} %weight.3, f32[4,32,2048]{2,1,0:T(8,128)} %weight.4), custom_call_target="tpu_custom_call" | custom-call | tf_op jit(solution)/shard_map/prepare/pallas_call | solution.py:233
  4.6 1.4 collective-permute-start
  6.1 0.4 plan.1
  6.5 0.5 fusion.6
  7.2 1.0 collective-permute-done.theirs.refs_1_
  8.1 1.5 take_rows.1
  9.7 1.4 collective-permute-start.1
  11.0 1.9 collective-permute-start.2
  13.1 1.6 dispatch.1
  14.7 2.0 copy-done
  16.7 0.6 copy-done.8
  17.3 2.9 collective-permute-done.1.refs_2_
  20.2 2.3 collective-permute-done.2.refs_3_
  22.5 10.5 %all-to-all-start = ((bf16[64,8,4096]{2,1,0:T(8,128)(2,1)}), bf16[64,8,4096]{2,1,0:T(8,128)(2,1)}, u32[]{:S(2)}, u32[]{:S(2)}) async-start(bf16[64,8,4096]{2,1,0:T(8,128)(2,1)} %bitcast.28), calls=%async_computation | async-start | bytes 8388608 | tf_op jit(solution)/shard_map/all_to_all | solution.py:614
  33.1 2.9 select_rows.3
  36.1 3.6 select_rows.2
  39.6 42.8 %all-to-all-done = bf16[64,8,4096]{2,1,0:T(8,128)(2,1)} async-done(((bf16[64,8,4096]{2,1,0:T(8,128)(2,1)}), bf16[64,8,4096]{2,1,0:T(8,128)(2,1)}, u32[]{:S(2)}, u32[]{:S(2)}) %all-to-all-start) | async-done | bytes 4194336 | tf_op jit(solution)/shard_map/all_to_all | solution.py:614
  82.4 59.4 %all_to_all.35 = bf16[32,64,1024]{2,1,0:T(8,128)(2,1)} all-to-all(bf16[32,64,1024]{2,1,0:T(8,128)(2,1)} %select_rows.2), channel_id=1, replica_groups=mesh['yl'=2,'core'=2,'x'=4,'z'=4,'yh'=2] {'yh','x','z'}, dimensions={0} | all-to-all | bytes 8388608 | tf_op jit(solution)/shard_map/all_to_all | solution.py:610
  141.9 3.2 collective-permute-start.3
  145.1 4.9 %all-to-all-start.2 = ((bf16[32,32,1024]{2,1,0:T(8,128)(2,1)}), bf16[32,32,1024]{2,1,0:T(8,128)(2,1)}, u32[]{:S(2)}, u32[]{:S(2)}) async-start(bf16[32,32,1024]{2,1,0:T(8,128)(2,1)} %select_rows.3), calls=%async_computation.2 | async-start | bytes 4194304 | tf_op jit(solution)/shard_map/all_to_all | solution.py:610
  150.0 0.6 dynamic_slice.9
  151.2 0.6 pad_add_fusion.core
  151.8 0.4 collective-permute-done.3.oth
  152.2 10.5 %hidden.1 = (bf16[512,1024]{1,0:T(8,128)(2,1)}, bf16[1024,512]{1,0:T(8,128)(2,1)}, f32[512,1024]{1,0:T(8,128)}, f32[512,1024]{1,0:T(8,128)}) custom-call(s32[2]{0:T(128)} %pad_add_fusion.core, bf16[512,4096]{1,0:T(8,128)(2,1)} %bitcast.9.x.b.one.dy_own.dy_oth, bf16[2,16,64,1024]{3,2,1,0:T(8,128)(2,1)} %bitcast.10.own, ...), custom_call_target="tpu_custom_call" | custom-call | flops 1 | bytes 1 | tf_op jit(solution)/shard_map/hidden/pallas_call | solution.py:384
  162.7 9.5 %other_hidden.1.a2_t = bf16[1024,512]{1,0:T(8,128)(2,1)} custom-call(s32[2]{0:T(128)} %pad_add_fusion.core, bf16[512,4096]{1,0:T(8,128)(2,1)} %collective-permute-done.4.x.b2.two, bf16[2,16,64,1024]{3,2,1,0:T(8,128)(2,1)} %bitcast.10.own, bf16[2,16,64,1024]{3,2,1,0:T(8,128)(2,1)} %collective-permute-done.3.oth), custom_call_target="tpu_custom_call" | custom-call | flops 1 | bytes 1 | tf_op jit(solution)/shard_map/other_hidden/pallas_call | solution.py:384
  172.2 6.7 %outer_out.1 = bf16[2,16,32,1024]{3,2,1,0:T(8,128)(2,1)} custom-call(s32[2]{0:T(128)} %pad_add_fusion.core, bf16[1024,512]{1,0:T(8,128)(2,1)} %get-tuple-element.71.a_t, bf16[1024,512]{1,0:T(8,128)(2,1)} %other_hidden.1.a2_t, bf16[512,4096]{1,0:T(8,128)(2,1)} %bitcast.9.x.b.one.dy_own.dy_oth, bf16[512,4096]{1,0:T(8,128)(2,1)} %collective-permute-done.4.x.b2.two), custom_call_target="tpu_custom_call" | custom-call | flops 1 | bytes 1 | tf_op jit(solution)/shard_map/outer_out/pallas_call | solution.py:384
  179.0 1.6 collective-permute-start.5
  180.6 8.2 %all-to-all-start.3 = ((bf16[32,32,1024]{2,1,0:T(8,128)(2,1)}), bf16[32,32,1024]{2,1,0:T(8,128)(2,1)S(1)}, u32[]{:S(2)}, u32[]{:S(2)}) async-start(bf16[32,32,1024]{2,1,0:T(8,128)(2,1)} %bitcast.35), calls=%async_computation.3 | async-start | bytes 4194304 | tf_op jit(solution)/shard_map/all_to_all | solution.py:610
  188.8 7.9 %back.1 = (bf16[512,1024]{1,0:T(8,128)(2,1)}, bf16[512,1024]{1,0:T(8,128)(2,1)}) custom-call(s32[2]{0:T(128)} %pad_add_fusion.core, bf16[512,4096]{1,0:T(8,128)(2,1)} %bitcast.9.x.b.one.dy_own.dy_oth, bf16[512,4096]{1,0:T(8,128)(2,1)} %bitcast.9.x.b.one.dy_own.dy_oth, bf16[2,16,32,1024]{3,2,1,0:T(8,128)(2,1)} %bitcast.11.own, ...), custom_call_target="tpu_custom_call" | custom-call | flops 1 | bytes 1 | tf_op jit(solution)/shard_map/back/pallas_call | solution.py:384
  197.0 5.6 %flip.1 = (bf16[2048,512]{1,0:T(8,128)(2,1)}, bf16[2048,512]{1,0:T(8,128)(2,1)}) custom-call(s32[2]{0:T(128)} %pad_add_fusion.core, bf16[512,4096]{1,0:T(8,128)(2,1)} %bitcast.9.x.b.one.dy_own.dy_oth, bf16[512,4096]{1,0:T(8,128)(2,1)} %collective-permute-done.4.x.b2.two), custom_call_target="tpu_custom_call" | custom-call | flops 10000000000 | bytes 20000000 | tf_op jit(solution)/shard_map/flip/pallas_call | solution.py:384
  202.6 1.0 copy-done.19
  203.5 9.4 %outer_in.1 = bf16[2,16,64,1024]{3,2,1,0:T(8,128)(2,1)} custom-call(s32[2]{0:T(128)} %pad_add_fusion.core, bf16[2048,512]{1,0:T(8,128)(2,1)} %get-tuple-element.75.a_t, bf16[2048,512]{1,0:T(8,128)(2,1)} %get-tuple-element.76.a2_t, bf16[512,1024]{1,0:T(8,128)(2,1)} %get-tuple-element.81.b.d_own, bf16[512,1024]{1,0:T(8,128)(2,1)} %copy-done.19), custom_call_target="tpu_custom_call" | custom-call | flops 1 | bytes 1 | tf_op jit(solution)/shard_map/outer_in/pallas_call | solution.py:384
  212.9 5.2 %all-to-all-done.3 = bf16[32,32,1024]{2,1,0:T(8,128)(2,1)S(1)} async-done(((bf16[32,32,1024]{2,1,0:T(8,128)(2,1)}), bf16[32,32,1024]{2,1,0:T(8,128)(2,1)S(1)}, u32[]{:S(2)}, u32[]{:S(2)}) %all-to-all-start.3) | async-done | bytes 2097184 | tf_op jit(solution)/shard_map/all_to_all | solution.py:610
  218.1 6.7 %all-to-all-start.4 = ((bf16[32,64,1024]{2,1,0:T(8,128)(2,1)}), bf16[32,64,1024]{2,1,0:T(8,128)(2,1)}, u32[]{:S(2)}, u32[]{:S(2)}) async-start(bf16[32,64,1024]{2,1,0:T(8,128)(2,1)} %bitcast.34), calls=%async_computation.4 | async-start | bytes 8388608 | tf_op jit(solution)/shard_map/all_to_all | solution.py:610
  224.8 9.4 %dx.1 = bf16[512,2048]{1,0:T(8,128)(2,1)} custom-call(s32[2]{0:T(128)} %pad_add_fusion.core, bf16[512,1024]{1,0:T(8,128)(2,1)} %get-tuple-element.81.b.d_own, bf16[512,1024]{1,0:T(8,128)(2,1)} %get-tuple-element.82.d_oth, bf16[2,16,64,1024]{3,2,1,0:T(8,128)(2,1)} %bitcast.10.own, bf16[2,16,64,1024]{3,2,1,0:T(8,128)(2,1)} %collective-permute-done.3.oth), custom_call_target="tpu_custom_call" | custom-call | flops 10000000000 | bytes 20000000 | tf_op jit(solution)/shard_map/dx/pallas_call | solution.py:384
  234.2 6.8 %result.1 = bf16[512,2048]{1,0:T(8,128)(2,1)} custom-call(s32[2]{0:T(128)} %pad_add_fusion.core, bf16[512,1024]{1,0:T(8,128)(2,1)} %get-tuple-element.70.hidden, bf16[2,16,32,1024]{3,2,1,0:T(8,128)(2,1)} %bitcast.11.own, bf16[2,16,32,1024]{3,2,1,0:T(8,128)(2,1)} %collective-permute-done.5.oth), custom_call_target="tpu_custom_call" | custom-call | flops 10000000000 | bytes 20000000 | tf_op jit(solution)/shard_map/result/pallas_call | solution.py:384
  241.0 1.6 sum_rows.2
  242.6 3.5 collective-permute-start.7
  246.1 2.2 collective-permute-start.8
  248.3 26.5 %collective-permute-done.7.refs_1_ = bf16[2,32,1024]{2,1,0:T(8,128)(2,1)} collective-permute-done((bf16[2,32,1024]{2,1,0:T(8,128)(2,1)S(1)}, bf16[2,32,1024]{2,1,0:T(8,128)(2,1)}, u32[]{:S(2)}, u32[]{:S(2)}) %collective-permute-start.7) | collective-permute-done | bytes 131104 | tf_op jit(solution)/shard_map/ppermute | solution.py:582
  274.8 4.7 %collective-permute-done.8.refs_2_ = bf16[2,32,1024]{2,1,0:T(8,128)(2,1)} collective-permute-done((bf16[2,32,1024]{2,1,0:T(8,128)(2,1)S(1)}, bf16[2,32,1024]{2,1,0:T(8,128)(2,1)}, u32[]{:S(2)}, u32[]{:S(2)}) %collective-permute-start.8) | collective-permute-done | bytes 131104 | tf_op jit(solution)/shard_map/ppermute | solution.py:586
  279.5 15.3 %all-to-all-start.5 = ((bf16[64,8,2048]{2,1,0:T(8,128)(2,1)}), bf16[64,8,2048]{2,1,0:T(8,128)(2,1)S(1)}, u32[]{:S(2)}, u32[]{:S(2)}) async-start(bf16[64,8,2048]{2,1,0:T(8,128)(2,1)} %bitcast.37), calls=%async_computation.5 | async-start | bytes 4194304 | tf_op jit(solution)/shard_map/all_to_all | solution.py:614
  295.1 1.8 collective-permute-start.14
  296.9 0.4 collective-permute-start.16
  297.3 5.2 %sum_rows.3 = (bf16[4,64,1024]{2,1,0:T(8,128)(2,1)S(1)}, bf16[4,64,1024]{2,1,0:T(8,128)(2,1)}, bf16[2,64,1024]{2,1,0:T(8,128)(2,1)}, bf16[2,64,1024]{2,1,0:T(8,128)(2,1)}) custom-call(s32[32]{0:T(128)S(1)} %select_reduce_fusion.index, bf16[32,64,1024]{2,1,0:T(8,128)(2,1)} %bitcast.22.rows), custom_call_target="tpu_custom_call" | custom-call | flops 10000000000 | bytes 20000000 | tf_op jit(solution)/shard_map/sum_rows/pallas_call | solution.py:319
  302.5 0.8 copy-done.15
  303.3 1.4 collective-permute-start.9
  304.7 1.7 collective-permute-start.10
  306.4 16.3 %all-to-all-done.5 = bf16[64,8,2048]{2,1,0:T(8,128)(2,1)S(1)} async-done(((bf16[64,8,2048]{2,1,0:T(8,128)(2,1)}), bf16[64,8,2048]{2,1,0:T(8,128)(2,1)S(1)}, u32[]{:S(2)}, u32[]{:S(2)}) %all-to-all-start.5) | async-done | bytes 2097184 | tf_op jit(solution)/shard_map/all_to_all | solution.py:614
  322.6 1.3 copy-done.2
  324.0 6.3 %all-to-all-start.6 = ((bf16[64,8,2048]{2,1,0:T(8,128)(2,1)}), bf16[64,8,2048]{2,1,0:T(8,128)(2,1)S(1)}, u32[]{:S(2)}, u32[]{:S(2)}) async-start(bf16[64,8,2048]{2,1,0:T(8,128)(2,1)} %bitcast.36), calls=%async_computation.6 | async-start | bytes 4194304 | tf_op jit(solution)/shard_map/all_to_all | solution.py:614
  330.3 1.4 copy-done.13
  331.7 1.2 copy-done.14
  332.9 0.9 copy-done.18
  333.9 4.8 %adam.3 = (f32[4,32,2048]{2,1,0:T(8,128)}, f32[4,32,2048]{2,1,0:T(8,128)}, f32[4,32,2048]{2,1,0:T(8,128)}) custom-call(s32[5]{0:T(128)S(1)} %pad_add_fusion.1.sel, f32[4,32,2048]{2,1,0:T(8,128)S(1)} %copy-done.4, f32[4,32,2048]{2,1,0:T(8,128)S(1)} %copy-done.13, f32[4,32,2048]{2,1,0:T(8,128)S(1)} %copy-done.14, bf16[4,32,1024]{2,1,0:T(8,128)(2,1)S(1)} %copy-done.18, ...), custom_call_target="tpu_custom_call" | custom-call | flops 10000000000 | bytes 20000000 | tf_op jit(solution)/shard_map/adam/pallas_call | solution.py:357
  338.7 2.0 collective-permute-start.11
  340.8 0.4 collective-permute-start.13
  341.2 1.7 mix_results.1
  342.9 0.6 copy.27
  343.6 1.6 copy-done.1
  345.1 1.0 copy-done.16
  346.2 7.1 %adam.2 = (f32[4,64,2048]{2,1,0:T(8,128)}, f32[4,64,2048]{2,1,0:T(8,128)}, f32[4,64,2048]{2,1,0:T(8,128)}) custom-call(s32[5]{0:T(128)S(1)} %pad_add_fusion.1.sel, f32[4,64,2048]{2,1,0:T(8,128)S(1)} %copy-done.1, f32[4,64,2048]{2,1,0:T(8,128)} %moment.2, f32[4,64,2048]{2,1,0:T(8,128)} %square.2, bf16[4,64,1024]{2,1,0:T(8,128)(2,1)S(1)} %copy-done.16, ...), custom_call_target="tpu_custom_call" | custom-call | flops 10000000000 | bytes 20000000 | tf_op jit(solution)/shard_map/adam/pallas_call | solution.py:357
  353.3 4.0 %all-to-all-done.6 = bf16[64,8,2048]{2,1,0:T(8,128)(2,1)S(1)} async-done(((bf16[64,8,2048]{2,1,0:T(8,128)(2,1)}), bf16[64,8,2048]{2,1,0:T(8,128)(2,1)S(1)}, u32[]{:S(2)}, u32[]{:S(2)}) %all-to-all-start.6) | async-done | bytes 2097184 | tf_op jit(solution)/shard_map/all_to_all | solution.py:614
  357.3 1.3 add_gradients.1
  (63 shorter events, 1.4 us)
Async XLA Ops:
  0.6 5.4 %copy-start.12 = (s32[128]{0:T(128)S(1)}, s32[128]{0:T(128)}, u32[]{:S(2)}) copy-start(s32[128]{0:T(128)} %param.14) | copy-start | bytes 1540
  0.7 12.3 %copy-start.10 = (s32[128,2]{0,1:T(2,128)S(1)}, s32[128,2]{0,1:T(2,128)}, u32[]{:S(2)}) copy-start(s32[128,2]{0,1:T(2,128)} %param.15) | copy-start | bytes 3076
  0.7 12.4 %copy-start.5 = (bf16[128,2048]{1,0:T(8,128)(2,1)S(1)}, bf16[128,2048]{1,0:T(8,128)(2,1)}, u32[]{:S(2)}) copy-start(bf16[128,2048]{1,0:T(8,128)(2,1)} %tok) | copy-start | bytes 1572868
  0.7 12.4 %copy-start.6 = (bf16[128,2048]{1,0:T(8,128)(2,1)S(1)}, bf16[128,2048]{1,0:T(8,128)(2,1)}, u32[]{:S(2)}) copy-start(bf16[128,2048]{1,0:T(8,128)(2,1)} %cot.3) | copy-start | bytes 1572868
  0.7 12.4 %copy-start.11 = (f32[128,2]{0,1:T(2,128)S(1)}, f32[128,2]{0,1:T(2,128)}, u32[]{:S(2)}) copy-start(f32[128,2]{0,1:T(2,128)} %param.13) | copy-start | bytes 3076
  4.6 3.6 collective-permute-start
  9.7 10.5 %collective-permute-start.1 = (bf16[2,96,1024]{2,1,0:T(8,128)(2,1)}, bf16[2,96,1024]{2,1,0:T(8,128)(2,1)S(1)}, u32[]{:S(2)}, u32[]{:S(2)}) collective-permute-start(bf16[2,96,1024]{2,1,0:T(8,128)(2,1)} %get-tuple-element.62), channel_id=1, source_target_pairs={{0,64},{64,0},{1,65},{65,1},{2,66},{66,2},{3,67},{67,3},{4,68},{68... | collective-permute-start | bytes 1179656 | tf_op jit(solution)/shard_map/ppermute | solution.py:582
  11.0 11.4 %collective-permute-start.2 = (bf16[2,96,1024]{2,1,0:T(8,128)(2,1)}, bf16[2,96,1024]{2,1,0:T(8,128)(2,1)S(1)}, u32[]{:S(2)}, u32[]{:S(2)}) collective-permute-start(bf16[2,96,1024]{2,1,0:T(8,128)(2,1)} %get-tuple-element.63), channel_id=1, source_target_pairs={{0,65},{65,0},{1,64},{64,1},{2,67},{67,2},{3,66},{66,3},{4,69},{69... | collective-permute-start | bytes 1179656 | tf_op jit(solution)/shard_map/ppermute | solution.py:586
  14.7 2.0 copy-start
  16.7 0.6 copy-start.8
  22.5 10.5 %copy-start.20 = (s32[16]{0:T(128)S(1)}, s32[16]{0:T(128)}, u32[]{:S(2)}) copy-start(s32[16]{0:T(128)} %get-tuple-element.127) | copy-start | bytes 196
  22.5 10.6 %copy-start.21 = (s32[1,16]{1,0:T(1,128)S(1)}, s32[1,16]{1,0:T(1,128)}, u32[]{:S(2)}) copy-start(s32[1,16]{1,0:T(1,128)} %get-tuple-element.128) | copy-start | bytes 196
  22.5 60.0 %all-to-all-start = ((bf16[64,8,4096]{2,1,0:T(8,128)(2,1)}), bf16[64,8,4096]{2,1,0:T(8,128)(2,1)}, u32[]{:S(2)}, u32[]{:S(2)}) async-start(bf16[64,8,4096]{2,1,0:T(8,128)(2,1)} %bitcast.28), calls=%async_computation | async-start | bytes 8388608 | tf_op jit(solution)/shard_map/all_to_all | solution.py:614
  141.9 10.3 %collective-permute-start.3 = (bf16[2,16,64,1024]{3,2,1,0:T(8,128)(2,1)}, bf16[2,16,64,1024]{3,2,1,0:T(8,128)(2,1)}, u32[]{:S(2)}, u32[]{:S(2)}) collective-permute-start(bf16[2,16,64,1024]{3,2,1,0:T(8,128)(2,1)} %bitcast.10.own), channel_id=1, source_target_pairs={{0,32},{32,0},{1,33},{33,1},{2,34},{34,2},{3,35},{35,3},{4,36},{36... | collective-permute-start | bytes 12582920 | tf_op jit(solution)/shard_map/ppermute | solution.py:578
  145.1 17.7 %collective-permute-start.4 = (bf16[512,4096]{1,0:T(8,128)(2,1)}, bf16[512,4096]{1,0:T(8,128)(2,1)}, u32[]{:S(2)}, u32[]{:S(2)}) collective-permute-start(bf16[512,4096]{1,0:T(8,128)(2,1)} %bitcast.9.x.b.one.dy_own.dy_oth), channel_id=1, source_target_pairs={{0,32},{32,0},{1,33},{33,1},{2,34},{34,2},{3,35},{35,3},{4,36},{36... | collective-permute-start | bytes 12582920 | tf_op jit(solution)/shard_map/ppermute | solution.py:578
  145.1 33.9 %all-to-all-start.2 = ((bf16[32,32,1024]{2,1,0:T(8,128)(2,1)}), bf16[32,32,1024]{2,1,0:T(8,128)(2,1)}, u32[]{:S(2)}, u32[]{:S(2)}) async-start(bf16[32,32,1024]{2,1,0:T(8,128)(2,1)} %select_rows.3), calls=%async_computation.2 | async-start | bytes 4194304 | tf_op jit(solution)/shard_map/all_to_all | solution.py:610
  179.0 9.8 %collective-permute-start.5 = (bf16[2,16,32,1024]{3,2,1,0:T(8,128)(2,1)}, bf16[2,16,32,1024]{3,2,1,0:T(8,128)(2,1)}, u32[]{:S(2)}, u32[]{:S(2)}) collective-permute-start(bf16[2,16,32,1024]{3,2,1,0:T(8,128)(2,1)} %bitcast.11.own), channel_id=1, source_target_pairs={{0,32},{32,0},{1,33},{33,1},{2,34},{34,2},{3,35},{35,3},{4,36},{36... | collective-permute-start | bytes 6291464 | tf_op jit(solution)/shard_map/ppermute | solution.py:578
  180.6 37.5 %all-to-all-start.3 = ((bf16[32,32,1024]{2,1,0:T(8,128)(2,1)}), bf16[32,32,1024]{2,1,0:T(8,128)(2,1)S(1)}, u32[]{:S(2)}, u32[]{:S(2)}) async-start(bf16[32,32,1024]{2,1,0:T(8,128)(2,1)} %bitcast.35), calls=%async_computation.3 | async-start | bytes 4194304 | tf_op jit(solution)/shard_map/all_to_all | solution.py:610
  196.7 5.9 %collective-permute-start.6 = (bf16[512,1024]{1,0:T(8,128)(2,1)}, bf16[512,1024]{1,0:T(8,128)(2,1)S(1)}, u32[]{:S(2)}, u32[]{:S(2)}) collective-permute-start(bf16[512,1024]{1,0:T(8,128)(2,1)} %get-tuple-element.82.d_oth), channel_id=1, source_target_pairs={{0,32},{32,0},{1,33},{33,1},{2,34},{34,2},{3,35},{35,3},{4,36},{36... | collective-permute-start | bytes 3145736 | tf_op jit(solution)/shard_map/ppermute | solution.py:578
  202.6 1.0 copy-start.19
  218.1 61.4 %all-to-all-start.4 = ((bf16[32,64,1024]{2,1,0:T(8,128)(2,1)}), bf16[32,64,1024]{2,1,0:T(8,128)(2,1)}, u32[]{:S(2)}, u32[]{:S(2)}) async-start(bf16[32,64,1024]{2,1,0:T(8,128)(2,1)} %bitcast.34), calls=%async_computation.4 | async-start | bytes 8388608 | tf_op jit(solution)/shard_map/all_to_all | solution.py:610
  242.6 36.9 %copy-start.17 = (bf16[4,32,1024]{2,1,0:T(8,128)(2,1)}, bf16[4,32,1024]{2,1,0:T(8,128)(2,1)S(1)}, u32[]{:S(2)}) copy-start(bf16[4,32,1024]{2,1,0:T(8,128)(2,1)S(1)} %get-tuple-element.85.refs_0_) | copy-start | bytes 786436
  242.6 32.2 %collective-permute-start.7 = (bf16[2,32,1024]{2,1,0:T(8,128)(2,1)S(1)}, bf16[2,32,1024]{2,1,0:T(8,128)(2,1)}, u32[]{:S(2)}, u32[]{:S(2)}) collective-permute-start(bf16[2,32,1024]{2,1,0:T(8,128)(2,1)S(1)} %get-tuple-element.86), channel_id=1, source_target_pairs={{0,64},{64,0},{1,65},{65,1},{2,66},{66,2},{3,67},{67,3},{4,68},{68... | collective-permute-start | bytes 393224 | tf_op jit(solution)/shard_map/ppermute | solution.py:582
  246.1 33.4 %collective-permute-start.8 = (bf16[2,32,1024]{2,1,0:T(8,128)(2,1)S(1)}, bf16[2,32,1024]{2,1,0:T(8,128)(2,1)}, u32[]{:S(2)}, u32[]{:S(2)}) collective-permute-start(bf16[2,32,1024]{2,1,0:T(8,128)(2,1)S(1)} %get-tuple-element.87), channel_id=1, source_target_pairs={{0,65},{65,0},{1,64},{64,1},{2,67},{67,2},{3,66},{66,3},{4,69},{69... | collective-permute-start | bytes 393224 | tf_op jit(solution)/shard_map/ppermute | solution.py:586
  279.5 15.4 %copy-start.22 = (s32[1,16]{1,0:T(1,128)S(1)}, s32[1,16]{1,0:T(1,128)}, u32[]{:S(2)}) copy-start(s32[1,16]{1,0:T(1,128)} %get-tuple-element.125) | copy-start | bytes 196
  279.5 43.1 %all-to-all-start.5 = ((bf16[64,8,2048]{2,1,0:T(8,128)(2,1)}), bf16[64,8,2048]{2,1,0:T(8,128)(2,1)S(1)}, u32[]{:S(2)}, u32[]{:S(2)}) async-start(bf16[64,8,2048]{2,1,0:T(8,128)(2,1)} %bitcast.37), calls=%async_computation.5 | async-start | bytes 4194304 | tf_op jit(solution)/shard_map/all_to_all | solution.py:614
  295.1 35.2 %collective-permute-start.14 = (bf16[4,32,1024]{2,1,0:T(8,128)(2,1)S(1)}, bf16[4,32,1024]{2,1,0:T(8,128)(2,1)}, u32[]{:S(2)}, u32[]{:S(2)}) collective-permute-start(bf16[4,32,1024]{2,1,0:T(8,128)(2,1)S(1)} %get-tuple-element.101), channel_id=1, source_target_pairs={{0,32},{32,0},{1,33},{33,1},{2,34},{34,2},{3,35},{35,3},{4,36},{36... | collective-permute-start | bytes 786440 | tf_op jit(solution)/shard_map/ppermute | solution.py:578
  296.8 33.4 %collective-permute-start.15 = (bf16[2,32,1024]{2,1,0:T(8,128)(2,1)}, bf16[2,32,1024]{2,1,0:T(8,128)(2,1)}, u32[]{:S(2)}, u32[]{:S(2)}) collective-permute-start(bf16[2,32,1024]{2,1,0:T(8,128)(2,1)} %collective-permute-done.7.refs_1_), channel_id=1, source_target_pairs={{0,32},{32,0},{1,33},{33,1},{2,34},{34,2},{3,35},{35,3},{4,36},{36... | collective-permute-start | bytes 393224 | tf_op jit(solution)/shard_map/ppermute | solution.py:578
  296.9 33.4 %collective-permute-start.16 = (bf16[2,32,1024]{2,1,0:T(8,128)(2,1)}, bf16[2,32,1024]{2,1,0:T(8,128)(2,1)}, u32[]{:S(2)}, u32[]{:S(2)}) collective-permute-start(bf16[2,32,1024]{2,1,0:T(8,128)(2,1)} %collective-permute-done.8.refs_2_), channel_id=1, source_target_pairs={{0,32},{32,0},{1,33},{33,1},{2,34},{34,2},{3,35},{35,3},{4,36},{36... | collective-permute-start | bytes 393224 | tf_op jit(solution)/shard_map/ppermute | solution.py:578
  302.5 0.8 copy-start.15
  303.3 37.4 %collective-permute-start.9 = (bf16[2,64,1024]{2,1,0:T(8,128)(2,1)}, bf16[2,64,1024]{2,1,0:T(8,128)(2,1)}, u32[]{:S(2)}, u32[]{:S(2)}) collective-permute-start(bf16[2,64,1024]{2,1,0:T(8,128)(2,1)} %get-tuple-element.95), channel_id=1, source_target_pairs={{0,64},{64,0},{1,65},{65,1},{2,66},{66,2},{3,67},{67,3},{4,68},{68... | collective-permute-start | bytes 786440 | tf_op jit(solution)/shard_map/ppermute | solution.py:582
  304.7 36.1 %collective-permute-start.10 = (bf16[2,64,1024]{2,1,0:T(8,128)(2,1)}, bf16[2,64,1024]{2,1,0:T(8,128)(2,1)}, u32[]{:S(2)}, u32[]{:S(2)}) collective-permute-start(bf16[2,64,1024]{2,1,0:T(8,128)(2,1)} %get-tuple-element.96), channel_id=1, source_target_pairs={{0,65},{65,0},{1,64},{64,1},{2,67},{67,2},{3,66},{66,3},{4,69},{69... | collective-permute-start | bytes 786440 | tf_op jit(solution)/shard_map/ppermute | solution.py:586
  322.6 1.3 copy-start.2
  324.0 6.3 %copy-start.4 = (f32[4,32,2048]{2,1,0:T(8,128)S(1)}, f32[4,32,2048]{2,1,0:T(8,128)}, u32[]{:S(2)}) copy-start(f32[4,32,2048]{2,1,0:T(8,128)} %weight.4) | copy-start | bytes 3145732
  324.0 33.4 %all-to-all-start.6 = ((bf16[64,8,2048]{2,1,0:T(8,128)(2,1)}), bf16[64,8,2048]{2,1,0:T(8,128)(2,1)S(1)}, u32[]{:S(2)}, u32[]{:S(2)}) async-start(bf16[64,8,2048]{2,1,0:T(8,128)(2,1)} %bitcast.36), calls=%async_computation.6 | async-start | bytes 4194304 | tf_op jit(solution)/shard_map/all_to_all | solution.py:614
  330.2 11.0 %copy-start.3 = (bf16[64,8,2048]{2,1,0:T(8,128)(2,1)S(1)}, bf16[64,8,2048]{2,1,0:T(8,128)(2,1)}, u32[]{:S(2)}) copy-start(bf16[64,8,2048]{2,1,0:T(8,128)(2,1)} %copy-done.2) | copy-start | bytes 6291460
  330.2 11.0 %copy-start.7 = (bf16[128,2048]{1,0:T(8,128)(2,1)S(1)}, bf16[128,2048]{1,0:T(8,128)(2,1)}, u32[]{:S(2)}) copy-start(bf16[128,2048]{1,0:T(8,128)(2,1)} %cot.3) | copy-start | bytes 1572868
  330.3 11.0 %copy-start.9 = (f32[128,2]{1,0:T(8,128)S(1)}, f32[128,2]{1,0:T(8,128)}, u32[]{:S(2)}) copy-start(f32[128,2]{1,0:T(8,128)} %copy-done.8) | copy-start | bytes 3076
  330.3 1.4 copy-start.13
  331.7 1.2 copy-start.14
  332.9 0.9 copy-start.18
  338.7 4.9 %collective-permute-start.11 = (bf16[4,64,1024]{2,1,0:T(8,128)(2,1)}, bf16[4,64,1024]{2,1,0:T(8,128)(2,1)S(1)}, u32[]{:S(2)}, u32[]{:S(2)}) collective-permute-start(bf16[4,64,1024]{2,1,0:T(8,128)(2,1)} %get-tuple-element.97), channel_id=1, source_target_pairs={{0,32},{32,0},{1,33},{33,1},{2,34},{34,2},{3,35},{35,3},{4,36},{36... | collective-permute-start | bytes 1572872 | tf_op jit(solution)/shard_map/ppermute | solution.py:578
  340.7 2.8 collective-permute-start.12
  340.8 2.7 collective-permute-start.13
  343.5 1.6 copy-start.1
  345.1 1.0 copy-start.16

commit v6 on v5

--- a/solution.py
+++ b/solution.py
@@ -229,15 +229,15 @@
 def prepare(core, w_in, w_out):
     n, r, c = w_in.shape
     ro = w_out.shape[1]
-    half = pl.BlockSpec((1, r + ro, HALF), lambda i, s: (i, 0, 0))
+    half = pl.BlockSpec((n // 2, r + ro, HALF), lambda i, s: (i, 0, 0))
     return pl.pallas_call(
         prepare_kernel,
         grid_spec=pltpu.PrefetchScalarGridSpec(
             num_scalar_prefetch=1,
-            grid=(n,),
+            grid=(2,),
             in_specs=[
-                pl.BlockSpec((1, r, c), lambda i, s: (i, 0, 0)),
-                pl.BlockSpec((1, ro, c), lambda i, s: (i, 0, 0)),
+                pl.BlockSpec((n // 2, r, c), lambda i, s: (i, 0, 0)),
+                pl.BlockSpec((n // 2, ro, c), lambda i, s: (i, 0, 0)),
             ],
             out_specs=[half, half],
         ),
@@ -369,8 +369,15 @@
     )(sel, weight, moment, square, *own, *other)
 
 
-def rows_of(w, flip):
-    return jnp.concatenate([w[y ^ flip, i] for i in range(w.shape[1]) for y in range(2)], axis=0)
+def rows_of(even, odd):
+    return jnp.concatenate([w[0, i] for i in range(even.shape[1]) for w in (even, odd)], axis=0)
+
+
+def halves(shape, place):
+    return [
+        pl.BlockSpec((1, *shape), lambda j, s: (s[1], *place(j))),
+        pl.BlockSpec((1, *shape), lambda j, s: (1 - s[1], *place(j))),
+    ]
 
 
 def put_rows(out, v, flip):
@@ -393,8 +400,8 @@
     )(core, *args)
 
 
-def hidden_kernel(core, x, own, oth, hidden, hidden_t, active, steep):
-    one, two = dot(x[...], rows_of(own, core[1])), dot(x[...], rows_of(oth, core[1]))
+def hidden_kernel(core, x, own0, own1, oth0, oth1, hidden, hidden_t, active, steep):
+    one, two = dot(x[...], rows_of(own0, own1)), dot(x[...], rows_of(oth0, oth1))
     is0 = core[0] == 0
     gating, upward = jnp.where(is0, one, two), jnp.where(is0, two, one)
     logistic = jax.nn.sigmoid(gating)
@@ -406,20 +413,20 @@
     steep[...] = upward * (logistic * (1.0 + gating * (1.0 - logistic)))
 
 
-def other_hidden_kernel(core, x, own, oth, hidden_t):
-    one, two = dot(x[...], rows_of(own, core[1])), dot(x[...], rows_of(oth, core[1]))
+def other_hidden_kernel(core, x, own0, own1, oth0, oth1, hidden_t):
+    one, two = dot(x[...], rows_of(own0, own1)), dot(x[...], rows_of(oth0, oth1))
     is0 = core[0] == 0
     gating, upward = jnp.where(is0, one, two), jnp.where(is0, two, one)
     hidden_t[...] = (gating * jax.nn.sigmoid(gating) * upward).T.astype(BF)
 
 
 def other_hidden_of(core, got, own, oth):
-    w = pl.BlockSpec((2, 16, 64, 256), lambda j, s: (0, 0, 0, j))
+    w = halves((16, 64, 256), lambda j: (0, 0, j))
     return call(
         other_hidden_kernel,
         core,
-        (got, own, oth),
-        [pl.BlockSpec((ROWS, D), lambda j, s: (0, 0)), w, w],
+        (got, own, own, oth, oth),
+        [pl.BlockSpec((ROWS, D), lambda j, s: (0, 0)), *w, *w],
         jax.ShapeDtypeStruct((FF, ROWS), BF),
         pl.BlockSpec((256, ROWS), lambda j, s: (j, 0)),
         FF // 256,
@@ -428,13 +435,13 @@
 
 
 def hidden_of(core, got, own, oth):
-    w = pl.BlockSpec((2, 16, 64, 256), lambda j, s: (0, 0, 0, j))
+    w = halves((16, 64, 256), lambda j: (0, 0, j))
     tile = pl.BlockSpec((ROWS, 256), lambda j, s: (0, j))
     return call(
         hidden_kernel,
         core,
-        (got, own, oth),
-        [pl.BlockSpec((ROWS, D), lambda j, s: (0, 0)), w, w],
+        (got, own, own, oth, oth),
+        [pl.BlockSpec((ROWS, D), lambda j, s: (0, 0)), *w, *w],
         [
             jax.ShapeDtypeStruct((ROWS, FF), BF),
             jax.ShapeDtypeStruct((FF, ROWS), BF),
@@ -487,8 +494,8 @@
     )
 
 
-def back_kernel(core, dy_own, dy_oth, own, oth, active, steep, d_own, d_oth):
-    dhidden = dot_nt(dy_own[...], rows_of(own, core[1])) + dot_nt(dy_oth[...], rows_of(oth, core[1]))
+def back_kernel(core, dy_own, dy_oth, own0, own1, oth0, oth1, active, steep, d_own, d_oth):
+    dhidden = dot_nt(dy_own[...], rows_of(own0, own1)) + dot_nt(dy_oth[...], rows_of(oth0, oth1))
     d_gate = (dhidden * steep[...]).astype(BF)
     d_up = (dhidden * active[...]).astype(BF)
     is0 = core[0] == 0
@@ -497,17 +504,17 @@
 
 
 def back_of(core, got, own, oth, active, steep):
-    w = pl.BlockSpec((2, 4, 32, HALF), lambda j, s: (0, j, 0, 0))
+    w = halves((4, 32, HALF), lambda j: (j, 0, 0))
     tile = pl.BlockSpec((ROWS, 256), lambda j, s: (0, j))
     return call(
         back_kernel,
         core,
-        (got, got, own, oth, active, steep),
+        (got, got, own, own, oth, oth, active, steep),
         [
             pl.BlockSpec((ROWS, HALF), lambda j, s: (0, 2 + s[0])),
             pl.BlockSpec((ROWS, HALF), lambda j, s: (0, 3 - s[0])),
-            w,
-            w,
+            *w,
+            *w,
             tile,
             tile,
         ],
@@ -518,25 +525,25 @@
     )
 
 
-def result_kernel(core, hidden, own, oth, out):
+def result_kernel(core, hidden, own0, own1, oth0, oth1, out):
     step = pl.program_id(0)
 
     @pl.when(step == 0)
     def _():
-        out[...] = dot(hidden[...], rows_of(own, core[1])).astype(BF)
+        out[...] = dot(hidden[...], rows_of(own0, own1)).astype(BF)
 
     @pl.when(step == 1)
     def _():
-        out[...] = dot(hidden[...], rows_of(oth, core[1])).astype(BF)
+        out[...] = dot(hidden[...], rows_of(oth0, oth1)).astype(BF)
 
 
 def result_of(core, hidden, own, oth):
-    w = pl.BlockSpec((2, 16, 32, HALF), lambda j, s: (0, 0, 0, 0))
+    w = halves((16, 32, HALF), lambda j: (0, 0, 0))
     return call(
         result_kernel,
         core,
-        (hidden, own, oth),
-        [pl.BlockSpec((ROWS, FF), lambda j, s: (0, 0)), w, w],
+        (hidden, own, own, oth, oth),
+        [pl.BlockSpec((ROWS, FF), lambda j, s: (0, 0)), *w, *w],
         jax.ShapeDtypeStruct((ROWS, D), BF),
         pl.BlockSpec((ROWS, HALF), lambda j, s: (0, jnp.where(j == 0, s[0], 1 - s[0]))),
         2,
@@ -545,19 +552,19 @@
     )
 
 
-def dx_kernel(core, d_own, d_oth, own, oth, out):
-    dx = dot_nt(d_own[...], rows_of(own, core[1])) + dot_nt(d_oth[...], rows_of(oth, core[1]))
+def dx_kernel(core, d_own, d_oth, own0, own1, oth0, oth1, out):
+    dx = dot_nt(d_own[...], rows_of(own0, own1)) + dot_nt(d_oth[...], rows_of(oth0, oth1))
     out[...] = dx.astype(BF)
 
 
 def dx_of(core, d_own, d_oth, own, oth):
     row = pl.BlockSpec((ROWS, FF), lambda j, s: (0, 0))
-    w = pl.BlockSpec((2, 4, 64, HALF), lambda j, s: (0, j, 0, 0))
+    w = halves((4, 64, HALF), lambda j: (j, 0, 0))
     return call(
         dx_kernel,
         core,
-        (d_own, d_oth, own, oth),
-        [row, row, w, w],
+        (d_own, d_oth, own, own, oth, oth),
+        [row, row, *w, *w],
         jax.ShapeDtypeStruct((ROWS, D), BF),
         pl.BlockSpec((ROWS, 512), lambda j, s: (0, j)),
         4,

time: 363 us -> 362 us (level)
  transfers between devices with their start and end apart: 23 -> 23, of which waited for: 11 -> 10; matrix products, arithmetic and copies ran while one was open for 1% -> 1% of each run, Pallas kernels for 26% -> 27%
where the time goes in v6:
time: 362 us; the launch traced here: 358 us
  waiting for transfers between devices  106 us (29%)
  Pallas kernels  101 us (28%)
  starting transfers between devices  75.5 us (21%)
  blocking collectives  59.4 us (16%)
  local copies, waits for them, and re-layouts  13.6 us (4%)
    pallas_call x8, Pallas kernels, call(): pl.pallas_call(kernel, grid_spec=pltpu.PrefetchScalarGridSpec(num_scalar_...  66.3 us
    all_to_all x3, waiting for transfers between devices, exchange(): lax.all_to_all(v.reshape(CHIPS, UNITS, -1), CHIP_AXES, split_axis=0, conc...  63.1 us
    all_to_all x1, blocking collectives, spread(): lax.all_to_all(v.reshape(32, *v.shape[-2:]), SEND_AXES, split_axis=0, con...  59.4 us
    all_to_all x3, starting transfers between devices, exchange(): lax.all_to_all(v.reshape(CHIPS, UNITS, -1), CHIP_AXES, split_axis=0, conc...  32 us
    ppermute x3, waiting for transfers between devices, over_pair(): return lax.ppermute(v, 'yl', [(0, 1), (1, 0)])  29.3 us
    all_to_all x3, starting transfers between devices, spread(): lax.all_to_all(v.reshape(32, *v.shape[-2:]), SEND_AXES, split_axis=0, con...  20 us
    unnamed x49, local copies, waits for them, and re-layouts  12.8 us
    pallas_call x2, Pallas kernels, adam(): pl.pallas_call(adam_kernel, grid_spec=pltpu.PrefetchScalarGridSpec(num_sc...  11.9 us
  transfers between devices with their start and end apart: 23, of which 10 were waited for; matrix products, arithmetic and copies ran while one was open for 1% of the time, Pallas kernels for 27%

profile of v6, /device:TPU:1, one launch (start us, length us, event | category | flops | bytes accessed | tf_op | source)
XLA Modules:
  0.0 357.8 jit_solution(8083087568954562544)
XLA Ops:
  0.7 2.8 prepare.1
  3.5 1.4 collective-permute-start
  5.5 0.5 fusion.6
  6.1 1.0 collective-permute-done.theirs.refs_1_
  7.1 1.5 take_rows.1
  8.6 1.4 collective-permute-start.1
  10.0 1.9 collective-permute-start.2
  12.0 1.6 dispatch.1
  13.7 2.0 copy-done
  15.7 0.6 copy-done.8
  16.3 2.9 collective-permute-done.1.refs_2_
  19.2 2.3 collective-permute-done.2.refs_3_
  21.4 10.5 %all-to-all-start = ((bf16[64,8,4096]{2,1,0:T(8,128)(2,1)}), bf16[64,8,4096]{2,1,0:T(8,128)(2,1)}, u32[]{:S(2)}, u32[]{:S(2)}) async-start(bf16[64,8,4096]{2,1,0:T(8,128)(2,1)} %bitcast.28), calls=%async_computation | async-start | bytes 8388608 | tf_op jit(solution)/shard_map/all_to_all | solution.py:621
  32.1 2.9 select_rows.3
  35.0 3.6 select_rows.2
  38.6 42.8 %all-to-all-done = bf16[64,8,4096]{2,1,0:T(8,128)(2,1)} async-done(((bf16[64,8,4096]{2,1,0:T(8,128)(2,1)}), bf16[64,8,4096]{2,1,0:T(8,128)(2,1)}, u32[]{:S(2)}, u32[]{:S(2)}) %all-to-all-start) | async-done | bytes 4194336 | tf_op jit(solution)/shard_map/all_to_all | solution.py:621
  81.4 59.4 %all_to_all.35 = bf16[32,64,1024]{2,1,0:T(8,128)(2,1)} all-to-all(bf16[32,64,1024]{2,1,0:T(8,128)(2,1)} %select_rows.2), channel_id=1, replica_groups=mesh['yl'=2,'core'=2,'x'=4,'z'=4,'yh'=2] {'yh','x','z'}, dimensions={0} | all-to-all | bytes 8388608 | tf_op jit(solution)/shard_map/all_to_all | solution.py:617
  140.8 3.2 collective-permute-start.3
  144.0 4.9 %all-to-all-start.2 = ((bf16[32,32,1024]{2,1,0:T(8,128)(2,1)}), bf16[32,32,1024]{2,1,0:T(8,128)(2,1)}, u32[]{:S(2)}, u32[]{:S(2)}) async-start(bf16[32,32,1024]{2,1,0:T(8,128)(2,1)} %select_rows.3), calls=%async_computation.2 | async-start | bytes 4194304 | tf_op jit(solution)/shard_map/all_to_all | solution.py:617
  148.9 0.6 dynamic_slice.9
  150.2 0.6 pad_add_fusion.core
  150.8 0.4 collective-permute-done.3.oth0.oth1
  151.2 10.6 %hidden.1 = (bf16[512,1024]{1,0:T(8,128)(2,1)}, bf16[1024,512]{1,0:T(8,128)(2,1)}, f32[512,1024]{1,0:T(8,128)}, f32[512,1024]{1,0:T(8,128)}) custom-call(s32[2]{0:T(128)} %pad_add_fusion.core, bf16[512,4096]{1,0:T(8,128)(2,1)} %bitcast.9.x.b.one.dy_own.dy_oth, bf16[2,16,64,1024]{3,2,1,0:T(8,128)(2,1)} %bitcast.10.own0.own1, ...), custom_call_target="tpu_custom_call" | custom-call | flops 1 | bytes 1 | tf_op jit(solution)/shard_map/hidden/pallas_call | solution.py:391
  161.8 9.6 %other_hidden.1.a2_t = bf16[1024,512]{1,0:T(8,128)(2,1)} custom-call(s32[2]{0:T(128)} %pad_add_fusion.core, bf16[512,4096]{1,0:T(8,128)(2,1)} %collective-permute-done.4.x.b2.two, bf16[2,16,64,1024]{3,2,1,0:T(8,128)(2,1)} %bitcast.10.own0.own1, bf16[2,16,64,1024]{3,2,1,0:T(8,128)(2,1)} %bitcast.10.own0.own1, ...), custom_call_target="tpu_custom_call" | custom-call | flops 1 | bytes 1 | tf_op jit(solution)/shard_map/other_hidden/pallas_call | solution.py:391
  171.4 6.7 %outer_out.1 = bf16[2,16,32,1024]{3,2,1,0:T(8,128)(2,1)} custom-call(s32[2]{0:T(128)} %pad_add_fusion.core, bf16[1024,512]{1,0:T(8,128)(2,1)} %get-tuple-element.71.a_t, bf16[1024,512]{1,0:T(8,128)(2,1)} %other_hidden.1.a2_t, bf16[512,4096]{1,0:T(8,128)(2,1)} %bitcast.9.x.b.one.dy_own.dy_oth, bf16[512,4096]{1,0:T(8,128)(2,1)} %collective-permute-done.4.x.b2.two), custom_call_target="tpu_custom_call" | custom-call | flops 1 | bytes 1 | tf_op jit(solution)/shard_map/outer_out/pallas_call | solution.py:391
  178.1 1.4 collective-permute-start.5
  179.5 8.4 %all-to-all-start.3 = ((bf16[32,32,1024]{2,1,0:T(8,128)(2,1)}), bf16[32,32,1024]{2,1,0:T(8,128)(2,1)S(1)}, u32[]{:S(2)}, u32[]{:S(2)}) async-start(bf16[32,32,1024]{2,1,0:T(8,128)(2,1)} %bitcast.35), calls=%async_computation.3 | async-start | bytes 4194304 | tf_op jit(solution)/shard_map/all_to_all | solution.py:617
  188.0 8.1 %back.1 = (bf16[512,1024]{1,0:T(8,128)(2,1)}, bf16[512,1024]{1,0:T(8,128)(2,1)}) custom-call(s32[2]{0:T(128)} %pad_add_fusion.core, bf16[512,4096]{1,0:T(8,128)(2,1)} %bitcast.9.x.b.one.dy_own.dy_oth, bf16[512,4096]{1,0:T(8,128)(2,1)} %bitcast.9.x.b.one.dy_own.dy_oth, bf16[2,16,32,1024]{3,2,1,0:T(8,128)(2,1)} %bitcast.11.own0.own1, ...), custom_call_target="tpu_custom_call" | custom-call | flops 1 | bytes 1 | tf_op jit(solution)/shard_map/back/pallas_call | solution.py:391
  196.1 0.5 collective-permute-start.6
  196.6 5.6 %flip.1 = (bf16[2048,512]{1,0:T(8,128)(2,1)}, bf16[2048,512]{1,0:T(8,128)(2,1)}) custom-call(s32[2]{0:T(128)} %pad_add_fusion.core, bf16[512,4096]{1,0:T(8,128)(2,1)} %bitcast.9.x.b.one.dy_own.dy_oth, bf16[512,4096]{1,0:T(8,128)(2,1)} %collective-permute-done.4.x.b2.two), custom_call_target="tpu_custom_call" | custom-call | flops 10000000000 | bytes 20000000 | tf_op jit(solution)/shard_map/flip/pallas_call | solution.py:391
  202.1 1.0 copy-done.19
  203.1 9.4 %outer_in.1 = bf16[2,16,64,1024]{3,2,1,0:T(8,128)(2,1)} custom-call(s32[2]{0:T(128)} %pad_add_fusion.core, bf16[2048,512]{1,0:T(8,128)(2,1)} %get-tuple-element.75.a_t, bf16[2048,512]{1,0:T(8,128)(2,1)} %get-tuple-element.76.a2_t, bf16[512,1024]{1,0:T(8,128)(2,1)} %get-tuple-element.81.b.d_own, bf16[512,1024]{1,0:T(8,128)(2,1)} %copy-done.19), custom_call_target="tpu_custom_call" | custom-call | flops 1 | bytes 1 | tf_op jit(solution)/shard_map/outer_in/pallas_call | solution.py:391
  212.5 4.8 %all-to-all-done.3 = bf16[32,32,1024]{2,1,0:T(8,128)(2,1)S(1)} async-done(((bf16[32,32,1024]{2,1,0:T(8,128)(2,1)}), bf16[32,32,1024]{2,1,0:T(8,128)(2,1)S(1)}, u32[]{:S(2)}, u32[]{:S(2)}) %all-to-all-start.3) | async-done | bytes 2097184 | tf_op jit(solution)/shard_map/all_to_all | solution.py:617
  217.3 6.7 %all-to-all-start.4 = ((bf16[32,64,1024]{2,1,0:T(8,128)(2,1)}), bf16[32,64,1024]{2,1,0:T(8,128)(2,1)}, u32[]{:S(2)}, u32[]{:S(2)}) async-start(bf16[32,64,1024]{2,1,0:T(8,128)(2,1)} %bitcast.34), calls=%async_computation.4 | async-start | bytes 8388608 | tf_op jit(solution)/shard_map/all_to_all | solution.py:617
  224.0 9.6 %dx.1 = bf16[512,2048]{1,0:T(8,128)(2,1)} custom-call(s32[2]{0:T(128)} %pad_add_fusion.core, bf16[512,1024]{1,0:T(8,128)(2,1)} %get-tuple-element.81.b.d_own, bf16[512,1024]{1,0:T(8,128)(2,1)} %get-tuple-element.82.d_oth, bf16[2,16,64,1024]{3,2,1,0:T(8,128)(2,1)} %bitcast.10.own0.own1, bf16[2,16,64,1024]{3,2,1,0:T(8,128)(2,1)} %bitcast.10.own0.own1, ...), custom_call_target="tpu_custom_call" | custom-call | flops 10000000000 | bytes 20000000 | tf_op jit(solution)/shard_map/dx/pallas_call | solution.py:391
  233.6 6.7 %result.1 = bf16[512,2048]{1,0:T(8,128)(2,1)} custom-call(s32[2]{0:T(128)} %pad_add_fusion.core, bf16[512,1024]{1,0:T(8,128)(2,1)} %get-tuple-element.70.hidden, bf16[2,16,32,1024]{3,2,1,0:T(8,128)(2,1)} %bitcast.11.own0.own1, bf16[2,16,32,1024]{3,2,1,0:T(8,128)(2,1)} %bitcast.11.own0.own1, bf16[2,16,32,1024]{3,2,1,0:T(8,128)(2,1)} %collective-permute-done.5.oth0.oth1, ...), custom_call_target="tpu_custom_call" | custom-call | flops 10000000000 | bytes 20000000 | tf_op jit(solution)/shard_map/result/pallas_call | solution.py:391
  240.3 1.5 sum_rows.2
  241.9 3.5 collective-permute-start.7
  245.4 2.2 collective-permute-start.8
  247.6 26.4 %collective-permute-done.7.refs_1_ = bf16[2,32,1024]{2,1,0:T(8,128)(2,1)} collective-permute-done((bf16[2,32,1024]{2,1,0:T(8,128)(2,1)S(1)}, bf16[2,32,1024]{2,1,0:T(8,128)(2,1)}, u32[]{:S(2)}, u32[]{:S(2)}) %collective-permute-start.7) | collective-permute-done | bytes 131104 | tf_op jit(solution)/shard_map/ppermute | solution.py:589
  274.0 4.7 %collective-permute-done.8.refs_2_ = bf16[2,32,1024]{2,1,0:T(8,128)(2,1)} collective-permute-done((bf16[2,32,1024]{2,1,0:T(8,128)(2,1)S(1)}, bf16[2,32,1024]{2,1,0:T(8,128)(2,1)}, u32[]{:S(2)}, u32[]{:S(2)}) %collective-permute-start.8) | collective-permute-done | bytes 131104 | tf_op jit(solution)/shard_map/ppermute | solution.py:593
  278.7 15.2 %all-to-all-start.5 = ((bf16[64,8,2048]{2,1,0:T(8,128)(2,1)}), bf16[64,8,2048]{2,1,0:T(8,128)(2,1)S(1)}, u32[]{:S(2)}, u32[]{:S(2)}) async-start(bf16[64,8,2048]{2,1,0:T(8,128)(2,1)} %bitcast.37), calls=%async_computation.5 | async-start | bytes 4194304 | tf_op jit(solution)/shard_map/all_to_all | solution.py:621
  294.2 1.8 collective-permute-start.14
  296.1 0.4 collective-permute-start.16
  296.5 5.2 %sum_rows.3 = (bf16[4,64,1024]{2,1,0:T(8,128)(2,1)S(1)}, bf16[4,64,1024]{2,1,0:T(8,128)(2,1)}, bf16[2,64,1024]{2,1,0:T(8,128)(2,1)}, bf16[2,64,1024]{2,1,0:T(8,128)(2,1)}) custom-call(s32[32]{0:T(128)S(1)} %select_reduce_fusion.index, bf16[32,64,1024]{2,1,0:T(8,128)(2,1)} %bitcast.22.rows), custom_call_target="tpu_custom_call" | custom-call | flops 10000000000 | bytes 20000000 | tf_op jit(solution)/shard_map/sum_rows/pallas_call | solution.py:319
  301.7 0.8 copy-done.15
  302.5 1.4 collective-permute-start.9
  303.9 1.7 collective-permute-start.10
  305.5 16.3 %all-to-all-done.5 = bf16[64,8,2048]{2,1,0:T(8,128)(2,1)S(1)} async-done(((bf16[64,8,2048]{2,1,0:T(8,128)(2,1)}), bf16[64,8,2048]{2,1,0:T(8,128)(2,1)S(1)}, u32[]{:S(2)}, u32[]{:S(2)}) %all-to-all-start.5) | async-done | bytes 2097184 | tf_op jit(solution)/shard_map/all_to_all | solution.py:621
  321.8 1.3 copy-done.2
  323.1 6.3 %all-to-all-start.6 = ((bf16[64,8,2048]{2,1,0:T(8,128)(2,1)}), bf16[64,8,2048]{2,1,0:T(8,128)(2,1)S(1)}, u32[]{:S(2)}, u32[]{:S(2)}) async-start(bf16[64,8,2048]{2,1,0:T(8,128)(2,1)} %bitcast.36), calls=%async_computation.6 | async-start | bytes 4194304 | tf_op jit(solution)/shard_map/all_to_all | solution.py:621
  329.5 1.4 copy-done.13
  330.9 1.2 copy-done.14
  332.1 0.9 copy-done.18
  333.0 4.8 %adam.3 = (f32[4,32,2048]{2,1,0:T(8,128)}, f32[4,32,2048]{2,1,0:T(8,128)}, f32[4,32,2048]{2,1,0:T(8,128)}) custom-call(s32[5]{0:T(128)S(1)} %pad_add_fusion.1.sel, f32[4,32,2048]{2,1,0:T(8,128)S(1)} %copy-done.4, f32[4,32,2048]{2,1,0:T(8,128)S(1)} %copy-done.13, f32[4,32,2048]{2,1,0:T(8,128)S(1)} %copy-done.14, bf16[4,32,1024]{2,1,0:T(8,128)(2,1)S(1)} %copy-done.18, ...), custom_call_target="tpu_custom_call" | custom-call | flops 10000000000 | bytes 20000000 | tf_op jit(solution)/shard_map/adam/pallas_call | solution.py:357
  337.9 2.0 collective-permute-start.11
  340.0 0.4 collective-permute-start.13
  340.4 1.7 mix_results.1
  342.1 0.6 copy.27
  342.7 1.6 copy-done.1
  344.3 1.0 copy-done.16
  345.4 7.1 %adam.2 = (f32[4,64,2048]{2,1,0:T(8,128)}, f32[4,64,2048]{2,1,0:T(8,128)}, f32[4,64,2048]{2,1,0:T(8,128)}) custom-call(s32[5]{0:T(128)S(1)} %pad_add_fusion.1.sel, f32[4,64,2048]{2,1,0:T(8,128)S(1)} %copy-done.1, f32[4,64,2048]{2,1,0:T(8,128)} %moment.2, f32[4,64,2048]{2,1,0:T(8,128)} %square.2, bf16[4,64,1024]{2,1,0:T(8,128)(2,1)S(1)} %copy-done.16, ...), custom_call_target="tpu_custom_call" | custom-call | flops 10000000000 | bytes 20000000 | tf_op jit(solution)/shard_map/adam/pallas_call | solution.py:357
  352.5 4.0 %all-to-all-done.6 = bf16[64,8,2048]{2,1,0:T(8,128)(2,1)S(1)} async-done(((bf16[64,8,2048]{2,1,0:T(8,128)(2,1)}), bf16[64,8,2048]{2,1,0:T(8,128)(2,1)S(1)}, u32[]{:S(2)}, u32[]{:S(2)}) %all-to-all-start.6) | async-done | bytes 2097184 | tf_op jit(solution)/shard_map/all_to_all | solution.py:621
  356.5 1.3 add_gradients.1
  (63 shorter events, 1.4 us)
Async XLA Ops:
  0.6 4.3 %copy-start.12 = (s32[128]{0:T(128)S(1)}, s32[128]{0:T(128)}, u32[]{:S(2)}) copy-start(s32[128]{0:T(128)} %param.14) | copy-start | bytes 1540
  0.7 11.2 %copy-start.10 = (s32[128,2]{0,1:T(2,128)S(1)}, s32[128,2]{0,1:T(2,128)}, u32[]{:S(2)}) copy-start(s32[128,2]{0,1:T(2,128)} %param.15) | copy-start | bytes 3076
  0.7 11.4 %copy-start.5 = (bf16[128,2048]{1,0:T(8,128)(2,1)S(1)}, bf16[128,2048]{1,0:T(8,128)(2,1)}, u32[]{:S(2)}) copy-start(bf16[128,2048]{1,0:T(8,128)(2,1)} %tok) | copy-start | bytes 1572868
  0.7 11.3 %copy-start.6 = (bf16[128,2048]{1,0:T(8,128)(2,1)S(1)}, bf16[128,2048]{1,0:T(8,128)(2,1)}, u32[]{:S(2)}) copy-start(bf16[128,2048]{1,0:T(8,128)(2,1)} %cot.3) | copy-start | bytes 1572868
  0.7 11.3 %copy-start.11 = (f32[128,2]{0,1:T(2,128)S(1)}, f32[128,2]{0,1:T(2,128)}, u32[]{:S(2)}) copy-start(f32[128,2]{0,1:T(2,128)} %param.13) | copy-start | bytes 3076
  3.5 3.5 collective-permute-start
  8.6 10.5 %collective-permute-start.1 = (bf16[2,96,1024]{2,1,0:T(8,128)(2,1)}, bf16[2,96,1024]{2,1,0:T(8,128)(2,1)S(1)}, u32[]{:S(2)}, u32[]{:S(2)}) collective-permute-start(bf16[2,96,1024]{2,1,0:T(8,128)(2,1)} %get-tuple-element.62), channel_id=1, source_target_pairs={{0,64},{64,0},{1,65},{65,1},{2,66},{66,2},{3,67},{67,3},{4,68},{68... | collective-permute-start | bytes 1179656 | tf_op jit(solution)/shard_map/ppermute | solution.py:589
  10.0 11.4 %collective-permute-start.2 = (bf16[2,96,1024]{2,1,0:T(8,128)(2,1)}, bf16[2,96,1024]{2,1,0:T(8,128)(2,1)S(1)}, u32[]{:S(2)}, u32[]{:S(2)}) collective-permute-start(bf16[2,96,1024]{2,1,0:T(8,128)(2,1)} %get-tuple-element.63), channel_id=1, source_target_pairs={{0,65},{65,0},{1,64},{64,1},{2,67},{67,2},{3,66},{66,3},{4,69},{69... | collective-permute-start | bytes 1179656 | tf_op jit(solution)/shard_map/ppermute | solution.py:593
  13.7 2.0 copy-start
  15.7 0.6 copy-start.8
  21.4 10.5 %copy-start.20 = (s32[16]{0:T(128)S(1)}, s32[16]{0:T(128)}, u32[]{:S(2)}) copy-start(s32[16]{0:T(128)} %get-tuple-element.127) | copy-start | bytes 196
  21.4 10.6 %copy-start.21 = (s32[1,16]{1,0:T(1,128)S(1)}, s32[1,16]{1,0:T(1,128)}, u32[]{:S(2)}) copy-start(s32[1,16]{1,0:T(1,128)} %get-tuple-element.128) | copy-start | bytes 196
  21.4 60.0 %all-to-all-start = ((bf16[64,8,4096]{2,1,0:T(8,128)(2,1)}), bf16[64,8,4096]{2,1,0:T(8,128)(2,1)}, u32[]{:S(2)}, u32[]{:S(2)}) async-start(bf16[64,8,4096]{2,1,0:T(8,128)(2,1)} %bitcast.28), calls=%async_computation | async-start | bytes 8388608 | tf_op jit(solution)/shard_map/all_to_all | solution.py:621
  140.8 10.3 %collective-permute-start.3 = (bf16[2,16,64,1024]{3,2,1,0:T(8,128)(2,1)}, bf16[2,16,64,1024]{3,2,1,0:T(8,128)(2,1)}, u32[]{:S(2)}, u32[]{:S(2)}) collective-permute-start(bf16[2,16,64,1024]{3,2,1,0:T(8,128)(2,1)} %bitcast.10.own0.own1), channel_id=1, source_target_pairs={{0,32},{32,0},{1,33},{33,1},{2,34},{34,2},{3,35},{35,3},{4,36},{36... | collective-permute-start | bytes 12582920 | tf_op jit(solution)/shard_map/ppermute | solution.py:585
  144.0 17.8 %collective-permute-start.4 = (bf16[512,4096]{1,0:T(8,128)(2,1)}, bf16[512,4096]{1,0:T(8,128)(2,1)}, u32[]{:S(2)}, u32[]{:S(2)}) collective-permute-start(bf16[512,4096]{1,0:T(8,128)(2,1)} %bitcast.9.x.b.one.dy_own.dy_oth), channel_id=1, source_target_pairs={{0,32},{32,0},{1,33},{33,1},{2,34},{34,2},{3,35},{35,3},{4,36},{36... | collective-permute-start | bytes 12582920 | tf_op jit(solution)/shard_map/ppermute | solution.py:585
  144.0 34.1 %all-to-all-start.2 = ((bf16[32,32,1024]{2,1,0:T(8,128)(2,1)}), bf16[32,32,1024]{2,1,0:T(8,128)(2,1)}, u32[]{:S(2)}, u32[]{:S(2)}) async-start(bf16[32,32,1024]{2,1,0:T(8,128)(2,1)} %select_rows.3), calls=%async_computation.2 | async-start | bytes 4194304 | tf_op jit(solution)/shard_map/all_to_all | solution.py:617
  178.1 9.9 %collective-permute-start.5 = (bf16[2,16,32,1024]{3,2,1,0:T(8,128)(2,1)}, bf16[2,16,32,1024]{3,2,1,0:T(8,128)(2,1)}, u32[]{:S(2)}, u32[]{:S(2)}) collective-permute-start(bf16[2,16,32,1024]{3,2,1,0:T(8,128)(2,1)} %bitcast.11.own0.own1), channel_id=1, source_target_pairs={{0,32},{32,0},{1,33},{33,1},{2,34},{34,2},{3,35},{35,3},{4,36},{36... | collective-permute-start | bytes 6291464 | tf_op jit(solution)/shard_map/ppermute | solution.py:585
  179.5 37.8 %all-to-all-start.3 = ((bf16[32,32,1024]{2,1,0:T(8,128)(2,1)}), bf16[32,32,1024]{2,1,0:T(8,128)(2,1)S(1)}, u32[]{:S(2)}, u32[]{:S(2)}) async-start(bf16[32,32,1024]{2,1,0:T(8,128)(2,1)} %bitcast.35), calls=%async_computation.3 | async-start | bytes 4194304 | tf_op jit(solution)/shard_map/all_to_all | solution.py:617
  196.1 6.1 %collective-permute-start.6 = (bf16[512,1024]{1,0:T(8,128)(2,1)}, bf16[512,1024]{1,0:T(8,128)(2,1)S(1)}, u32[]{:S(2)}, u32[]{:S(2)}) collective-permute-start(bf16[512,1024]{1,0:T(8,128)(2,1)} %get-tuple-element.82.d_oth), channel_id=1, source_target_pairs={{0,32},{32,0},{1,33},{33,1},{2,34},{34,2},{3,35},{35,3},{4,36},{36... | collective-permute-start | bytes 3145736 | tf_op jit(solution)/shard_map/ppermute | solution.py:585
  202.1 1.0 copy-start.19
  217.3 61.4 %all-to-all-start.4 = ((bf16[32,64,1024]{2,1,0:T(8,128)(2,1)}), bf16[32,64,1024]{2,1,0:T(8,128)(2,1)}, u32[]{:S(2)}, u32[]{:S(2)}) async-start(bf16[32,64,1024]{2,1,0:T(8,128)(2,1)} %bitcast.34), calls=%async_computation.4 | async-start | bytes 8388608 | tf_op jit(solution)/shard_map/all_to_all | solution.py:617
  241.9 36.8 %copy-start.17 = (bf16[4,32,1024]{2,1,0:T(8,128)(2,1)}, bf16[4,32,1024]{2,1,0:T(8,128)(2,1)S(1)}, u32[]{:S(2)}) copy-start(bf16[4,32,1024]{2,1,0:T(8,128)(2,1)S(1)} %get-tuple-element.85.refs_0_) | copy-start | bytes 786436
  241.9 32.1 %collective-permute-start.7 = (bf16[2,32,1024]{2,1,0:T(8,128)(2,1)S(1)}, bf16[2,32,1024]{2,1,0:T(8,128)(2,1)}, u32[]{:S(2)}, u32[]{:S(2)}) collective-permute-start(bf16[2,32,1024]{2,1,0:T(8,128)(2,1)S(1)} %get-tuple-element.86), channel_id=1, source_target_pairs={{0,64},{64,0},{1,65},{65,1},{2,66},{66,2},{3,67},{67,3},{4,68},{68... | collective-permute-start | bytes 393224 | tf_op jit(solution)/shard_map/ppermute | solution.py:589
  245.4 33.3 %collective-permute-start.8 = (bf16[2,32,1024]{2,1,0:T(8,128)(2,1)S(1)}, bf16[2,32,1024]{2,1,0:T(8,128)(2,1)}, u32[]{:S(2)}, u32[]{:S(2)}) collective-permute-start(bf16[2,32,1024]{2,1,0:T(8,128)(2,1)S(1)} %get-tuple-element.87), channel_id=1, source_target_pairs={{0,65},{65,0},{1,64},{64,1},{2,67},{67,2},{3,66},{66,3},{4,69},{69... | collective-permute-start | bytes 393224 | tf_op jit(solution)/shard_map/ppermute | solution.py:593
  278.7 15.4 %copy-start.22 = (s32[1,16]{1,0:T(1,128)S(1)}, s32[1,16]{1,0:T(1,128)}, u32[]{:S(2)}) copy-start(s32[1,16]{1,0:T(1,128)} %get-tuple-element.125) | copy-start | bytes 196
  278.7 43.1 %all-to-all-start.5 = ((bf16[64,8,2048]{2,1,0:T(8,128)(2,1)}), bf16[64,8,2048]{2,1,0:T(8,128)(2,1)S(1)}, u32[]{:S(2)}, u32[]{:S(2)}) async-start(bf16[64,8,2048]{2,1,0:T(8,128)(2,1)} %bitcast.37), calls=%async_computation.5 | async-start | bytes 4194304 | tf_op jit(solution)/shard_map/all_to_all | solution.py:621
  294.2 35.2 %collective-permute-start.14 = (bf16[4,32,1024]{2,1,0:T(8,128)(2,1)S(1)}, bf16[4,32,1024]{2,1,0:T(8,128)(2,1)}, u32[]{:S(2)}, u32[]{:S(2)}) collective-permute-start(bf16[4,32,1024]{2,1,0:T(8,128)(2,1)S(1)} %get-tuple-element.101), channel_id=1, source_target_pairs={{0,32},{32,0},{1,33},{33,1},{2,34},{34,2},{3,35},{35,3},{4,36},{36... | collective-permute-start | bytes 786440 | tf_op jit(solution)/shard_map/ppermute | solution.py:585
  296.0 33.4 %collective-permute-start.15 = (bf16[2,32,1024]{2,1,0:T(8,128)(2,1)}, bf16[2,32,1024]{2,1,0:T(8,128)(2,1)}, u32[]{:S(2)}, u32[]{:S(2)}) collective-permute-start(bf16[2,32,1024]{2,1,0:T(8,128)(2,1)} %collective-permute-done.7.refs_1_), channel_id=1, source_target_pairs={{0,32},{32,0},{1,33},{33,1},{2,34},{34,2},{3,35},{35,3},{4,36},{36... | collective-permute-start | bytes 393224 | tf_op jit(solution)/shard_map/ppermute | solution.py:585
  296.1 33.4 %collective-permute-start.16 = (bf16[2,32,1024]{2,1,0:T(8,128)(2,1)}, bf16[2,32,1024]{2,1,0:T(8,128)(2,1)}, u32[]{:S(2)}, u32[]{:S(2)}) collective-permute-start(bf16[2,32,1024]{2,1,0:T(8,128)(2,1)} %collective-permute-done.8.refs_2_), channel_id=1, source_target_pairs={{0,32},{32,0},{1,33},{33,1},{2,34},{34,2},{3,35},{35,3},{4,36},{36... | collective-permute-start | bytes 393224 | tf_op jit(solution)/shard_map/ppermute | solution.py:585
  301.7 0.8 copy-start.15
  302.5 37.4 %collective-permute-start.9 = (bf16[2,64,1024]{2,1,0:T(8,128)(2,1)}, bf16[2,64,1024]{2,1,0:T(8,128)(2,1)}, u32[]{:S(2)}, u32[]{:S(2)}) collective-permute-start(bf16[2,64,1024]{2,1,0:T(8,128)(2,1)} %get-tuple-element.95), channel_id=1, source_target_pairs={{0,64},{64,0},{1,65},{65,1},{2,66},{66,2},{3,67},{67,3},{4,68},{68... | collective-permute-start | bytes 786440 | tf_op jit(solution)/shard_map/ppermute | solution.py:589
  303.9 36.1 %collective-permute-start.10 = (bf16[2,64,1024]{2,1,0:T(8,128)(2,1)}, bf16[2,64,1024]{2,1,0:T(8,128)(2,1)}, u32[]{:S(2)}, u32[]{:S(2)}) collective-permute-start(bf16[2,64,1024]{2,1,0:T(8,128)(2,1)} %get-tuple-element.96), channel_id=1, source_target_pairs={{0,65},{65,0},{1,64},{64,1},{2,67},{67,2},{3,66},{66,3},{4,69},{69... | collective-permute-start | bytes 786440 | tf_op jit(solution)/shard_map/ppermute | solution.py:593
  321.8 1.3 copy-start.2
  323.1 6.3 %copy-start.4 = (f32[4,32,2048]{2,1,0:T(8,128)S(1)}, f32[4,32,2048]{2,1,0:T(8,128)}, u32[]{:S(2)}) copy-start(f32[4,32,2048]{2,1,0:T(8,128)} %weight.4) | copy-start | bytes 3145732
  323.1 33.4 %all-to-all-start.6 = ((bf16[64,8,2048]{2,1,0:T(8,128)(2,1)}), bf16[64,8,2048]{2,1,0:T(8,128)(2,1)S(1)}, u32[]{:S(2)}, u32[]{:S(2)}) async-start(bf16[64,8,2048]{2,1,0:T(8,128)(2,1)} %bitcast.36), calls=%async_computation.6 | async-start | bytes 4194304 | tf_op jit(solution)/shard_map/all_to_all | solution.py:621
  329.4 11.0 %copy-start.3 = (bf16[64,8,2048]{2,1,0:T(8,128)(2,1)S(1)}, bf16[64,8,2048]{2,1,0:T(8,128)(2,1)}, u32[]{:S(2)}) copy-start(bf16[64,8,2048]{2,1,0:T(8,128)(2,1)} %copy-done.2) | copy-start | bytes 6291460
  329.4 11.0 %copy-start.7 = (bf16[128,2048]{1,0:T(8,128)(2,1)S(1)}, bf16[128,2048]{1,0:T(8,128)(2,1)}, u32[]{:S(2)}) copy-start(bf16[128,2048]{1,0:T(8,128)(2,1)} %cot.3) | copy-start | bytes 1572868
  329.4 11.0 %copy-start.9 = (f32[128,2]{1,0:T(8,128)S(1)}, f32[128,2]{1,0:T(8,128)}, u32[]{:S(2)}) copy-start(f32[128,2]{1,0:T(8,128)} %copy-done.8) | copy-start | bytes 3076
  329.5 1.4 copy-start.13
  330.9 1.2 copy-start.14
  332.1 0.9 copy-start.18
  337.9 4.9 %collective-permute-start.11 = (bf16[4,64,1024]{2,1,0:T(8,128)(2,1)}, bf16[4,64,1024]{2,1,0:T(8,128)(2,1)S(1)}, u32[]{:S(2)}, u32[]{:S(2)}) collective-permute-start(bf16[4,64,1024]{2,1,0:T(8,128)(2,1)} %get-tuple-element.97), channel_id=1, source_target_pairs={{0,32},{32,0},{1,33},{33,1},{2,34},{34,2},{3,35},{35,3},{4,36},{36... | collective-permute-start | bytes 1572872 | tf_op jit(solution)/shard_map/ppermute | solution.py:585
  339.9 2.8 collective-permute-start.12
  340.0 2.7 collective-permute-start.13
  342.7 1.6 copy-start.1
  344.3 1.0 copy-start.16

commit v7 on v6

--- a/solution.py
+++ b/solution.py
@@ -406,9 +406,9 @@
     gating, upward = jnp.where(is0, one, two), jnp.where(is0, two, one)
     logistic = jax.nn.sigmoid(gating)
     act = gating * logistic
-    hid = act * upward
-    hidden[...] = hid.astype(BF)
-    hidden_t[...] = hid.T.astype(BF)
+    hid = (act * upward).astype(BF)
+    hidden[...] = hid
+    hidden_t[...] = hid.T
     active[...] = act
     steep[...] = upward * (logistic * (1.0 + gating * (1.0 - logistic)))
 
@@ -417,7 +417,7 @@
     one, two = dot(x[...], rows_of(own0, own1)), dot(x[...], rows_of(oth0, oth1))
     is0 = core[0] == 0
     gating, upward = jnp.where(is0, one, two), jnp.where(is0, two, one)
-    hidden_t[...] = (gating * jax.nn.sigmoid(gating) * upward).T.astype(BF)
+    hidden_t[...] = (gating * jax.nn.sigmoid(gating) * upward).astype(BF).T
 
 
 def other_hidden_of(core, got, own, oth):

time: 362 us -> 362 us (level)
  no operation moved by 1% of the time
where the time goes in v7:
time: 362 us; the launch traced here: 358 us
  waiting for transfers between devices  105 us (29%)
  Pallas kernels  101 us (28%)
  starting transfers between devices  75.7 us (21%)
  blocking collectives  59.4 us (16%)
  local copies, waits for them, and re-layouts  13.6 us (4%)
    pallas_call x8, Pallas kernels, call(): pl.pallas_call(kernel, grid_spec=pltpu.PrefetchScalarGridSpec(num_scalar_...  66.2 us
    all_to_all x3, waiting for transfers between devices, exchange(): lax.all_to_all(v.reshape(CHIPS, UNITS, -1), CHIP_AXES, split_axis=0, conc...  62.9 us
    all_to_all x1, blocking collectives, spread(): lax.all_to_all(v.reshape(32, *v.shape[-2:]), SEND_AXES, split_axis=0, con...  59.4 us
    all_to_all x3, starting transfers between devices, exchange(): lax.all_to_all(v.reshape(CHIPS, UNITS, -1), CHIP_AXES, split_axis=0, conc...  32 us
    ppermute x3, waiting for transfers between devices, over_pair(): return lax.ppermute(v, 'yl', [(0, 1), (1, 0)])  29.3 us
    all_to_all x3, starting transfers between devices, spread(): lax.all_to_all(v.reshape(32, *v.shape[-2:]), SEND_AXES, split_axis=0, con...  20 us
    unnamed x49, local copies, waits for them, and re-layouts  12.8 us
    pallas_call x2, Pallas kernels, adam(): pl.pallas_call(adam_kernel, grid_spec=pltpu.PrefetchScalarGridSpec(num_sc...  11.8 us
  transfers between devices with their start and end apart: 23, of which 10 were waited for; matrix products, arithmetic and copies ran while one was open for 1% of the time, Pallas kernels for 27%

profile of v7, /device:TPU:1, one launch (start us, length us, event | category | flops | bytes accessed | tf_op | source)
XLA Modules:
  0.0 357.7 jit_solution(11325774419625935786)
XLA Ops:
  0.7 2.8 prepare.1
  3.5 1.4 collective-permute-start
  5.5 0.5 fusion.6
  6.1 1.0 collective-permute-done.theirs.refs_1_
  7.1 1.5 take_rows.1
  8.6 1.4 collective-permute-start.1
  10.0 1.9 collective-permute-start.2
  12.0 1.6 dispatch.1
  13.7 2.0 copy-done
  15.7 0.6 copy-done.8
  16.3 2.9 collective-permute-done.1.refs_2_
  19.2 2.3 collective-permute-done.2.refs_3_
  21.4 10.5 %all-to-all-start = ((bf16[64,8,4096]{2,1,0:T(8,128)(2,1)}), bf16[64,8,4096]{2,1,0:T(8,128)(2,1)}, u32[]{:S(2)}, u32[]{:S(2)}) async-start(bf16[64,8,4096]{2,1,0:T(8,128)(2,1)} %bitcast.28), calls=%async_computation | async-start | bytes 8388608 | tf_op jit(solution)/shard_map/all_to_all | solution.py:621
  32.1 2.9 select_rows.3
  35.0 3.6 select_rows.2
  38.6 42.8 %all-to-all-done = bf16[64,8,4096]{2,1,0:T(8,128)(2,1)} async-done(((bf16[64,8,4096]{2,1,0:T(8,128)(2,1)}), bf16[64,8,4096]{2,1,0:T(8,128)(2,1)}, u32[]{:S(2)}, u32[]{:S(2)}) %all-to-all-start) | async-done | bytes 4194336 | tf_op jit(solution)/shard_map/all_to_all | solution.py:621
  81.4 59.4 %all_to_all.35 = bf16[32,64,1024]{2,1,0:T(8,128)(2,1)} all-to-all(bf16[32,64,1024]{2,1,0:T(8,128)(2,1)} %select_rows.2), channel_id=1, replica_groups=mesh['yl'=2,'core'=2,'x'=4,'z'=4,'yh'=2] {'yh','x','z'}, dimensions={0} | all-to-all | bytes 8388608 | tf_op jit(solution)/shard_map/all_to_all | solution.py:617
  140.8 3.2 collective-permute-start.3
  144.0 4.9 %all-to-all-start.2 = ((bf16[32,32,1024]{2,1,0:T(8,128)(2,1)}), bf16[32,32,1024]{2,1,0:T(8,128)(2,1)}, u32[]{:S(2)}, u32[]{:S(2)}) async-start(bf16[32,32,1024]{2,1,0:T(8,128)(2,1)} %select_rows.3), calls=%async_computation.2 | async-start | bytes 4194304 | tf_op jit(solution)/shard_map/all_to_all | solution.py:617
  148.9 0.6 dynamic_slice.9
  150.2 0.6 pad_add_fusion.core
  150.8 0.4 collective-permute-done.3.oth0.oth1
  151.2 10.6 %hidden.1 = (bf16[512,1024]{1,0:T(8,128)(2,1)}, bf16[1024,512]{1,0:T(8,128)(2,1)}, f32[512,1024]{1,0:T(8,128)}, f32[512,1024]{1,0:T(8,128)}) custom-call(s32[2]{0:T(128)} %pad_add_fusion.core, bf16[512,4096]{1,0:T(8,128)(2,1)} %bitcast.9.x.b.one.dy_own.dy_oth, bf16[2,16,64,1024]{3,2,1,0:T(8,128)(2,1)} %bitcast.10.own0.own1, ...), custom_call_target="tpu_custom_call" | custom-call | flops 1 | bytes 1 | tf_op jit(solution)/shard_map/hidden/pallas_call | solution.py:391
  161.8 9.6 %other_hidden.1.a2_t = bf16[1024,512]{1,0:T(8,128)(2,1)} custom-call(s32[2]{0:T(128)} %pad_add_fusion.core, bf16[512,4096]{1,0:T(8,128)(2,1)} %collective-permute-done.4.x.b2.two, bf16[2,16,64,1024]{3,2,1,0:T(8,128)(2,1)} %bitcast.10.own0.own1, bf16[2,16,64,1024]{3,2,1,0:T(8,128)(2,1)} %bitcast.10.own0.own1, ...), custom_call_target="tpu_custom_call" | custom-call | flops 1 | bytes 1 | tf_op jit(solution)/shard_map/other_hidden/pallas_call | solution.py:391
  171.4 6.7 %outer_out.1 = bf16[2,16,32,1024]{3,2,1,0:T(8,128)(2,1)} custom-call(s32[2]{0:T(128)} %pad_add_fusion.core, bf16[1024,512]{1,0:T(8,128)(2,1)} %get-tuple-element.71.a_t, bf16[1024,512]{1,0:T(8,128)(2,1)} %other_hidden.1.a2_t, bf16[512,4096]{1,0:T(8,128)(2,1)} %bitcast.9.x.b.one.dy_own.dy_oth, bf16[512,4096]{1,0:T(8,128)(2,1)} %collective-permute-done.4.x.b2.two), custom_call_target="tpu_custom_call" | custom-call | flops 1 | bytes 1 | tf_op jit(solution)/shard_map/outer_out/pallas_call | solution.py:391
  178.1 1.5 collective-permute-start.5
  179.5 8.4 %all-to-all-start.3 = ((bf16[32,32,1024]{2,1,0:T(8,128)(2,1)}), bf16[32,32,1024]{2,1,0:T(8,128)(2,1)S(1)}, u32[]{:S(2)}, u32[]{:S(2)}) async-start(bf16[32,32,1024]{2,1,0:T(8,128)(2,1)} %bitcast.35), calls=%async_computation.3 | async-start | bytes 4194304 | tf_op jit(solution)/shard_map/all_to_all | solution.py:617
  188.0 8.1 %back.1 = (bf16[512,1024]{1,0:T(8,128)(2,1)}, bf16[512,1024]{1,0:T(8,128)(2,1)}) custom-call(s32[2]{0:T(128)} %pad_add_fusion.core, bf16[512,4096]{1,0:T(8,128)(2,1)} %bitcast.9.x.b.one.dy_own.dy_oth, bf16[512,4096]{1,0:T(8,128)(2,1)} %bitcast.9.x.b.one.dy_own.dy_oth, bf16[2,16,32,1024]{3,2,1,0:T(8,128)(2,1)} %bitcast.11.own0.own1, ...), custom_call_target="tpu_custom_call" | custom-call | flops 1 | bytes 1 | tf_op jit(solution)/shard_map/back/pallas_call | solution.py:391
  196.0 0.5 collective-permute-start.6
  196.5 5.6 %flip.1 = (bf16[2048,512]{1,0:T(8,128)(2,1)}, bf16[2048,512]{1,0:T(8,128)(2,1)}) custom-call(s32[2]{0:T(128)} %pad_add_fusion.core, bf16[512,4096]{1,0:T(8,128)(2,1)} %bitcast.9.x.b.one.dy_own.dy_oth, bf16[512,4096]{1,0:T(8,128)(2,1)} %collective-permute-done.4.x.b2.two), custom_call_target="tpu_custom_call" | custom-call | flops 10000000000 | bytes 20000000 | tf_op jit(solution)/shard_map/flip/pallas_call | solution.py:391
  202.1 1.0 copy-done.19
  203.1 9.4 %outer_in.1 = bf16[2,16,64,1024]{3,2,1,0:T(8,128)(2,1)} custom-call(s32[2]{0:T(128)} %pad_add_fusion.core, bf16[2048,512]{1,0:T(8,128)(2,1)} %get-tuple-element.75.a_t, bf16[2048,512]{1,0:T(8,128)(2,1)} %get-tuple-element.76.a2_t, bf16[512,1024]{1,0:T(8,128)(2,1)} %get-tuple-element.81.b.d_own, bf16[512,1024]{1,0:T(8,128)(2,1)} %copy-done.19), custom_call_target="tpu_custom_call" | custom-call | flops 1 | bytes 1 | tf_op jit(solution)/shard_map/outer_in/pallas_call | solution.py:391
  212.4 4.8 %all-to-all-done.3 = bf16[32,32,1024]{2,1,0:T(8,128)(2,1)S(1)} async-done(((bf16[32,32,1024]{2,1,0:T(8,128)(2,1)}), bf16[32,32,1024]{2,1,0:T(8,128)(2,1)S(1)}, u32[]{:S(2)}, u32[]{:S(2)}) %all-to-all-start.3) | async-done | bytes 2097184 | tf_op jit(solution)/shard_map/all_to_all | solution.py:617
  217.2 6.7 %all-to-all-start.4 = ((bf16[32,64,1024]{2,1,0:T(8,128)(2,1)}), bf16[32,64,1024]{2,1,0:T(8,128)(2,1)}, u32[]{:S(2)}, u32[]{:S(2)}) async-start(bf16[32,64,1024]{2,1,0:T(8,128)(2,1)} %bitcast.34), calls=%async_computation.4 | async-start | bytes 8388608 | tf_op jit(solution)/shard_map/all_to_all | solution.py:617
  223.9 9.6 %dx.1 = bf16[512,2048]{1,0:T(8,128)(2,1)} custom-call(s32[2]{0:T(128)} %pad_add_fusion.core, bf16[512,1024]{1,0:T(8,128)(2,1)} %get-tuple-element.81.b.d_own, bf16[512,1024]{1,0:T(8,128)(2,1)} %get-tuple-element.82.d_oth, bf16[2,16,64,1024]{3,2,1,0:T(8,128)(2,1)} %bitcast.10.own0.own1, bf16[2,16,64,1024]{3,2,1,0:T(8,128)(2,1)} %bitcast.10.own0.own1, ...), custom_call_target="tpu_custom_call" | custom-call | flops 10000000000 | bytes 20000000 | tf_op jit(solution)/shard_map/dx/pallas_call | solution.py:391
  233.5 6.7 %result.1 = bf16[512,2048]{1,0:T(8,128)(2,1)} custom-call(s32[2]{0:T(128)} %pad_add_fusion.core, bf16[512,1024]{1,0:T(8,128)(2,1)} %get-tuple-element.70.hidden, bf16[2,16,32,1024]{3,2,1,0:T(8,128)(2,1)} %bitcast.11.own0.own1, bf16[2,16,32,1024]{3,2,1,0:T(8,128)(2,1)} %bitcast.11.own0.own1, bf16[2,16,32,1024]{3,2,1,0:T(8,128)(2,1)} %collective-permute-done.5.oth0.oth1, ...), custom_call_target="tpu_custom_call" | custom-call | flops 10000000000 | bytes 20000000 | tf_op jit(solution)/shard_map/result/pallas_call | solution.py:391
  240.3 1.6 sum_rows.2
  241.8 3.5 collective-permute-start.7
  245.4 2.2 collective-permute-start.8
  247.5 26.4 %collective-permute-done.7.refs_1_ = bf16[2,32,1024]{2,1,0:T(8,128)(2,1)} collective-permute-done((bf16[2,32,1024]{2,1,0:T(8,128)(2,1)S(1)}, bf16[2,32,1024]{2,1,0:T(8,128)(2,1)}, u32[]{:S(2)}, u32[]{:S(2)}) %collective-permute-start.7) | collective-permute-done | bytes 131104 | tf_op jit(solution)/shard_map/ppermute | solution.py:589
  273.9 4.7 %collective-permute-done.8.refs_2_ = bf16[2,32,1024]{2,1,0:T(8,128)(2,1)} collective-permute-done((bf16[2,32,1024]{2,1,0:T(8,128)(2,1)S(1)}, bf16[2,32,1024]{2,1,0:T(8,128)(2,1)}, u32[]{:S(2)}, u32[]{:S(2)}) %collective-permute-start.8) | collective-permute-done | bytes 131104 | tf_op jit(solution)/shard_map/ppermute | solution.py:593
  278.6 15.2 %all-to-all-start.5 = ((bf16[64,8,2048]{2,1,0:T(8,128)(2,1)}), bf16[64,8,2048]{2,1,0:T(8,128)(2,1)S(1)}, u32[]{:S(2)}, u32[]{:S(2)}) async-start(bf16[64,8,2048]{2,1,0:T(8,128)(2,1)} %bitcast.37), calls=%async_computation.5 | async-start | bytes 4194304 | tf_op jit(solution)/shard_map/all_to_all | solution.py:621
  294.1 1.8 collective-permute-start.14
  296.0 0.4 collective-permute-start.16
  296.4 5.2 %sum_rows.3 = (bf16[4,64,1024]{2,1,0:T(8,128)(2,1)S(1)}, bf16[4,64,1024]{2,1,0:T(8,128)(2,1)}, bf16[2,64,1024]{2,1,0:T(8,128)(2,1)}, bf16[2,64,1024]{2,1,0:T(8,128)(2,1)}) custom-call(s32[32]{0:T(128)S(1)} %select_reduce_fusion.index, bf16[32,64,1024]{2,1,0:T(8,128)(2,1)} %bitcast.22.rows), custom_call_target="tpu_custom_call" | custom-call | flops 10000000000 | bytes 20000000 | tf_op jit(solution)/shard_map/sum_rows/pallas_call | solution.py:319
  301.6 0.8 copy-done.15
  302.4 1.4 collective-permute-start.9
  303.8 1.7 collective-permute-start.10
  305.5 16.3 %all-to-all-done.5 = bf16[64,8,2048]{2,1,0:T(8,128)(2,1)S(1)} async-done(((bf16[64,8,2048]{2,1,0:T(8,128)(2,1)}), bf16[64,8,2048]{2,1,0:T(8,128)(2,1)S(1)}, u32[]{:S(2)}, u32[]{:S(2)}) %all-to-all-start.5) | async-done | bytes 2097184 | tf_op jit(solution)/shard_map/all_to_all | solution.py:621
  321.7 1.3 copy-done.2
  323.0 6.3 %all-to-all-start.6 = ((bf16[64,8,2048]{2,1,0:T(8,128)(2,1)}), bf16[64,8,2048]{2,1,0:T(8,128)(2,1)S(1)}, u32[]{:S(2)}, u32[]{:S(2)}) async-start(bf16[64,8,2048]{2,1,0:T(8,128)(2,1)} %bitcast.36), calls=%async_computation.6 | async-start | bytes 4194304 | tf_op jit(solution)/shard_map/all_to_all | solution.py:621
  329.4 1.4 copy-done.13
  330.8 1.2 copy-done.14
  332.0 0.9 copy-done.18
  332.9 4.7 %adam.3 = (f32[4,32,2048]{2,1,0:T(8,128)}, f32[4,32,2048]{2,1,0:T(8,128)}, f32[4,32,2048]{2,1,0:T(8,128)}) custom-call(s32[5]{0:T(128)S(1)} %pad_add_fusion.1.sel, f32[4,32,2048]{2,1,0:T(8,128)S(1)} %copy-done.4, f32[4,32,2048]{2,1,0:T(8,128)S(1)} %copy-done.13, f32[4,32,2048]{2,1,0:T(8,128)S(1)} %copy-done.14, bf16[4,32,1024]{2,1,0:T(8,128)(2,1)S(1)} %copy-done.18, ...), custom_call_target="tpu_custom_call" | custom-call | flops 10000000000 | bytes 20000000 | tf_op jit(solution)/shard_map/adam/pallas_call | solution.py:357
  337.6 2.3 collective-permute-start.11
  340.0 0.4 collective-permute-start.13
  340.5 1.7 mix_results.1
  342.1 0.6 copy.27
  342.8 1.6 copy-done.1
  344.4 1.0 copy-done.16
  345.4 7.1 %adam.2 = (f32[4,64,2048]{2,1,0:T(8,128)}, f32[4,64,2048]{2,1,0:T(8,128)}, f32[4,64,2048]{2,1,0:T(8,128)}) custom-call(s32[5]{0:T(128)S(1)} %pad_add_fusion.1.sel, f32[4,64,2048]{2,1,0:T(8,128)S(1)} %copy-done.1, f32[4,64,2048]{2,1,0:T(8,128)} %moment.2, f32[4,64,2048]{2,1,0:T(8,128)} %square.2, bf16[4,64,1024]{2,1,0:T(8,128)(2,1)S(1)} %copy-done.16, ...), custom_call_target="tpu_custom_call" | custom-call | flops 10000000000 | bytes 20000000 | tf_op jit(solution)/shard_map/adam/pallas_call | solution.py:357
  352.5 3.9 %all-to-all-done.6 = bf16[64,8,2048]{2,1,0:T(8,128)(2,1)S(1)} async-done(((bf16[64,8,2048]{2,1,0:T(8,128)(2,1)}), bf16[64,8,2048]{2,1,0:T(8,128)(2,1)S(1)}, u32[]{:S(2)}, u32[]{:S(2)}) %all-to-all-start.6) | async-done | bytes 2097184 | tf_op jit(solution)/shard_map/all_to_all | solution.py:621
  356.4 1.3 add_gradients.1
  (63 shorter events, 1.4 us)
Async XLA Ops:
  0.6 4.3 %copy-start.12 = (s32[128]{0:T(128)S(1)}, s32[128]{0:T(128)}, u32[]{:S(2)}) copy-start(s32[128]{0:T(128)} %param.14) | copy-start | bytes 1540
  0.7 11.2 %copy-start.10 = (s32[128,2]{0,1:T(2,128)S(1)}, s32[128,2]{0,1:T(2,128)}, u32[]{:S(2)}) copy-start(s32[128,2]{0,1:T(2,128)} %param.15) | copy-start | bytes 3076
  0.7 11.4 %copy-start.5 = (bf16[128,2048]{1,0:T(8,128)(2,1)S(1)}, bf16[128,2048]{1,0:T(8,128)(2,1)}, u32[]{:S(2)}) copy-start(bf16[128,2048]{1,0:T(8,128)(2,1)} %tok) | copy-start | bytes 1572868
  0.7 11.3 %copy-start.6 = (bf16[128,2048]{1,0:T(8,128)(2,1)S(1)}, bf16[128,2048]{1,0:T(8,128)(2,1)}, u32[]{:S(2)}) copy-start(bf16[128,2048]{1,0:T(8,128)(2,1)} %cot.3) | copy-start | bytes 1572868
  0.7 11.3 %copy-start.11 = (f32[128,2]{0,1:T(2,128)S(1)}, f32[128,2]{0,1:T(2,128)}, u32[]{:S(2)}) copy-start(f32[128,2]{0,1:T(2,128)} %param.13) | copy-start | bytes 3076
  3.5 3.5 collective-permute-start
  8.6 10.5 %collective-permute-start.1 = (bf16[2,96,1024]{2,1,0:T(8,128)(2,1)}, bf16[2,96,1024]{2,1,0:T(8,128)(2,1)S(1)}, u32[]{:S(2)}, u32[]{:S(2)}) collective-permute-start(bf16[2,96,1024]{2,1,0:T(8,128)(2,1)} %get-tuple-element.62), channel_id=1, source_target_pairs={{0,64},{64,0},{1,65},{65,1},{2,66},{66,2},{3,67},{67,3},{4,68},{68... | collective-permute-start | bytes 1179656 | tf_op jit(solution)/shard_map/ppermute | solution.py:589
  10.0 11.4 %collective-permute-start.2 = (bf16[2,96,1024]{2,1,0:T(8,128)(2,1)}, bf16[2,96,1024]{2,1,0:T(8,128)(2,1)S(1)}, u32[]{:S(2)}, u32[]{:S(2)}) collective-permute-start(bf16[2,96,1024]{2,1,0:T(8,128)(2,1)} %get-tuple-element.63), channel_id=1, source_target_pairs={{0,65},{65,0},{1,64},{64,1},{2,67},{67,2},{3,66},{66,3},{4,69},{69... | collective-permute-start | bytes 1179656 | tf_op jit(solution)/shard_map/ppermute | solution.py:593
  13.7 2.0 copy-start
  15.7 0.6 copy-start.8
  21.4 10.6 %copy-start.20 = (s32[16]{0:T(128)S(1)}, s32[16]{0:T(128)}, u32[]{:S(2)}) copy-start(s32[16]{0:T(128)} %get-tuple-element.127) | copy-start | bytes 196
  21.4 10.6 %copy-start.21 = (s32[1,16]{1,0:T(1,128)S(1)}, s32[1,16]{1,0:T(1,128)}, u32[]{:S(2)}) copy-start(s32[1,16]{1,0:T(1,128)} %get-tuple-element.128) | copy-start | bytes 196
  21.4 60.0 %all-to-all-start = ((bf16[64,8,4096]{2,1,0:T(8,128)(2,1)}), bf16[64,8,4096]{2,1,0:T(8,128)(2,1)}, u32[]{:S(2)}, u32[]{:S(2)}) async-start(bf16[64,8,4096]{2,1,0:T(8,128)(2,1)} %bitcast.28), calls=%async_computation | async-start | bytes 8388608 | tf_op jit(solution)/shard_map/all_to_all | solution.py:621
  140.8 10.3 %collective-permute-start.3 = (bf16[2,16,64,1024]{3,2,1,0:T(8,128)(2,1)}, bf16[2,16,64,1024]{3,2,1,0:T(8,128)(2,1)}, u32[]{:S(2)}, u32[]{:S(2)}) collective-permute-start(bf16[2,16,64,1024]{3,2,1,0:T(8,128)(2,1)} %bitcast.10.own0.own1), channel_id=1, source_target_pairs={{0,32},{32,0},{1,33},{33,1},{2,34},{34,2},{3,35},{35,3},{4,36},{36... | collective-permute-start | bytes 12582920 | tf_op jit(solution)/shard_map/ppermute | solution.py:585
  144.0 17.8 %collective-permute-start.4 = (bf16[512,4096]{1,0:T(8,128)(2,1)}, bf16[512,4096]{1,0:T(8,128)(2,1)}, u32[]{:S(2)}, u32[]{:S(2)}) collective-permute-start(bf16[512,4096]{1,0:T(8,128)(2,1)} %bitcast.9.x.b.one.dy_own.dy_oth), channel_id=1, source_target_pairs={{0,32},{32,0},{1,33},{33,1},{2,34},{34,2},{3,35},{35,3},{4,36},{36... | collective-permute-start | bytes 12582920 | tf_op jit(solution)/shard_map/ppermute | solution.py:585
  144.0 34.0 %all-to-all-start.2 = ((bf16[32,32,1024]{2,1,0:T(8,128)(2,1)}), bf16[32,32,1024]{2,1,0:T(8,128)(2,1)}, u32[]{:S(2)}, u32[]{:S(2)}) async-start(bf16[32,32,1024]{2,1,0:T(8,128)(2,1)} %select_rows.3), calls=%async_computation.2 | async-start | bytes 4194304 | tf_op jit(solution)/shard_map/all_to_all | solution.py:617
  178.1 9.9 %collective-permute-start.5 = (bf16[2,16,32,1024]{3,2,1,0:T(8,128)(2,1)}, bf16[2,16,32,1024]{3,2,1,0:T(8,128)(2,1)}, u32[]{:S(2)}, u32[]{:S(2)}) collective-permute-start(bf16[2,16,32,1024]{3,2,1,0:T(8,128)(2,1)} %bitcast.11.own0.own1), channel_id=1, source_target_pairs={{0,32},{32,0},{1,33},{33,1},{2,34},{34,2},{3,35},{35,3},{4,36},{36... | collective-permute-start | bytes 6291464 | tf_op jit(solution)/shard_map/ppermute | solution.py:585
  179.5 37.7 %all-to-all-start.3 = ((bf16[32,32,1024]{2,1,0:T(8,128)(2,1)}), bf16[32,32,1024]{2,1,0:T(8,128)(2,1)S(1)}, u32[]{:S(2)}, u32[]{:S(2)}) async-start(bf16[32,32,1024]{2,1,0:T(8,128)(2,1)} %bitcast.35), calls=%async_computation.3 | async-start | bytes 4194304 | tf_op jit(solution)/shard_map/all_to_all | solution.py:617
  196.0 6.1 %collective-permute-start.6 = (bf16[512,1024]{1,0:T(8,128)(2,1)}, bf16[512,1024]{1,0:T(8,128)(2,1)S(1)}, u32[]{:S(2)}, u32[]{:S(2)}) collective-permute-start(bf16[512,1024]{1,0:T(8,128)(2,1)} %get-tuple-element.82.d_oth), channel_id=1, source_target_pairs={{0,32},{32,0},{1,33},{33,1},{2,34},{34,2},{3,35},{35,3},{4,36},{36... | collective-permute-start | bytes 3145736 | tf_op jit(solution)/shard_map/ppermute | solution.py:585
  202.1 1.0 copy-start.19
  217.2 61.4 %all-to-all-start.4 = ((bf16[32,64,1024]{2,1,0:T(8,128)(2,1)}), bf16[32,64,1024]{2,1,0:T(8,128)(2,1)}, u32[]{:S(2)}, u32[]{:S(2)}) async-start(bf16[32,64,1024]{2,1,0:T(8,128)(2,1)} %bitcast.34), calls=%async_computation.4 | async-start | bytes 8388608 | tf_op jit(solution)/shard_map/all_to_all | solution.py:617
  241.8 36.8 %copy-start.17 = (bf16[4,32,1024]{2,1,0:T(8,128)(2,1)}, bf16[4,32,1024]{2,1,0:T(8,128)(2,1)S(1)}, u32[]{:S(2)}) copy-start(bf16[4,32,1024]{2,1,0:T(8,128)(2,1)S(1)} %get-tuple-element.85.refs_0_) | copy-start | bytes 786436
  241.8 32.1 %collective-permute-start.7 = (bf16[2,32,1024]{2,1,0:T(8,128)(2,1)S(1)}, bf16[2,32,1024]{2,1,0:T(8,128)(2,1)}, u32[]{:S(2)}, u32[]{:S(2)}) collective-permute-start(bf16[2,32,1024]{2,1,0:T(8,128)(2,1)S(1)} %get-tuple-element.86), channel_id=1, source_target_pairs={{0,64},{64,0},{1,65},{65,1},{2,66},{66,2},{3,67},{67,3},{4,68},{68... | collective-permute-start | bytes 393224 | tf_op jit(solution)/shard_map/ppermute | solution.py:589
  245.4 33.3 %collective-permute-start.8 = (bf16[2,32,1024]{2,1,0:T(8,128)(2,1)S(1)}, bf16[2,32,1024]{2,1,0:T(8,128)(2,1)}, u32[]{:S(2)}, u32[]{:S(2)}) collective-permute-start(bf16[2,32,1024]{2,1,0:T(8,128)(2,1)S(1)} %get-tuple-element.87), channel_id=1, source_target_pairs={{0,65},{65,0},{1,64},{64,1},{2,67},{67,2},{3,66},{66,3},{4,69},{69... | collective-permute-start | bytes 393224 | tf_op jit(solution)/shard_map/ppermute | solution.py:593
  278.6 15.3 %copy-start.22 = (s32[1,16]{1,0:T(1,128)S(1)}, s32[1,16]{1,0:T(1,128)}, u32[]{:S(2)}) copy-start(s32[1,16]{1,0:T(1,128)} %get-tuple-element.125) | copy-start | bytes 196
  278.6 43.1 %all-to-all-start.5 = ((bf16[64,8,2048]{2,1,0:T(8,128)(2,1)}), bf16[64,8,2048]{2,1,0:T(8,128)(2,1)S(1)}, u32[]{:S(2)}, u32[]{:S(2)}) async-start(bf16[64,8,2048]{2,1,0:T(8,128)(2,1)} %bitcast.37), calls=%async_computation.5 | async-start | bytes 4194304 | tf_op jit(solution)/shard_map/all_to_all | solution.py:621
  294.1 35.2 %collective-permute-start.14 = (bf16[4,32,1024]{2,1,0:T(8,128)(2,1)S(1)}, bf16[4,32,1024]{2,1,0:T(8,128)(2,1)}, u32[]{:S(2)}, u32[]{:S(2)}) collective-permute-start(bf16[4,32,1024]{2,1,0:T(8,128)(2,1)S(1)} %get-tuple-element.101), channel_id=1, source_target_pairs={{0,32},{32,0},{1,33},{33,1},{2,34},{34,2},{3,35},{35,3},{4,36},{36... | collective-permute-start | bytes 786440 | tf_op jit(solution)/shard_map/ppermute | solution.py:585
  295.9 33.4 %collective-permute-start.15 = (bf16[2,32,1024]{2,1,0:T(8,128)(2,1)}, bf16[2,32,1024]{2,1,0:T(8,128)(2,1)}, u32[]{:S(2)}, u32[]{:S(2)}) collective-permute-start(bf16[2,32,1024]{2,1,0:T(8,128)(2,1)} %collective-permute-done.7.refs_1_), channel_id=1, source_target_pairs={{0,32},{32,0},{1,33},{33,1},{2,34},{34,2},{3,35},{35,3},{4,36},{36... | collective-permute-start | bytes 393224 | tf_op jit(solution)/shard_map/ppermute | solution.py:585
  296.0 33.4 %collective-permute-start.16 = (bf16[2,32,1024]{2,1,0:T(8,128)(2,1)}, bf16[2,32,1024]{2,1,0:T(8,128)(2,1)}, u32[]{:S(2)}, u32[]{:S(2)}) collective-permute-start(bf16[2,32,1024]{2,1,0:T(8,128)(2,1)} %collective-permute-done.8.refs_2_), channel_id=1, source_target_pairs={{0,32},{32,0},{1,33},{33,1},{2,34},{34,2},{3,35},{35,3},{4,36},{36... | collective-permute-start | bytes 393224 | tf_op jit(solution)/shard_map/ppermute | solution.py:585
  301.6 0.8 copy-start.15
  302.4 37.6 %collective-permute-start.9 = (bf16[2,64,1024]{2,1,0:T(8,128)(2,1)}, bf16[2,64,1024]{2,1,0:T(8,128)(2,1)}, u32[]{:S(2)}, u32[]{:S(2)}) collective-permute-start(bf16[2,64,1024]{2,1,0:T(8,128)(2,1)} %get-tuple-element.95), channel_id=1, source_target_pairs={{0,64},{64,0},{1,65},{65,1},{2,66},{66,2},{3,67},{67,3},{4,68},{68... | collective-permute-start | bytes 786440 | tf_op jit(solution)/shard_map/ppermute | solution.py:589
  303.8 36.2 %collective-permute-start.10 = (bf16[2,64,1024]{2,1,0:T(8,128)(2,1)}, bf16[2,64,1024]{2,1,0:T(8,128)(2,1)}, u32[]{:S(2)}, u32[]{:S(2)}) collective-permute-start(bf16[2,64,1024]{2,1,0:T(8,128)(2,1)} %get-tuple-element.96), channel_id=1, source_target_pairs={{0,65},{65,0},{1,64},{64,1},{2,67},{67,2},{3,66},{66,3},{4,69},{69... | collective-permute-start | bytes 786440 | tf_op jit(solution)/shard_map/ppermute | solution.py:593
  321.7 1.3 copy-start.2
  323.0 6.3 %copy-start.4 = (f32[4,32,2048]{2,1,0:T(8,128)S(1)}, f32[4,32,2048]{2,1,0:T(8,128)}, u32[]{:S(2)}) copy-start(f32[4,32,2048]{2,1,0:T(8,128)} %weight.4) | copy-start | bytes 3145732
  323.0 33.4 %all-to-all-start.6 = ((bf16[64,8,2048]{2,1,0:T(8,128)(2,1)}), bf16[64,8,2048]{2,1,0:T(8,128)(2,1)S(1)}, u32[]{:S(2)}, u32[]{:S(2)}) async-start(bf16[64,8,2048]{2,1,0:T(8,128)(2,1)} %bitcast.36), calls=%async_computation.6 | async-start | bytes 4194304 | tf_op jit(solution)/shard_map/all_to_all | solution.py:621
  329.3 11.1 %copy-start.3 = (bf16[64,8,2048]{2,1,0:T(8,128)(2,1)S(1)}, bf16[64,8,2048]{2,1,0:T(8,128)(2,1)}, u32[]{:S(2)}) copy-start(bf16[64,8,2048]{2,1,0:T(8,128)(2,1)} %copy-done.2) | copy-start | bytes 6291460
  329.3 11.1 %copy-start.7 = (bf16[128,2048]{1,0:T(8,128)(2,1)S(1)}, bf16[128,2048]{1,0:T(8,128)(2,1)}, u32[]{:S(2)}) copy-start(bf16[128,2048]{1,0:T(8,128)(2,1)} %cot.3) | copy-start | bytes 1572868
  329.3 11.1 %copy-start.9 = (f32[128,2]{1,0:T(8,128)S(1)}, f32[128,2]{1,0:T(8,128)}, u32[]{:S(2)}) copy-start(f32[128,2]{1,0:T(8,128)} %copy-done.8) | copy-start | bytes 3076
  329.4 1.4 copy-start.13
  330.8 1.2 copy-start.14
  332.0 0.9 copy-start.18
  337.6 5.1 %collective-permute-start.11 = (bf16[4,64,1024]{2,1,0:T(8,128)(2,1)}, bf16[4,64,1024]{2,1,0:T(8,128)(2,1)S(1)}, u32[]{:S(2)}, u32[]{:S(2)}) collective-permute-start(bf16[4,64,1024]{2,1,0:T(8,128)(2,1)} %get-tuple-element.97), channel_id=1, source_target_pairs={{0,32},{32,0},{1,33},{33,1},{2,34},{34,2},{3,35},{35,3},{4,36},{36... | collective-permute-start | bytes 1572872 | tf_op jit(solution)/shard_map/ppermute | solution.py:585
  339.9 2.8 collective-permute-start.12
  340.0 2.7 collective-permute-start.13
  342.8 1.6 copy-start.1
  344.4 1.0 copy-start.16
